TPU v7x, 32 devices: a whole 2x2x4 slice. The times are simulated.
32 devices in a mesh: ctx: 8 (over y, x, core), shard: 4 (over z).
Axes of the slice: x: 2, y: 2, z: 4, core: 2. Of those that a mesh axis runs over, the one named last changes fastest.
Arguments:
- tokens: bfloat16 [4, 1024, 2048], P('shard', 'ctx'), may hold values from -6 to 6
- qkv_weight: bfloat16 [2048, 6144], P('shard'), may hold values from -0.1875 to 0.1875
- qkv_bias: float32 [6144], replicated, may hold values from -1.5 to 1.5
- out_weight: bfloat16 [2048, 2048], P('shard'), may hold values from -0.75 to 0.75
- out_bias: float32 [2048], replicated, may hold values from -1.5 to 1.5
- up_weight: bfloat16 [2048, 8192], P('shard'), may hold values from -0.125 to 0.125
- up_bias: float32 [8192], replicated, may hold values from -2.5 to 2.5
- down_weight: bfloat16 [2048, 8192], P('shard'), may hold values from -0.0625 to 0.0625
- down_bias: float32 [2048], replicated, may hold values from -1.5 to 1.5
- attn_norm_gain: float32 [2048], replicated, may hold values from 0.5 to 1.5
- attn_norm_bias: float32 [2048], replicated, may hold values from -1.5 to 1.5
- mlp_norm_gain: float32 [2048], replicated, may hold values from 0.5 to 1.5
- mlp_norm_bias: float32 [2048], replicated, may hold values from -1.5 to 1.5
- cotangent: bfloat16 [4, 1024, 2048], P('shard', 'ctx'), may hold values from -6 to 6
Outputs:
- output: bfloat16 [4, 1024, 2048], P('shard', 'ctx')
- tokens_grad: float32 [4, 1024, 2048], P('shard', 'ctx')
- qkv_weight_grad: float32 [2048, 6144], P(('ctx', 'shard'))
- qkv_bias_grad: float32 [6144], replicated
- out_weight_grad: float32 [2048, 2048], P(('ctx', 'shard'))
- out_bias_grad: float32 [2048], replicated
- up_weight_grad: float32 [2048, 8192], P(('ctx', 'shard'))
- up_bias_grad: float32 [8192], replicated
- down_weight_grad: float32 [2048, 8192], P(('ctx', 'shard'))
- down_bias_grad: float32 [2048], replicated
- attn_norm_gain_grad: float32 [2048], replicated
- attn_norm_bias_grad: float32 [2048], replicated
- mlp_norm_gain_grad: float32 [2048], replicated
- mlp_norm_bias_grad: float32 [2048], replicated
All inputs are finite; a program needn't handle non-finite values.
Results may differ from a plain program's by a relative error of at most 0.012.
The roundings to bfloat16 on the way count: a program that leaves them out, or rounds other values in their place, can miss the bound.
Values may be sent and summed in bfloat16 or wider, within the bound.
A program may use at most 704 MiB of HBM per device.

v0:
```python
import jax
import jax.numpy as jnp
from jax import lax
from jax.sharding import PartitionSpec as P

H = 8
HD = 256
ROT = 64


norm_epsilon = 1e-05
masked_score = -1e30


def layer_norm(values, gain, shift):
    center = values - jnp.mean(values, axis=-1, keepdims=True)
    spread = jnp.mean(center * center, axis=-1, keepdims=True)
    return center * lax.rsqrt(spread + norm_epsilon) * gain + shift


def rotary(values, positions):
    half_rot = ROT // 2
    inv_freq = 10000.0 ** (-(jnp.arange(half_rot, dtype=jnp.float32) * 2.0) / ROT)
    angles = positions.astype(jnp.float32)[:, None] * inv_freq[None, :]
    cosine = jnp.cos(angles)[:, None, :]
    sine = jnp.sin(angles)[:, None, :]
    first_half = values[..., :half_rot]
    second_half = values[..., half_rot:ROT]
    return jnp.concatenate(
        [
            first_half * cosine - second_half * sine,
            second_half * cosine + first_half * sine,
            values[..., ROT:],
        ],
        axis=-1,
    )


def exact_gelu(values):
    return jax.nn.gelu(values, approximate=False)


def row_product(left, right):
    return lax.dot_general(
        left, right, (((0,), (0,)), ((), ())), preferred_element_type=jnp.float32
    )


def local(
    tokens,
    qkv_weight,
    qkv_bias,
    out_weight,
    out_bias,
    up_weight,
    up_bias,
    down_weight,
    down_bias,
    attn_norm_gain,
    attn_norm_bias,
    mlp_norm_gain,
    mlp_norm_bias,
    cotangent,
):
    rows_here = tokens.shape[1]
    width = tokens.shape[2]
    hidden_width = up_weight.shape[1]
    score_scale = HD ** (-0.5)
    contract_last = (((1,), (1,)), ((), ()))
    residual = tokens[0].astype(jnp.float32)
    normed_attn, attn_pull = jax.vjp(layer_norm, residual, attn_norm_gain, attn_norm_bias)
    normed_mlp, mlp_pull = jax.vjp(layer_norm, residual, mlp_norm_gain, mlp_norm_bias)
    attn_in = normed_attn.astype(jnp.bfloat16)
    mlp_in = normed_mlp.astype(jnp.bfloat16)
    qkv_full, out_full, up_full, down_full = (
        lax.all_gather(qkv_weight, "shard", axis=0, tiled=True),
        lax.all_gather(out_weight, "shard", axis=0, tiled=True),
        lax.all_gather(up_weight, "shard", axis=0, tiled=True),
        lax.all_gather(down_weight, "shard", axis=0, tiled=True),
    )
    projected = jnp.dot(attn_in, qkv_full, preferred_element_type=jnp.float32) + qkv_bias
    offset = lax.axis_index("ctx") * rows_here
    positions = offset + jnp.arange(rows_here, dtype=jnp.int32)
    queries = rotary(projected[:, :width].reshape(rows_here, H, HD), positions).astype(jnp.bfloat16)
    keys = rotary(projected[:, width : 2 * width].reshape(rows_here, H, HD), positions).astype(
        jnp.bfloat16
    )
    values = projected[:, 2 * width :].reshape(rows_here, H, HD).astype(jnp.bfloat16)
    query_last = offset + rows_here - 1
    start_state = (
        jnp.full((H, rows_here), masked_score, jnp.float32),
        jnp.zeros((H, rows_here), jnp.float32),
        jnp.zeros((rows_here, H, HD), jnp.float32),
    )
    key_block = lax.all_gather(keys, "ctx", axis=0, tiled=True)
    value_block = lax.all_gather(values, "ctx", axis=0, tiled=True)

    def attend_compute(running):
        running_max, running_total, accum = running
        scores = (
            jnp.einsum("qhd,khd->hqk", queries, key_block, preferred_element_type=jnp.float32)
            * score_scale
        )
        key_pos = jnp.arange(key_block.shape[0], dtype=jnp.int32)
        causal = positions[:, None] >= key_pos[None, :]
        scores = jnp.where(causal[None], scores, masked_score)
        new_max = jnp.maximum(running_max, jnp.max(scores, axis=-1))
        probs = jnp.where(causal[None], jnp.exp(scores - new_max[..., None]), 0.0)
        new_total = jnp.sum(probs, axis=-1)
        update = jnp.einsum(
            "hqk,khd->qhd",
            probs.astype(jnp.bfloat16),
            value_block,
            preferred_element_type=jnp.float32,
        )
        return (new_max, new_total, update)

    run_max, run_total, accum = lax.cond(
        jnp.int32(0) <= query_last, attend_compute, lambda unchanged: unchanged, start_state
    )
    log_total = run_max + jnp.log(run_total)
    mixed_full = accum / jnp.transpose(run_total)[..., None]
    mixed = mixed_full.reshape(rows_here, width).astype(jnp.bfloat16)
    attn_branch = jnp.dot(mixed, out_full, preferred_element_type=jnp.float32) + out_bias
    hidden = jnp.dot(mlp_in, up_full, preferred_element_type=jnp.float32) + up_bias
    activated_full, gelu_pull = jax.vjp(exact_gelu, hidden)
    activated = activated_full.astype(jnp.bfloat16)
    mlp_branch = (
        lax.dot_general(activated, down_full, contract_last, preferred_element_type=jnp.float32)
        + down_bias
    )
    output = (residual + attn_branch + mlp_branch).astype(jnp.bfloat16)[None]
    qkv_back, out_back, up_back, down_back = (
        lax.all_gather(qkv_weight, "shard", axis=0, tiled=True),
        lax.all_gather(out_weight, "shard", axis=0, tiled=True),
        lax.all_gather(up_weight, "shard", axis=0, tiled=True),
        lax.all_gather(down_weight, "shard", axis=0, tiled=True),
    )
    grad_out = cotangent[0]
    grad_out_full = grad_out.astype(jnp.float32)
    grad_activated = jnp.dot(grad_out, down_back, preferred_element_type=jnp.float32)
    grad_hidden = gelu_pull(grad_activated)[0].astype(jnp.bfloat16)
    grad_mixed = lax.dot_general(
        grad_out, out_back, contract_last, preferred_element_type=jnp.float32
    )
    grad_mixed = grad_mixed.astype(jnp.bfloat16).reshape(rows_here, H, HD)
    row_dot = jnp.sum(grad_mixed.astype(jnp.float32) * mixed_full, axis=-1)
    row_dot_heads = jnp.transpose(row_dot)
    all_log_total, all_row_dot = (
        lax.all_gather(jnp.transpose(log_total), "ctx", axis=0, tiled=True),
        lax.all_gather(row_dot, "ctx", axis=0, tiled=True),
    )
    query_key_block = lax.all_gather(keys, "ctx", axis=0, tiled=True)
    query_value_block = lax.all_gather(values, "ctx", axis=0, tiled=True)

    def query_compute(running):
        scores = (
            jnp.einsum("qhd,khd->hqk", queries, query_key_block, preferred_element_type=jnp.float32)
            * score_scale
        )
        key_pos = jnp.arange(query_key_block.shape[0], dtype=jnp.int32)
        causal = positions[:, None] >= key_pos[None, :]
        probs = jnp.where(causal[None], jnp.exp(scores - log_total[..., None]), 0.0)
        grad_probs = jnp.einsum(
            "qhd,khd->hqk", grad_mixed, query_value_block, preferred_element_type=jnp.float32
        )
        grad_scores = (probs * (grad_probs - row_dot_heads[..., None])).astype(jnp.bfloat16)
        return (
            jnp.einsum(
                "hqk,khd->qhd", grad_scores, query_key_block, preferred_element_type=jnp.float32
            )
            * score_scale
        )

    grad_queries = lax.cond(
        jnp.int32(0) <= query_last,
        query_compute,
        lambda unchanged: unchanged,
        jnp.zeros((rows_here, H, HD), jnp.float32),
    )
    zero_heads = jnp.zeros((rows_here, H, HD), jnp.float32)
    query_block = lax.all_gather(queries, "ctx", axis=0, tiled=True)
    grad_block = lax.all_gather(grad_mixed, "ctx", axis=0, tiled=True)
    block_len = query_block.shape[0]

    def key_compute(running):
        total_block = jnp.transpose(all_log_total)
        dot_block = jnp.transpose(all_row_dot)
        scores = (
            jnp.einsum("qhd,khd->hqk", query_block, keys, preferred_element_type=jnp.float32)
            * score_scale
        )
        query_pos = jnp.arange(block_len, dtype=jnp.int32)
        causal = query_pos[:, None] >= positions[None, :]
        probs = jnp.where(causal[None], jnp.exp(scores - total_block[..., None]), 0.0)
        grad_values_acc = jnp.einsum(
            "hqk,qhd->khd",
            probs.astype(jnp.bfloat16),
            grad_block,
            preferred_element_type=jnp.float32,
        )
        grad_probs = jnp.einsum(
            "qhd,khd->hqk", grad_block, values, preferred_element_type=jnp.float32
        )
        grad_scores = (probs * (grad_probs - dot_block[..., None])).astype(jnp.bfloat16)
        grad_keys_acc = (
            jnp.einsum("hqk,qhd->khd", grad_scores, query_block, preferred_element_type=jnp.float32)
            * score_scale
        )
        return (grad_keys_acc, grad_values_acc)

    grad_keys, grad_values = lax.cond(
        jnp.int32(0) + block_len - 1 >= offset,
        key_compute,
        lambda unchanged: unchanged,
        (zero_heads, zero_heads),
    )
    grad_projected = jnp.concatenate(
        [
            rotary(grad_queries, -positions).reshape(rows_here, width),
            rotary(grad_keys, -positions).reshape(rows_here, width),
            grad_values.reshape(rows_here, width),
        ],
        axis=1,
    ).astype(jnp.bfloat16)
    grad_attn_in = lax.dot_general(
        grad_projected, qkv_back, contract_last, preferred_element_type=jnp.float32
    )
    grad_mlp_in = lax.dot_general(
        grad_hidden, up_back, contract_last, preferred_element_type=jnp.float32
    )
    input_attn, gain_attn, shift_attn = attn_pull(grad_attn_in)
    input_mlp, gain_mlp, shift_mlp = mlp_pull(grad_mlp_in)
    tokens_grad = (grad_out_full + input_attn + input_mlp)[None]
    qkv_bias_part = jnp.sum(grad_projected.astype(jnp.float32), axis=0)
    out_bias_part = jnp.sum(grad_out_full, axis=0)
    up_bias_part = jnp.sum(grad_hidden.astype(jnp.float32), axis=0)
    summed_small = lax.psum(
        (qkv_bias_part, out_bias_part, up_bias_part, gain_attn, shift_attn, gain_mlp, shift_mlp),
        ("ctx", "shard"),
    )
    weight_terms = lax.psum_scatter(
        jnp.concatenate(
            [
                row_product(attn_in, grad_projected),
                row_product(mixed, grad_out),
                row_product(mlp_in, grad_hidden),
                row_product(grad_out, activated),
            ],
            axis=1,
        ),
        ("ctx", "shard"),
        scatter_dimension=0,
        tiled=True,
    )
    qkv_weight_grad = weight_terms[:, : 3 * width]
    out_weight_grad = weight_terms[:, 3 * width : 4 * width]
    up_weight_grad = weight_terms[:, 4 * width : 4 * width + hidden_width]
    down_weight_grad = weight_terms[:, 4 * width + hidden_width :]
    return (
        output,
        tokens_grad,
        qkv_weight_grad,
        summed_small[0],
        out_weight_grad,
        summed_small[1],
        up_weight_grad,
        summed_small[2],
        down_weight_grad,
        summed_small[1],
        summed_small[3],
        summed_small[4],
        summed_small[5],
        summed_small[6],
    )


def solution(mesh):
    in_specs = (
        P("shard", "ctx", None),
        P("shard", None),
        P(),
        P("shard", None),
        P(),
        P("shard", None),
        P(),
        P("shard", None),
        P(),
        P(),
        P(),
        P(),
        P(),
        P("shard", "ctx", None),
    )
    out_specs = (
        P("shard", "ctx", None),
        P("shard", "ctx", None),
        P(("ctx", "shard"), None),
        P(),
        P(("ctx", "shard"), None),
        P(),
        P(("ctx", "shard"), None),
        P(),
        P(("ctx", "shard"), None),
        P(),
        P(),
        P(),
        P(),
        P(),
    )
    return jax.shard_map(local, mesh=mesh, in_specs=in_specs, out_specs=out_specs, check_vma=False)
```

profile of v0, /device:TPU:0, one launch (start us, length us, event | category | flops | bytes accessed | tf_op | source)
XLA Modules:
  0.0 3705.6 jit_solution(9666657228392437350)
XLA Ops:
  9.2 428.3 %all-gather.9.cloned.1.call-done = bf16[2048,6144]{1,0:T(8,128)(2,1)} async-done(((bf16[512,6144]{1,0:T(8,128)(2,1)}), bf16[2048,6144]{1,0:T(8,128)(2,1)}) %all-gather.9.cloned.1.call-update) | async-done | bytes 25165840 | tf_op jit(solution)/shard_map/all_gather | solution.py:76
  437.6 11.0 convolution_add_fusion.1
  456.7 130.3 %all-gather.15.cloned.1.call-done = bf16[2048,2048]{1,0:T(8,128)(2,1)} async-done(((bf16[512,2048]{1,0:T(8,128)(2,1)}), bf16[2048,2048]{1,0:T(8,128)(2,1)}) %all-gather.15.cloned.1.call-update) | async-done | bytes 8388624 | tf_op jit(solution)/shard_map/all_gather | solution.py:77
  587.0 6.3 convolution_convert_fusion
  598.1 26.3 all-gather.13.cloned.1.call-done
  624.4 39.1 %all-gather.11.cloned.1.call-done = bf16[1024,8,256]{2,0,1:T(8,128)(2,1)} async-done(((bf16[128,8,256]{2,0,1:T(8,128)(2,1)}), bf16[1024,8,256]{2,0,1:T(8,128)(2,1)}) %all-gather.11.cloned.1.call-update) | async-done | bytes 4194320 | tf_op jit(solution)/shard_map/all_gather | solution.py:95
  663.5 13.0 conditional.3
  678.2 16.5 conditional.4
  678.4 5.6 fusion.110
  684.1 8.7 fusion.23
  694.7 10.6 all_gather.45
  705.3 8.3 all_gather.43
  713.6 28.8 all-gather.21.cloned.1.call-done
  742.4 23.1 conditional.5
  742.7 5.5 fusion.111
  748.2 8.7 fusion.37
  756.9 6.3 fusion.41
  774.8 8.1 fusion.83
  782.9 21.5 fusion.96
  804.3 501.0 %all-gather.17.cloned.1.call-done = bf16[2048,8192]{1,0:T(8,128)(2,1)} async-done(((bf16[512,8192]{1,0:T(8,128)(2,1)}), bf16[2048,8192]{1,0:T(8,128)(2,1)}) %all-gather.17.cloned.1.call-update) | async-done | bytes 33554448 | tf_op jit(solution)/shard_map/all_gather | solution.py:78
  1305.4 21.3 convolution_add_fusion
  1326.7 27.8 convolution_bitcast_fusion
  1354.4 512.1 %all-gather.19.cloned.1.call-done = bf16[2048,8192]{1,0:T(8,128)(2,1)} async-done(((bf16[512,8192]{1,0:T(8,128)(2,1)}), bf16[2048,8192]{1,0:T(8,128)(2,1)}) %all-gather.19.cloned.1.call-update) | async-done | bytes 33554448 | tf_op jit(solution)/shard_map/all_gather | solution.py:79
  1866.6 21.8 convert_reduce_fusion
  1888.4 23.6 fusion.93
  1911.9 15.9 fusion.112
  1927.8 21.5 fusion.103
  1955.9 130.8 %pad_maximum_fusion = f32[2048,24576]{1,0:T(8,128)} fusion(f32[2048,8192]{1,0:T(8,128)} %convolution_bitcast_fusion, f32[2048,8192]{1,0:T(8,128)} %fusion.93, f32[2048,2048]{1,0:T(8,128)} %fusion.83, f32[2048,6144]{1,0:T(8,128)} %fusion.96), kind=kLoop, calls=%fused_computation.47 | loop fusion | flops 150994944 | bytes 402653184 | tf_op jit(solution)/shard_map/concatenate | solution.py:243
  2087.4 24.3 convolution_add_fusion.2
  2111.8 7.1 fusion.59
  2118.8 1565.3 %reduce-scatter.2.cloned.1.call-done = f32[64,24576]{1,0:T(8,128)} async-done(((f32[2048,24576]{1,0:T(8,128)}), f32[64,24576]{1,0:T(8,128)}) %reduce-scatter.2.cloned.1.call-update) | async-done | bytes 6291472 | tf_op jit(solution)/shard_map/reduce_scatter | solution.py:242
  3688.8 4.7 fusion.106
  (155 shorter events, 60.0 us)
Async XLA Ops:
  7.2 430.4 %copy-start.12 = (f32[2048]{0:T(1024)S(1)}, f32[2048]{0:T(1024)}, u32[]{:S(2)}) copy-start(f32[2048]{0:T(1024)} %param.29) | copy-start | bytes 24580
  7.2 430.4 %copy-start.14 = (f32[2048]{0:T(1024)S(1)}, f32[2048]{0:T(1024)}, u32[]{:S(2)}) copy-start(f32[2048]{0:T(1024)} %param.30) | copy-start | bytes 24580
  7.2 430.3 %copy-start.23 = (f32[6144]{0:T(1024)S(1)}, f32[6144]{0:T(1024)}, u32[]{:S(2)}) copy-start(f32[6144]{0:T(1024)} %param.22) | copy-start | bytes 73732
  7.2 430.3 %all-gather.9.cloned.1.call-start = ((), (), s32[]{:S(2)}) async-start(), calls=%async_computation.1 | async-start | bytes 31457280 | tf_op jit(solution)/shard_map/all_gather | solution.py:76
  8.0 579.0 %all-gather.15.cloned.1.call-start = ((), (), s32[]{:S(2)}) async-start(), calls=%async_computation.4 | async-start | bytes 10485760 | tf_op jit(solution)/shard_map/all_gather | solution.py:77
  8.7 615.7 %all-gather.13.cloned.1.call-start = ((), (), s32[]{:S(2)}) async-start(), calls=%async_computation.3 | async-start | bytes 4718592 | tf_op jit(solution)/shard_map/all_gather | solution.py:96
  8.9 439.7 %copy-start.16 = (f32[128]{0:T(128)}, f32[128]{0:T(128)S(1)}, u32[]{:S(2)}) copy-start(f32[128]{0:T(128)S(1)} %broadcast_multiply_fusion) | copy-start | bytes 1540
  9.2 439.4 %copy-start.30 = (f32[128]{0:T(128)}, f32[128]{0:T(128)S(1)}, u32[]{:S(2)}) copy-start(f32[128]{0:T(128)S(1)} %fusion.77) | copy-start | bytes 1540
  9.2 439.4 %copy-start.18 = (f32[128]{0:T(128)}, f32[128]{0:T(128)S(1)}, u32[]{:S(2)}) copy-start(f32[128]{0:T(128)S(1)} %fusion.91) | copy-start | bytes 1540
  451.2 212.3 %all-gather.11.cloned.1.call-start = ((), (), s32[]{:S(2)}) async-start(), calls=%async_computation.2 | async-start | bytes 4718592 | tf_op jit(solution)/shard_map/all_gather | solution.py:95
  454.6 132.4 %copy-start.6 = (bf16[1,128,2048]{2,1,0:T(8,128)(2,1)S(1)}, bf16[1,128,2048]{2,1,0:T(8,128)(2,1)}, u32[]{:S(2)}) copy-start(bf16[1,128,2048]{2,1,0:T(8,128)(2,1)} %param.33) | copy-start | bytes 1572868
  456.7 256.9 %all-gather.23.cloned.1.call-start = ((), (), s32[]{:S(2)}) async-start(), calls=%async_computation.8 | async-start | bytes 4718592 | tf_op jit(solution)/shard_map/all_gather | solution.py:183
  594.1 148.3 %all-gather.21.cloned.1.call-start = ((), (), s32[]{:S(2)}) async-start(), calls=%async_computation.7 | async-start | bytes 4718592 | tf_op jit(solution)/shard_map/all_gather | solution.py:182
  595.8 709.6 %all-gather.17.cloned.1.call-start = ((), (), s32[]{:S(2)}) async-start(), calls=%async_computation.5 | async-start | bytes 41943040 | tf_op jit(solution)/shard_map/all_gather | solution.py:78
  596.5 67.0 %copy-start.3 = (bf16[128,8,256]{2,0,1:T(8,128)(2,1)S(1)}, bf16[128,8,256]{2,0,1:T(8,128)(2,1)}, u32[]{:S(2)}) copy-start(bf16[128,8,256]{2,0,1:T(8,128)(2,1)} %pad_maximum_fusion.2) | copy-start | bytes 1572868
  596.5 1270.0 %all-gather.19.cloned.1.call-start = ((), (), s32[]{:S(2)}) async-start(), calls=%async_computation.6 | async-start | bytes 41943040 | tf_op jit(solution)/shard_map/all_gather | solution.py:79
  597.3 1521.6 %all-reduce.3.cloned.1.call-start = ((), (), s32[]{:S(2)}) async-start(), calls=%async_computation.10 | async-start | bytes 196608 | tf_op jit(solution)/shard_map/psum | solution.py:238
  597.6 65.9 %copy-start.11 = (bf16[16,8,8,256]{3,2,1,0:T(8,128)(2,1)}, bf16[16,8,8,256]{3,2,1,0:T(8,128)(2,1)S(1)}, u32[]{:S(2)}) copy-start(bf16[16,8,8,256]{3,2,1,0:T(8,128)(2,1)S(1)} %copy.127) | copy-start | bytes 1572868
  677.4 97.4 %copy-start.4 = (bf16[128,8,256]{0,2,1:T(8,128)(2,1)}, bf16[128,8,256]{0,2,1:T(8,128)(2,1)S(1)}, u32[]{:S(2)}) copy-start(bf16[128,8,256]{0,2,1:T(8,128)(2,1)S(1)} %get-tuple-element.227) | copy-start | bytes 1572868
  678.2 64.1 %copy-start.8 = (bf16[128,8,256]{2,0,1:T(8,128)(2,1)S(1)}, bf16[128,8,256]{2,0,1:T(8,128)(2,1)}, u32[]{:S(2)}) copy-start(bf16[128,8,256]{2,0,1:T(8,128)(2,1)} %pad_maximum_fusion.3) | copy-start | bytes 1572868
  694.7 47.7 %copy-start.9 = (f32[128,8,32]{2,0,1:T(8,128)}, f32[128,8,32]{2,0,1:T(8,128)S(1)}, u32[]{:S(2)}) copy-start(f32[128,8,32]{2,0,1:T(8,128)S(1)} %get-tuple-element.121) | copy-start | bytes 393220
  774.8 8.1 copy-start.19
  782.9 522.5 %copy-start.13 = (f32[2048]{0:T(1024)S(1)}, f32[2048]{0:T(1024)}, u32[]{:S(2)}) copy-start(f32[2048]{0:T(1024)} %param.31) | copy-start | bytes 24580
  782.9 522.5 %copy-start.15 = (f32[2048]{0:T(1024)S(1)}, f32[2048]{0:T(1024)}, u32[]{:S(2)}) copy-start(f32[2048]{0:T(1024)} %param.32) | copy-start | bytes 24580
  782.9 522.5 %copy-start.22 = (f32[8192]{0:T(1024)S(1)}, f32[8192]{0:T(1024)}, u32[]{:S(2)}) copy-start(f32[8192]{0:T(1024)} %param.26) | copy-start | bytes 98308
  1927.8 21.5 copy-start.31
  1955.8 1728.3 %reduce-scatter.2.cloned.1.call-start = ((), (), s32[]{:S(2)}) async-start(), calls=%async_computation.9 | async-start | bytes 207618048 | tf_op jit(solution)/shard_map/reduce_scatter | solution.py:242
  2087.4 24.4 copy-start.1
  2087.4 24.4 copy-start.5
  2087.4 24.4 copy-start.25
  3688.7 8.4 copy-start.27
  3688.7 9.0 copy-start.26
  (12 other events, 60.5 us)
Sparse Core Ops, SparseCore 0:
  9.6 427.8 all-gather.8
  439.1 147.8 all-gather.14
  589.4 34.9 all-gather.12
  626.8 36.7 all-gather.10
  665.8 37.4 all-gather.22
  705.6 36.7 all-gather.20
  743.9 561.3 all-gather.16
  1306.9 559.5 all-gather.18
  1955.9 121.9 all-reduce.2
  2086.8 1597.2 reduce-scatter.1
where the time goes:
time: 3710 us
  waiting for transfers between devices  3230 us (87%)
  matrix products  252 us (7%)
  other arithmetic  154 us (4%)
    reduce_scatter x1, waiting for transfers between devices, local(): lax.psum_scatter(jnp.concatenate([row_product(attn_in, grad_projected), r...  1570 us
    all_gather x1, waiting for transfers between devices, local(): lax.all_gather(down_weight, 'shard', axis=0, tiled=True)  512 us
    all_gather x1, waiting for transfers between devices, local(): lax.all_gather(up_weight, 'shard', axis=0, tiled=True)  501 us
    all_gather x1, waiting for transfers between devices, local(): lax.all_gather(qkv_weight, 'shard', axis=0, tiled=True)  428 us
    concatenate x1, other arithmetic, local(): jnp.concatenate([row_product(attn_in, grad_projected), row_product(mixed,...  131 us
    all_gather x1, waiting for transfers between devices, local(): lax.all_gather(out_weight, 'shard', axis=0, tiled=True)  130 us
    dot_general x4, matrix products, row_product(): lax.dot_general(left, right, (((0,), (0,)), ((), ())), preferred_element_...  80.8 us
  transfers between devices with their start and end apart: 10, of which 8 were waited for; matrix products, arithmetic and copies ran while one was open for 9% of the time, Pallas kernels for 0%

commit v1 on v0

v1 whole, which is shorter than its diff:
```python
import jax
import jax.numpy as jnp
from jax import lax
from jax.sharding import PartitionSpec as P

H = 8
HD = 256
ROT = 64
AXES = ("ctx", "shard")

norm_epsilon = 1e-05
masked_score = -1e30
contract_last = (((1,), (1,)), ((), ()))
contract_first = (((0,), (0,)), ((), ()))


def dot32(left, right, dims=(((1,), (0,)), ((), ()))):
    return lax.dot_general(left, right, dims, preferred_element_type=jnp.float32)


def normalize(values):
    center = values - jnp.mean(values, axis=-1, keepdims=True)
    spread = jnp.mean(center * center, axis=-1, keepdims=True)
    scale = lax.rsqrt(spread + norm_epsilon)
    return center * scale, scale


def rotary(values, positions):
    half_rot = ROT // 2
    inv_freq = 10000.0 ** (-(jnp.arange(half_rot, dtype=jnp.float32) * 2.0) / ROT)
    angles = positions.astype(jnp.float32)[:, None] * inv_freq[None, :]
    cosine = jnp.cos(angles)
    sine = jnp.sin(angles)
    first_half = values[:, :half_rot]
    second_half = values[:, half_rot:ROT]
    return jnp.concatenate(
        [
            first_half * cosine - second_half * sine,
            second_half * cosine + first_half * sine,
            values[:, ROT:],
        ],
        axis=-1,
    )


def exact_gelu(values):
    return jax.nn.gelu(values, approximate=False)


class Layout:
    def __init__(self, mesh):
        self.nz = mesh.shape["shard"]
        self.nc = mesh.shape["ctx"]
        self.nlo = self.nz
        self.nhi = self.nc // self.nlo
        assert self.nhi == 2 and self.nz * self.nhi == self.nc
        self.bits = [1 << b for b in range(self.nlo.bit_length() - 1)]
        assert 1 << len(self.bits) == self.nlo
        self.seq_of_lo = [
            lo // 2 if lo % 2 == 0 else self.nz - 1 - lo // 2 for lo in range(self.nlo)
        ]
        self.lo_of_seq = [self.seq_of_lo.index(s) for s in range(self.nz)]

    def flat(self, z, hi, lo):
        return (hi * self.nlo + lo) * self.nz + z

    def permute(self, value, pairs):
        return lax.ppermute(
            value, AXES, [(self.flat(*a), self.flat(*b)) for a, b in pairs]
        )

    def everywhere(self, where_to):
        pairs = []
        for z in range(self.nz):
            for hi in range(self.nhi):
                for lo in range(self.nlo):
                    pairs.append(((z, hi, lo), where_to(z, hi, lo)))
        return pairs

    def swap_lo(self, value, bit):
        return self.permute(value, self.everywhere(lambda z, hi, lo: (z, hi, lo ^ bit)))

    def swap_hi(self, value):
        return self.permute(value, self.everywhere(lambda z, hi, lo: (z, 1 - hi, lo)))

    def shift_z(self, value, by):
        return self.permute(
            value, self.everywhere(lambda z, hi, lo: ((z + by) % self.nz, hi, lo))
        )

    def in_plane(self, j):
        pairs = []
        for z in range(self.nz):
            home = self.lo_of_seq[z]
            for hi in range(self.nhi):
                pairs.append(((z, hi, home ^ j), (z, hi, home)))
        return pairs

    def chain(self):
        steps = [[] for _ in range(self.nz - 1)]
        for lo in range(self.nlo):
            s = self.seq_of_lo[lo]
            late = 1 if s < self.nz - 1 else 0
            for hi in range(self.nhi):
                for k in range(self.nz - 1 - s):
                    steps[k].append(((s + k, hi, lo), (s + k + 1, hi, lo)))
                for k in range(s):
                    steps[k + late].append(((s - k, hi, lo), (s - k - 1, hi, lo)))
        return steps


def lookup(table, index):
    return jnp.asarray(table, jnp.int32)[index]


def local_block(
    lay,
    tokens,
    qkv_weight,
    qkv_bias,
    out_weight,
    out_bias,
    up_weight,
    up_bias,
    down_weight,
    down_bias,
    attn_norm_gain,
    attn_norm_bias,
    mlp_norm_gain,
    mlp_norm_bias,
    cotangent,
):
    f32, bf16 = jnp.float32, jnp.bfloat16
    nz, nlo, nhi = lay.nz, lay.nlo, lay.nhi
    ranks = nz * nhi
    rows = tokens.shape[1]
    width = tokens.shape[2]
    hidden_width = up_weight.shape[1]
    weight_rows = qkv_weight.shape[0]
    half = nlo * rows
    ctx = lax.axis_index("ctx")
    z = lax.axis_index("shard")
    hi, lo = ctx // nlo, ctx % nlo
    rank = z * nhi + hi
    ff = hidden_width // ranks
    repeat = max(1, ranks // H)
    head = rank // repeat
    score_scale = HD ** (-0.5)
    steps = lay.chain()

    def received(step):
        table = [0] * (nz * nhi * nlo)
        for _, target in steps[step]:
            table[lay.flat(*target)] = 1
        return lookup(table, ctx * nz + z) > 0

    def gather_sequence(block):
        parts = [block] + [lay.permute(block, lay.in_plane(j)) for j in range(1, nlo)]
        current = jnp.concatenate(parts, axis=0)
        for k in range(nz - 1):
            arrived = lay.permute(current, steps[k])
            current = jnp.where(received(k), arrived, current)
        return jnp.concatenate([current, lay.swap_hi(current)], axis=0)

    def reduce_sequence(partial):
        other = lay.swap_hi(partial[half:].astype(bf16))
        current = (partial[:half] + other.astype(f32)).astype(bf16)
        for k in reversed(range(nz - 1)):
            arrived = lay.permute(current, [(b, a) for a, b in steps[k]])
            current = (current.astype(f32) + arrived.astype(f32)).astype(bf16)
        home = lookup(lay.lo_of_seq, z)
        mine = jnp.where(lo == home, current[:rows].astype(f32), 0.0)
        for j in range(1, nlo):
            block = current[j * rows : (j + 1) * rows]
            arrived = lay.permute(block, [(b, a) for a, b in lay.in_plane(j)])
            mine = mine + arrived.astype(f32)
        return mine

    quarter = weight_rows // nlo

    def gather_weight(columns_of):
        pieces = []
        for by in range(1, nz):
            target = ((z + by) % nz) * nhi + hi
            pieces.append(lay.shift_z(columns_of(target, lo * quarter, quarter), by))
        held = jnp.stack(pieces)[:, None]
        for bit in reversed(lay.bits):
            other = lay.swap_lo(held, bit)
            first = (lo & bit) == 0
            held = jnp.concatenate(
                [jnp.where(first, held, other), jnp.where(first, other, held)], axis=1
            )
        order = [0]
        for bit in reversed(lay.bits):
            order = [v for v in order] + [v + bit for v in order]
        inverse = [order.index(v) for v in range(nlo)]
        held = held[:, jnp.asarray(inverse)] if inverse != list(range(nlo)) else held
        held = held.reshape(nz - 1, weight_rows, -1)
        mine = columns_of(rank, 0, weight_rows)
        stack = jnp.concatenate([mine[None], held], axis=0)
        return jnp.concatenate(
            [
                lax.dynamic_index_in_dim(stack, (z - k) % nz, 0, keepdims=False)
                for k in range(nz)
            ],
            axis=0,
        )

    def qkv_columns(of_rank, row, count):
        first = (of_rank // repeat) * HD
        return jnp.concatenate(
            [
                lax.dynamic_slice(qkv_weight, (row, part * width + first), (count, HD))
                for part in range(3)
            ],
            axis=1,
        )

    def up_columns(of_rank, row, count):
        return lax.dynamic_slice(up_weight, (row, of_rank * ff), (count, ff))

    def down_columns(of_rank, row, count):
        return lax.dynamic_slice(down_weight, (row, of_rank * ff), (count, ff))

    own = tokens[0]
    own_cotangent = cotangent[0]
    seq_tokens = gather_sequence(own)
    qkv_here = gather_weight(qkv_columns)
    up_here = gather_weight(up_columns)
    seq_cotangent = gather_sequence(own_cotangent)
    down_here = gather_weight(down_columns)
    out_head = lax.dynamic_slice(out_weight, (head * HD - z * weight_rows, 0), (HD, width))
    out_rows = width // ranks
    out_at = rank * out_rows - head * HD

    block_index = lo ^ jnp.arange(nlo, dtype=jnp.int32)
    within = (block_index[:, None] * rows + jnp.arange(rows, dtype=jnp.int32)[None, :]).reshape(-1)
    positions = jnp.concatenate([hi * half + within, (1 - hi) * half + within])

    normed, _ = normalize(seq_tokens.astype(f32))
    attn_in = (normed * attn_norm_gain + attn_norm_bias).astype(bf16)
    mlp_in = (normed * mlp_norm_gain + mlp_norm_bias).astype(bf16)
    bias_here = jnp.concatenate(
        [lax.dynamic_slice(qkv_bias, (part * width + head * HD,), (HD,)) for part in range(3)]
    )
    projected = dot32(attn_in, qkv_here) + bias_here
    queries = rotary(projected[:, :HD], positions).astype(bf16)
    keys = rotary(projected[:, HD : 2 * HD], positions).astype(bf16)
    values = projected[:, 2 * HD :].astype(bf16)
    causal = positions[:, None] >= positions[None, :]
    scores = jnp.where(causal, dot32(queries, keys, contract_last) * score_scale, masked_score)
    top = jnp.max(scores, axis=-1, keepdims=True)
    weights = jnp.where(causal, jnp.exp(scores - top), 0.0)
    total = jnp.sum(weights, axis=-1, keepdims=True)
    mixed_full = dot32(weights.astype(bf16), values) / total
    log_total = top + jnp.log(total)
    mixed = mixed_full.astype(bf16)
    mixed_mine = lax.dynamic_slice(mixed, (0, out_at), (mixed.shape[0], out_rows))
    out_mine = lax.dynamic_slice(out_head, (out_at, 0), (out_rows, width))
    hidden = dot32(mlp_in, up_here) + lax.dynamic_slice(up_bias, (rank * ff,), (ff,))
    activated_full, gelu_pull = jax.vjp(exact_gelu, hidden)
    activated = activated_full.astype(bf16)
    out_partial = dot32(mixed_mine, out_mine) + dot32(activated, down_here, contract_last)
    summed_out = reduce_sequence(out_partial)
    output = (own.astype(f32) + summed_out + (out_bias + down_bias)).astype(bf16)[None]

    down_grad = dot32(seq_cotangent, activated, contract_first)
    out_grad = dot32(mixed_mine, seq_cotangent, contract_first)
    grad_hidden = gelu_pull(dot32(seq_cotangent, down_here))[0].astype(bf16)
    up_grad = dot32(mlp_in, grad_hidden, contract_first)
    grad_mixed = dot32(seq_cotangent, out_head, contract_last).astype(bf16)
    row_dot = jnp.sum(grad_mixed.astype(f32) * mixed_full, axis=-1, keepdims=True)
    probs = jnp.where(causal, jnp.exp(scores - log_total), 0.0)
    grad_values = dot32(probs.astype(bf16), grad_mixed, contract_first)
    grad_probs = dot32(grad_mixed, values, contract_last)
    grad_scores = (probs * (grad_probs - row_dot)).astype(bf16)
    grad_queries = dot32(grad_scores, keys) * score_scale
    grad_keys = dot32(grad_scores, queries, contract_first) * score_scale
    grad_projected = jnp.concatenate(
        [rotary(grad_queries, -positions), rotary(grad_keys, -positions), grad_values], axis=1
    ).astype(bf16)
    qkv_grad = dot32(attn_in, grad_projected, contract_first)
    grad_attn_in = dot32(grad_projected, qkv_here, contract_last) * (1.0 / repeat)
    grad_mlp_in = dot32(grad_hidden, up_here, contract_last)
    summed_in = reduce_sequence(grad_attn_in * attn_norm_gain + grad_mlp_in * mlp_norm_gain)
    own_normed, own_scale = normalize(own.astype(f32))
    input_grad = own_scale * (
        summed_in
        - jnp.mean(summed_in, axis=-1, keepdims=True)
        - own_normed * jnp.mean(summed_in * own_normed, axis=-1, keepdims=True)
    )
    tokens_grad = (own_cotangent.astype(f32) + input_grad)[None]

    first_copy = jnp.where(rank % repeat == 0, 1.0, 0.0)
    qkv_bias_part = jnp.sum(grad_projected.astype(f32), axis=0) * first_copy
    qkv_bias_full = jnp.zeros((3, width), f32)
    qkv_bias_full = lax.dynamic_update_slice(
        qkv_bias_full, qkv_bias_part.reshape(3, HD), (0, head * HD)
    ).reshape(-1)
    up_bias_full = lax.dynamic_update_slice(
        jnp.zeros((hidden_width,), f32),
        jnp.sum(grad_hidden.astype(f32), axis=0),
        (rank * ff,),
    )
    small = lax.psum(
        jnp.concatenate(
            [
                qkv_bias_full,
                up_bias_full,
                jnp.sum(own_cotangent.astype(f32), axis=0),
                jnp.sum(grad_attn_in * normed, axis=0),
                jnp.sum(grad_attn_in, axis=0),
                jnp.sum(grad_mlp_in * normed, axis=0),
                jnp.sum(grad_mlp_in, axis=0),
            ]
        ),
        AXES,
    )
    cuts = [3 * width, hidden_width, width, width, width, width, width]
    small_parts, at = [], 0
    for size in cuts:
        small_parts.append(small[at : at + size])
        at += size

    grain = width // (lay.nc * nz)

    def scatter_weight(partial):
        cols = partial.shape[1]
        held = partial.astype(bf16).reshape((nhi,) + (2,) * len(lay.bits) + (nz, grain, cols))
        for bit in lay.bits:
            axis = len(held.shape) - 4
            which = jnp.where((lo & bit) == 0, 0, 1)
            send = lax.dynamic_index_in_dim(held, 1 - which, axis, keepdims=False)
            keep = lax.dynamic_index_in_dim(held, which, axis, keepdims=False)
            held = (keep.astype(f32) + lay.swap_lo(send, bit).astype(f32)).astype(bf16)
        pieces = [lax.dynamic_index_in_dim(held, z, 1, keepdims=False)]
        for by in range(1, nz):
            pieces.append(
                lay.shift_z(
                    lax.dynamic_index_in_dim(held, (z + by) % nz, 1, keepdims=False), by
                )
            )
        stack = jnp.stack(pieces)
        other = lay.swap_hi(lax.dynamic_index_in_dim(stack, 1 - hi, 1, keepdims=False))
        keep = lax.dynamic_index_in_dim(stack, hi, 1, keepdims=False)
        result = []
        for k in range(nz):
            a = lax.dynamic_index_in_dim(keep, (z - k) % nz, 0, keepdims=False)
            b = lax.dynamic_index_in_dim(other, (z - k) % nz, 0, keepdims=False)
            result.append(jnp.where(hi == 0, a, b))
            result.append(jnp.where(hi == 0, b, a))
        return jnp.stack(result).astype(f32)

    down_all = scatter_weight(down_grad)
    up_all = scatter_weight(up_grad)
    qkv_all = scatter_weight(qkv_grad)[::repeat]
    down_weight_grad = jnp.transpose(down_all, (1, 0, 2)).reshape(grain, hidden_width)
    up_weight_grad = jnp.transpose(up_all, (1, 0, 2)).reshape(grain, hidden_width)
    qkv_weight_grad = jnp.transpose(
        qkv_all.reshape(H, grain, 3, HD), (1, 2, 0, 3)
    ).reshape(grain, 3 * width)

    held = out_grad.astype(bf16).reshape((2,) * len(lay.bits) + (grain, width))
    for bit in lay.bits:
        axis = len(held.shape) - 3
        which = jnp.where((lo & bit) == 0, 0, 1)
        send = lax.dynamic_index_in_dim(held, 1 - which, axis, keepdims=False)
        keep = lax.dynamic_index_in_dim(held, which, axis, keepdims=False)
        held = (keep.astype(f32) + lay.swap_lo(send, bit).astype(f32)).astype(bf16)
    pairs = []
    for zz in range(nz):
        for h in range(nhi):
            for l in range(nlo):
                owner = zz * nhi + h
                pairs.append(((zz, h, l), (l, owner // nlo, owner % nlo)))
    out_weight_grad = lay.permute(held, pairs).astype(f32)

    return (
        output,
        tokens_grad,
        qkv_weight_grad,
        small_parts[0],
        out_weight_grad,
        small_parts[2],
        up_weight_grad,
        small_parts[1],
        down_weight_grad,
        small_parts[2],
        small_parts[3],
        small_parts[4],
        small_parts[5],
        small_parts[6],
    )


def solution(mesh):
    lay = Layout(mesh)

    def local(*args):
        return local_block(lay, *args)

    sharded = P("shard", "ctx", None)
    by_rows = P("shard", None)
    owned = P(("ctx", "shard"), None)
    in_specs = (
        sharded, by_rows, P(), by_rows, P(), by_rows, P(), by_rows, P(),
        P(), P(), P(), P(), sharded,
    )
    out_specs = (
        sharded, sharded, owned, P(), owned, P(), owned, P(), owned,
        P(), P(), P(), P(), P(),
    )
    return jax.shard_map(
        local, mesh=mesh, in_specs=in_specs, out_specs=out_specs, check_vma=False
    )
```

time: 3710 us -> 826 us (0.22)
  waiting for transfers between devices: 3230 us -> 328 us
  starting transfers between devices: 0.57 us -> 177 us
  matrix products: 252 us -> 112 us
  other arithmetic: 154 us -> 95.8 us
  local copies, waits for them, and re-layouts: 30.5 us -> 83.7 us
    all_gather x8 -> x0, waiting for transfers between devices: 1670 us -> none  [the longest x1 512 us: local(): lax.all_gather(down_weight, 'shard', axis=0, tiled=True)]
    reduce_scatter x1 -> x0, waiting for transfers between devices: 1570 us -> none  [local(): lax.psum_scatter(jnp.concatenate([row_product(attn_in, grad_projected), r...]
    ppermute x0 -> x64, waiting for transfers between devices: none -> 207 us  [permute(): lax.ppermute(value, AXES, [(self.flat(*a), self.flat(*b)) for a, b in pai...]
    ppermute x0 -> x64, starting transfers between devices: none -> 177 us  [permute(): lax.ppermute(value, AXES, [(self.flat(*a), self.flat(*b)) for a, b in pai...]
    dot_general x19 -> x18, matrix products: 252 us -> 112 us  [dot32(): lax.dot_general(left, right, dims, preferred_element_type=jnp.float32)]
    concatenate x5 -> x12, other arithmetic: 137 us -> 16.2 us  [the longest x6 8.28 us: gather_weight(): jnp.concatenate([jnp.where(first, held, other), jnp.where(first, other, h...]
    psum x1, waiting for transfers between devices: 0.01 us -> 120 us  [local_block(): lax.psum(jnp.concatenate([qkv_bias_full, up_bias_full, jnp.sum(own_cotang...]
  transfers between devices with their start and end apart: 10 -> 65, of which waited for: 8 -> 24; matrix products, arithmetic and copies ran while one was open for 9% -> 28% of each run, Pallas kernels for 0% -> 0%
where the time goes in v1:
time: 826 us; the launch traced here: 816 us
  waiting for transfers between devices  328 us (40%)
  starting transfers between devices  177 us (21%)
  matrix products  112 us (14%)
  other arithmetic  95.8 us (12%)
  local copies, waits for them, and re-layouts  83.7 us (10%)
  between operations  19.3 us (2%)
    ppermute x64, waiting for transfers between devices, permute(): lax.ppermute(value, AXES, [(self.flat(*a), self.flat(*b)) for a, b in pai...  207 us
    ppermute x64, starting transfers between devices, permute(): lax.ppermute(value, AXES, [(self.flat(*a), self.flat(*b)) for a, b in pai...  177 us
    psum x1, waiting for transfers between devices, local_block(): lax.psum(jnp.concatenate([qkv_bias_full, up_bias_full, jnp.sum(own_cotang...  120 us
    dot_general x18, matrix products, dot32(): lax.dot_general(left, right, dims, preferred_element_type=jnp.float32)  112 us
    gather x6, local copies, waits for them, and re-layouts, gather_weight(): held[:, jnp.asarray(inverse)]  20.6 us
    select_n x6, other arithmetic, gather_sequence(): current = jnp.where(received(k), arrived, current)  18.7 us
    unnamed x185, local copies, waits for them, and re-layouts  17.5 us
  transfers between devices with their start and end apart: 65, of which 24 were waited for; matrix products, arithmetic and copies ran while one was open for 28% of the time, Pallas kernels for 0%

profile of v1, /device:TPU:0, one launch (start us, length us, event | category | flops | bytes accessed | tf_op | source)
XLA Modules:
  0.0 815.8 jit_solution(10637835358102192122)
XLA Ops:
  17.5 7.5 collective-permute-done.1
  54.0 6.0 collective-permute-done.3
  66.8 10.2 %collective-permute-start.13 = (bf16[128,1024]{1,0:T(8,128)(2,1)}, bf16[128,1024]{1,0:T(8,128)(2,1)S(1)}, u32[]{:S(2)}, u32[]{:S(2)}) collective-permute-start(bf16[128,1024]{1,0:T(8,128)(2,1)} %get-tuple-element.31), channel_id=1, source_target_pairs={{0,2},{4,6},{8,10},{12,14},{16,18},{20,22},{24,26},{28,30},{1,3},{... | collective-permute-start | bytes 786440 | tf_op jit(solution)/shard_map/ppermute | solution.py:68
  83.3 10.4 %collective-permute-done.8 = bf16[128,768]{1,0:T(8,128)(2,1)S(1)} collective-permute-done((bf16[128,768]{1,0:T(8,128)(2,1)}, bf16[128,768]{1,0:T(8,128)(2,1)S(1)}, u32[]{:S(2)}, u32[]{:S(2)}) %collective-permute-start.8) | collective-permute-done | bytes 196640 | tf_op jit(solution)/shard_map/ppermute | solution.py:68
  94.5 18.4 %collective-permute-start.14 = (bf16[128,1024]{1,0:T(8,128)(2,1)}, bf16[128,1024]{1,0:T(8,128)(2,1)S(1)}, u32[]{:S(2)}, u32[]{:S(2)}) collective-permute-start(bf16[128,1024]{1,0:T(8,128)(2,1)} %get-tuple-element.30), channel_id=1, source_target_pairs={{0,3},{4,7},{8,11},{12,15},{16,19},{20,23},{24,27},{28,31},{1,0},{... | collective-permute-start | bytes 786440 | tf_op jit(solution)/shard_map/ppermute | solution.py:68
  114.7 5.3 collective-permute-done.14
  127.4 8.7 %collective-permute-done.18 = bf16[128,1024]{1,0:T(8,128)(2,1)S(1)} collective-permute-done((bf16[128,1024]{1,0:T(8,128)(2,1)}, bf16[128,1024]{1,0:T(8,128)(2,1)S(1)}, u32[]{:S(2)}, u32[]{:S(2)}) %collective-permute-start.18) | collective-permute-done | bytes 262176 | tf_op jit(solution)/shard_map/ppermute | solution.py:68
  136.1 9.0 %collective-permute-start.15 = (bf16[3,1,128,1024]{3,2,1,0:T(8,128)(2,1)S(1)}, bf16[3,1,128,1024]{3,2,1,0:T(8,128)(2,1)S(1)}, u32[]{:S(2)}, u32[]{:S(2)}) collective-permute-start(bf16[3,1,128,1024]{3,2,1,0:T(8,128)(2,1)S(1)} %maximum_bitcast_fusion.1), channel_id=1, source_target_pairs={{0,8},{4,12},{8,0},{12,4},{16,24},{20,28},{24,16},{28,20},{1,9},{5... | collective-permute-start | bytes 2359304 | tf_op jit(solution)/shard_map/ppermute | solution.py:68
  145.2 7.9 collective-permute-start.20
  167.2 5.5 collective-permute-done.20
  225.7 17.0 %collective-permute-done.6 = bf16[512,2048]{1,0:T(8,128)(2,1)} collective-permute-done((bf16[512,2048]{1,0:T(8,128)(2,1)}, bf16[512,2048]{1,0:T(8,128)(2,1)}, u32[]{:S(2)}, u32[]{:S(2)}) %collective-permute-start.6) | collective-permute-done | bytes 2097184 | tf_op jit(solution)/shard_map/ppermute | solution.py:68
  248.5 6.3 fusion.184
  257.3 29.5 %collective-permute-done.35 = bf16[512,2048]{1,0:T(8,128)(2,1)S(1)} collective-permute-done((bf16[512,2048]{1,0:T(8,128)(2,1)S(1)}, bf16[512,2048]{1,0:T(8,128)(2,1)S(1)}, u32[]{:S(2)}, u32[]{:S(2)}) %collective-permute-start.35) | collective-permute-done | bytes 2097184 | tf_op jit(solution)/shard_map/ppermute | solution.py:68
  290.0 10.3 %multiply_convert_fusion = bf16[1024,1024]{0,1:T(8,128)(2,1)S(1)} fusion(f32[1024,1024]{0,1:T(8,128)S(1)} %get-tuple-element.120, bf16[1024,256]{0,1:T(8,128)(2,1)S(1)} %convolution_convert_fusion.4, f32[1024]{0:T(1024)S(1)} %get-tuple-element.121, f32[1024]{0:T(1024)S(1)} %log_add_fusion, s32[1024]{0:T(1024)S(1)} %get-tuple-element.113, ...), kind=kOutput, calls=%fused_computation.64 | convolution fusion | flops 543162368 | bytes 7356416 | tf_op jit(solution)/shard_map/dot_general | solution.py:18
  303.8 20.5 %multiply_convert_fusion.1 = (bf16[1024,1024]{0,1:T(8,128)(2,1)}, f32[1024,1024]{0,1:T(8,128)}, f32[1024,1024]{0,1:T(8,128)}) fusion(f32[1024]{0:T(1024)S(1)} %dynamic_slice.351, bf16[512,1024]{1,0:T(8,128)(2,1)S(1)} %get-tuple-element.51, bf16[512,1024]{1,0:T(8,128)(2,1)S(1)} %get-tuple-element.50, bf16[512,1024]{1,0:T(8,128)(2,1)S(1)} %get-tuple-element.49, ...), kind=kOutput, calls=%fused_computation.68 | convolution fusion | flops 4399824896 | bytes 18903040 | tf_op jit(solution)/shard_map/dot_general | solution.py:18
  324.3 6.6 convolution_convert_fusion
  332.4 20.7 %collective-permute-start.58 = (bf16[2,2,4,64,1024]{4,3,2,1,0:T(8,128)(2,1)}, bf16[2,2,4,64,1024]{4,3,2,1,0:T(8,128)(2,1)}, u32[]{:S(2)}, u32[]{:S(2)}) collective-permute-start(bf16[2,2,4,64,1024]{4,3,2,1,0:T(8,128)(2,1)} %dynamic-slice_bitcast_fusion), channel_id=1, source_target_pairs={{0,4},{4,0},{8,12},{12,8},{16,20},{20,16},{24,28},{28,24},{1,5},{5... | collective-permute-start | bytes 6291464 | tf_op jit(solution)/shard_map/ppermute | solution.py:68
  357.7 11.2 %convert_reduce_fusion.1 = (f32[1024]{0:T(1024)S(1)}, bf16[1024,1024]{0,1:T(8,128)(2,1)}) fusion(f32[1024,1024]{0,1:T(8,128)} %get-tuple-element.22, bf16[512,1024]{1,0:T(8,128)(2,1)} %get-tuple-element.47, bf16[512,1024]{1,0:T(8,128)(2,1)} %get-tuple-element.46, bf16[512,1024]{1,0:T(8,128)(2,1)} %get-tuple-element.45, ...), kind=kOutput, calls=%fused_computation.59 | convolution fusion | flops 4337957888 | bytes 18882560 | tf_op jit(solution)/shard_map/dot_general | solution.py:18
  368.9 7.9 convolution_convert_fusion.1
  387.2 8.7 %fusion.93 = f32[1024,2048]{1,0:T(8,128)} fusion(bf16[1024,768]{0,1:T(8,128)(2,1)S(1)} %fusion.45, bf16[512,768]{1,0:T(8,128)(2,1)S(1)} %copy-done.53, bf16[512,768]{1,0:T(8,128)(2,1)S(1)} %copy-done.51, bf16[512,768]{1,0:T(8,128)(2,1)S(1)} %copy-done.49, bf16[512,768]{1,0:T(8,128)(2,1)S(1)} %copy-done.47), kind=kOutput, calls=%fused_computation.216 | convolution fusion | flops 3233808384 | bytes 13107200 | tf_op jit(solution)/shard_map/dot_general | solution.py:18
  395.9 14.9 %fusion.172 = (f32[2048]{0:T(1024)S(1)}, f32[2048]{0:T(1024)S(1)}, f32[1024,2048]{1,0:T(8,128)}, f32[2048]{0:T(1024)}, f32[2048]{0:T(1024)}) fusion(f32[1024]{0:T(1024)S(1)} %add_rsqrt_fusion, f32[1024]{0:T(1024)S(1)} %broadcast_multiply_fusion, bf16[512,2048]{1,0:T(8,128)(2,1)} %collective-permute-done.6, bf16[512,2048]{1,0:T(8,128)(2,1)} %broadcast_select_fusion.5, ...), kind=kOutput, calls=%fused_computation.377 | convolution fusion | flops 4343193600 | bytes 27320320 | tf_op jit(solution)/shard_map/dot_general | solution.py:18
  416.3 6.8 convolution_convert_fusion.2
  437.2 27.8 %collective-permute-start.22 = (bf16[512,2048]{1,0:T(8,128)(2,1)S(1)}, bf16[512,2048]{1,0:T(8,128)(2,1)S(1)}, u32[]{:S(2)}, u32[]{:S(2)}) collective-permute-start(bf16[512,2048]{1,0:T(8,128)(2,1)S(1)} %slice.234), channel_id=1, source_target_pairs={{0,16},{4,20},{8,24},{12,28},{16,0},{20,4},{24,8},{28,12},{1,17},{... | collective-permute-start | bytes 6291464 | tf_op jit(solution)/shard_map/ppermute | solution.py:68
  477.0 11.7 %collective-permute-done.44 = bf16[2,4,64,768]{3,2,1,0:T(8,128)(2,1)S(1)} collective-permute-done((bf16[2,4,64,768]{3,2,1,0:T(8,128)(2,1)S(1)}, bf16[2,4,64,768]{3,2,1,0:T(8,128)(2,1)S(1)}, u32[]{:S(2)}, u32[]{:S(2)}) %collective-permute-start.44) | collective-permute-done | bytes 786464 | tf_op jit(solution)/shard_map/ppermute | solution.py:68
  489.0 5.7 collective-permute-start.46
  546.1 21.5 %collective-permute-done.60 = bf16[2,64,1024]{2,1,0:T(8,128)(2,1)S(1)} collective-permute-done((bf16[2,64,1024]{2,1,0:T(8,128)(2,1)S(1)}, bf16[2,64,1024]{2,1,0:T(8,128)(2,1)S(1)}, u32[]{:S(2)}, u32[]{:S(2)}) %collective-permute-start.60) | collective-permute-done | bytes 262176 | tf_op jit(solution)/shard_map/ppermute | solution.py:68
  567.7 10.7 %collective-permute-start.56 = (bf16[2,64,1024]{2,1,0:T(8,128)(2,1)S(1)}, bf16[2,64,1024]{2,1,0:T(8,128)(2,1)S(1)}, u32[]{:S(2)}, u32[]{:S(2)}) collective-permute-start(bf16[2,64,1024]{2,1,0:T(8,128)(2,1)S(1)} %get-tuple-element.93), channel_id=1, source_target_pairs={{0,3},{4,7},{8,11},{12,15},{16,19},{20,23},{24,27},{28,31},{1,0},{... | collective-permute-start | bytes 786440 | tf_op jit(solution)/shard_map/ppermute | solution.py:68
  587.3 17.1 %collective-permute-done.55 = bf16[2,64,1024]{2,1,0:T(8,128)(2,1)S(1)} collective-permute-done((bf16[2,64,1024]{2,1,0:T(8,128)(2,1)S(1)}, bf16[2,64,1024]{2,1,0:T(8,128)(2,1)S(1)}, u32[]{:S(2)}, u32[]{:S(2)}) %collective-permute-start.55) | collective-permute-done | bytes 262176 | tf_op jit(solution)/shard_map/ppermute | solution.py:68
  618.3 17.5 %collective-permute-done.39 = bf16[512,2048]{1,0:T(8,128)(2,1)S(1)} collective-permute-done((bf16[512,2048]{1,0:T(8,128)(2,1)S(1)}, bf16[512,2048]{1,0:T(8,128)(2,1)S(1)}, u32[]{:S(2)}, u32[]{:S(2)}) %collective-permute-start.39) | collective-permute-done | bytes 2097184 | tf_op jit(solution)/shard_map/ppermute | solution.py:68
  641.0 17.2 %collective-permute-done.25 = bf16[512,2048]{1,0:T(8,128)(2,1)S(1)} collective-permute-done((bf16[512,2048]{1,0:T(8,128)(2,1)S(1)}, bf16[512,2048]{1,0:T(8,128)(2,1)S(1)}, u32[]{:S(2)}, u32[]{:S(2)}) %collective-permute-start.25) | collective-permute-done | bytes 2097184 | tf_op jit(solution)/shard_map/ppermute | solution.py:68
  668.6 5.6 collective-permute-done.28
  683.7 120.1 %all-reduce.2.cloned.1.call-done = f32[24576]{0:T(1024)} async-done(((f32[24576]{0:T(1024)}), f32[24576]{0:T(1024)}) %all-reduce.2.cloned.1.call-update) | async-done | bytes 98320 | tf_op jit(solution)/shard_map/psum | solution.py:305
  (459 shorter events, 292.5 us)
Async XLA Ops:
  7.2 796.6 %all-reduce.2.cloned.1.call-start = ((), (), s32[]{:S(2)}) async-start(), calls=%async_computation | async-start | bytes 196608 | tf_op jit(solution)/shard_map/psum | solution.py:305
  11.3 34.3 %collective-permute-start.29 = (bf16[128,2048]{1,0:T(8,128)(2,1)}, bf16[128,2048]{1,0:T(8,128)(2,1)}, u32[]{:S(2)}, u32[]{:S(2)}) collective-permute-start(bf16[128,2048]{1,0:T(8,128)(2,1)} %bitcast.278), channel_id=1, source_target_pairs={{4,0},{20,16},{13,9},{29,25},{10,14},{26,30},{3,7},{19,23}} | collective-permute-start | bytes 1572872 | tf_op jit(solution)/shard_map/ppermute | solution.py:68
  12.6 33.6 %collective-permute-start.30 = (bf16[128,2048]{1,0:T(8,128)(2,1)}, bf16[128,2048]{1,0:T(8,128)(2,1)}, u32[]{:S(2)}, u32[]{:S(2)}) collective-permute-start(bf16[128,2048]{1,0:T(8,128)(2,1)} %bitcast.279), channel_id=1, source_target_pairs={{8,0},{24,16},{1,9},{17,25},{6,14},{22,30},{15,7},{31,23}} | collective-permute-start | bytes 1572872 | tf_op jit(solution)/shard_map/ppermute | solution.py:68
  16.1 31.6 %collective-permute-start.31 = (bf16[128,2048]{1,0:T(8,128)(2,1)}, bf16[128,2048]{1,0:T(8,128)(2,1)}, u32[]{:S(2)}, u32[]{:S(2)}) collective-permute-start(bf16[128,2048]{1,0:T(8,128)(2,1)} %bitcast.280), channel_id=1, source_target_pairs={{12,0},{28,16},{5,9},{21,25},{2,14},{18,30},{11,7},{27,23}} | collective-permute-start | bytes 1572872 | tf_op jit(solution)/shard_map/ppermute | solution.py:68
  25.0 87.9 %collective-permute-start.12 = (bf16[128,1024]{1,0:T(8,128)(2,1)}, bf16[128,1024]{1,0:T(8,128)(2,1)S(1)}, u32[]{:S(2)}, u32[]{:S(2)}) collective-permute-start(bf16[128,1024]{1,0:T(8,128)(2,1)} %get-tuple-element.29), channel_id=1, source_target_pairs={{0,1},{4,5},{8,9},{12,13},{16,17},{20,21},{24,25},{28,29},{1,2},{5... | collective-permute-start | bytes 786440 | tf_op jit(solution)/shard_map/ppermute | solution.py:68
  29.9 30.1 %collective-permute-start.3 = (bf16[512,2048]{1,0:T(8,128)(2,1)}, bf16[512,2048]{1,0:T(8,128)(2,1)}, u32[]{:S(2)}, u32[]{:S(2)}) collective-permute-start(bf16[512,2048]{1,0:T(8,128)(2,1)} %pad_maximum_fusion.8), channel_id=1, source_target_pairs={{0,1},{16,17},{7,6},{23,22},{9,10},{25,26},{14,15},{30,31}} | collective-permute-start | bytes 6291464 | tf_op jit(solution)/shard_map/ppermute | solution.py:68
  50.6 104.1 %collective-permute-start.32 = (bf16[512,2048]{1,0:T(8,128)(2,1)}, bf16[512,2048]{1,0:T(8,128)(2,1)}, u32[]{:S(2)}, u32[]{:S(2)}) collective-permute-start(bf16[512,2048]{1,0:T(8,128)(2,1)} %pad_maximum_fusion.9), channel_id=1, source_target_pairs={{0,1},{16,17},{7,6},{23,22},{9,10},{25,26},{14,15},{30,31}} | collective-permute-start | bytes 6291464 | tf_op jit(solution)/shard_map/ppermute | solution.py:68
  63.8 96.6 %collective-permute-start.4 = (bf16[512,2048]{1,0:T(8,128)(2,1)}, bf16[512,2048]{1,0:T(8,128)(2,1)}, u32[]{:S(2)}, u32[]{:S(2)}) collective-permute-start(bf16[512,2048]{1,0:T(8,128)(2,1)} %broadcast_select_fusion.1), channel_id=1, source_target_pairs={{1,2},{17,18},{6,5},{22,21},{10,11},{9,8},{26,27},{25,24},{14,13},... | collective-permute-start | bytes 6291464 | tf_op jit(solution)/shard_map/ppermute | solution.py:68
  66.8 47.2 %collective-permute-start.13 = (bf16[128,1024]{1,0:T(8,128)(2,1)}, bf16[128,1024]{1,0:T(8,128)(2,1)S(1)}, u32[]{:S(2)}, u32[]{:S(2)}) collective-permute-start(bf16[128,1024]{1,0:T(8,128)(2,1)} %get-tuple-element.31), channel_id=1, source_target_pairs={{0,2},{4,6},{8,10},{12,14},{16,18},{20,22},{24,26},{28,30},{1,3},{... | collective-permute-start | bytes 786440 | tf_op jit(solution)/shard_map/ppermute | solution.py:68
  114.1 39.0 %collective-permute-start.10 = (bf16[3,1,128,768]{3,2,1,0:T(8,128)(2,1)S(1)}, bf16[3,1,128,768]{3,2,1,0:T(8,128)(2,1)S(1)}, u32[]{:S(2)}, u32[]{:S(2)}) collective-permute-start(bf16[3,1,128,768]{3,2,1,0:T(8,128)(2,1)S(1)} %maximum_bitcast_fusion.3), channel_id=1, source_target_pairs={{0,8},{4,12},{8,0},{12,4},{16,24},{20,28},{24,16},{28,20},{1,9},{5... | collective-permute-start | bytes 1769480 | tf_op jit(solution)/shard_map/ppermute | solution.py:68
  136.1 29.6 %collective-permute-start.15 = (bf16[3,1,128,1024]{3,2,1,0:T(8,128)(2,1)S(1)}, bf16[3,1,128,1024]{3,2,1,0:T(8,128)(2,1)S(1)}, u32[]{:S(2)}, u32[]{:S(2)}) collective-permute-start(bf16[3,1,128,1024]{3,2,1,0:T(8,128)(2,1)S(1)} %maximum_bitcast_fusion.1), channel_id=1, source_target_pairs={{0,8},{4,12},{8,0},{12,4},{16,24},{20,28},{24,16},{28,20},{1,9},{5... | collective-permute-start | bytes 2359304 | tf_op jit(solution)/shard_map/ppermute | solution.py:68
  175.1 32.1 %collective-permute-start.21 = (bf16[3,2,128,1024]{3,2,1,0:T(8,128)(2,1)}, bf16[3,2,128,1024]{3,2,1,0:T(8,128)(2,1)}, u32[]{:S(2)}, u32[]{:S(2)}) collective-permute-start(bf16[3,2,128,1024]{3,2,1,0:T(8,128)(2,1)} %pad_maximum_fusion.11), channel_id=1, source_target_pairs={{0,4},{4,0},{8,12},{12,8},{16,20},{20,16},{24,28},{28,24},{1,5},{5... | collective-permute-start | bytes 4718600 | tf_op jit(solution)/shard_map/ppermute | solution.py:68
  188.3 34.9 %collective-permute-start.34 = (bf16[512,2048]{1,0:T(8,128)(2,1)}, bf16[512,2048]{1,0:T(8,128)(2,1)}, u32[]{:S(2)}, u32[]{:S(2)}) collective-permute-start(bf16[512,2048]{1,0:T(8,128)(2,1)} %broadcast_select_fusion.2), channel_id=1, source_target_pairs={{2,3},{18,19},{5,4},{21,20},{13,12},{29,28}} | collective-permute-start | bytes 6291464 | tf_op jit(solution)/shard_map/ppermute | solution.py:68
  193.9 48.8 %collective-permute-start.6 = (bf16[512,2048]{1,0:T(8,128)(2,1)}, bf16[512,2048]{1,0:T(8,128)(2,1)}, u32[]{:S(2)}, u32[]{:S(2)}) collective-permute-start(bf16[512,2048]{1,0:T(8,128)(2,1)} %broadcast_select_fusion.5), channel_id=1, source_target_pairs={{0,16},{4,20},{8,24},{12,28},{16,0},{20,4},{24,8},{28,12},{1,17},{... | collective-permute-start | bytes 6291464 | tf_op jit(solution)/shard_map/ppermute | solution.py:68
  225.0 61.7 %collective-permute-start.35 = (bf16[512,2048]{1,0:T(8,128)(2,1)S(1)}, bf16[512,2048]{1,0:T(8,128)(2,1)S(1)}, u32[]{:S(2)}, u32[]{:S(2)}) collective-permute-start(bf16[512,2048]{1,0:T(8,128)(2,1)S(1)} %broadcast_select_fusion.4), channel_id=1, source_target_pairs={{0,16},{4,20},{8,24},{12,28},{16,0},{20,4},{24,8},{28,12},{1,17},{... | collective-permute-start | bytes 6291464 | tf_op jit(solution)/shard_map/ppermute | solution.py:68
  332.4 135.9 %collective-permute-start.58 = (bf16[2,2,4,64,1024]{4,3,2,1,0:T(8,128)(2,1)}, bf16[2,2,4,64,1024]{4,3,2,1,0:T(8,128)(2,1)}, u32[]{:S(2)}, u32[]{:S(2)}) collective-permute-start(bf16[2,2,4,64,1024]{4,3,2,1,0:T(8,128)(2,1)} %dynamic-slice_bitcast_fusion), channel_id=1, source_target_pairs={{0,4},{4,0},{8,12},{12,8},{16,20},{20,16},{24,28},{28,24},{1,5},{5... | collective-permute-start | bytes 6291464 | tf_op jit(solution)/shard_map/ppermute | solution.py:68
  378.6 116.2 %collective-permute-start.52 = (bf16[2,2,4,64,1024]{4,3,2,1,0:T(8,128)(2,1)}, bf16[2,2,4,64,1024]{4,3,2,1,0:T(8,128)(2,1)}, u32[]{:S(2)}, u32[]{:S(2)}) collective-permute-start(bf16[2,2,4,64,1024]{4,3,2,1,0:T(8,128)(2,1)} %dynamic-slice_bitcast_fusion.1), channel_id=1, source_target_pairs={{0,4},{4,0},{8,12},{12,8},{16,20},{20,16},{24,28},{28,24},{1,5},{5... | collective-permute-start | bytes 6291464 | tf_op jit(solution)/shard_map/ppermute | solution.py:68
  382.7 41.7 %collective-permute-start.49 = (bf16[2,64,2048]{2,1,0:T(8,128)(2,1)}, bf16[2,64,2048]{2,1,0:T(8,128)(2,1)S(1)}, u32[]{:S(2)}, u32[]{:S(2)}) collective-permute-start(bf16[2,64,2048]{2,1,0:T(8,128)(2,1)} %dynamic-slice_bitcast_fusion.10), channel_id=1, source_target_pairs={{0,4},{4,0},{8,12},{12,8},{16,20},{20,16},{24,28},{28,24},{1,5},{5... | collective-permute-start | bytes 1572872 | tf_op jit(solution)/shard_map/ppermute | solution.py:68
  414.6 58.5 %collective-permute-start.36 = (bf16[512,2048]{1,0:T(8,128)(2,1)}, bf16[512,2048]{1,0:T(8,128)(2,1)}, u32[]{:S(2)}, u32[]{:S(2)}) collective-permute-start(bf16[512,2048]{1,0:T(8,128)(2,1)} %slice.233), channel_id=1, source_target_pairs={{0,16},{4,20},{8,24},{12,28},{16,0},{20,4},{24,8},{28,12},{1,17},{... | collective-permute-start | bytes 6291464 | tf_op jit(solution)/shard_map/ppermute | solution.py:68
  424.4 41.5 %collective-permute-start.43 = (bf16[2,2,4,64,768]{4,3,2,1,0:T(8,128)(2,1)}, bf16[2,2,4,64,768]{4,3,2,1,0:T(8,128)(2,1)}, u32[]{:S(2)}, u32[]{:S(2)}) collective-permute-start(bf16[2,2,4,64,768]{4,3,2,1,0:T(8,128)(2,1)} %dynamic-slice_bitcast_fusion.2), channel_id=1, source_target_pairs={{0,4},{4,0},{8,12},{12,8},{16,20},{20,16},{24,28},{28,24},{1,5},{5... | collective-permute-start | bytes 4718600 | tf_op jit(solution)/shard_map/ppermute | solution.py:68
  437.2 73.4 %collective-permute-start.22 = (bf16[512,2048]{1,0:T(8,128)(2,1)S(1)}, bf16[512,2048]{1,0:T(8,128)(2,1)S(1)}, u32[]{:S(2)}, u32[]{:S(2)}) collective-permute-start(bf16[512,2048]{1,0:T(8,128)(2,1)S(1)} %slice.234), channel_id=1, source_target_pairs={{0,16},{4,20},{8,24},{12,28},{16,0},{20,4},{24,8},{28,12},{1,17},{... | collective-permute-start | bytes 6291464 | tf_op jit(solution)/shard_map/ppermute | solution.py:68
  471.2 62.8 %collective-permute-start.59 = (bf16[2,4,64,1024]{3,2,1,0:T(8,128)(2,1)S(1)}, bf16[2,4,64,1024]{3,2,1,0:T(8,128)(2,1)}, u32[]{:S(2)}, u32[]{:S(2)}) collective-permute-start(bf16[2,4,64,1024]{3,2,1,0:T(8,128)(2,1)S(1)} %dynamic-slice_bitcast_fusion.3), channel_id=1, source_target_pairs={{0,8},{4,12},{8,0},{12,4},{16,24},{20,28},{24,16},{28,20},{1,9},{5... | collective-permute-start | bytes 3145736 | tf_op jit(solution)/shard_map/ppermute | solution.py:68
  500.0 39.1 %collective-permute-start.53 = (bf16[2,4,64,1024]{3,2,1,0:T(8,128)(2,1)}, bf16[2,4,64,1024]{3,2,1,0:T(8,128)(2,1)}, u32[]{:S(2)}, u32[]{:S(2)}) collective-permute-start(bf16[2,4,64,1024]{3,2,1,0:T(8,128)(2,1)} %dynamic-slice_bitcast_fusion.4), channel_id=1, source_target_pairs={{0,8},{4,12},{8,0},{12,4},{16,24},{20,28},{24,16},{28,20},{1,9},{5... | collective-permute-start | bytes 3145736 | tf_op jit(solution)/shard_map/ppermute | solution.py:68
  505.1 37.1 %collective-permute-start.37 = (bf16[512,2048]{1,0:T(8,128)(2,1)}, bf16[512,2048]{1,0:T(8,128)(2,1)}, u32[]{:S(2)}, u32[]{:S(2)}) collective-permute-start(bf16[512,2048]{1,0:T(8,128)(2,1)} %fusion.14), channel_id=1, source_target_pairs={{3,2},{19,18},{4,5},{20,21},{12,13},{28,29}} | collective-permute-start | bytes 6291464 | tf_op jit(solution)/shard_map/ppermute | solution.py:68
  512.7 65.9 %collective-permute-start.23 = (bf16[512,2048]{1,0:T(8,128)(2,1)}, bf16[512,2048]{1,0:T(8,128)(2,1)}, u32[]{:S(2)}, u32[]{:S(2)}) collective-permute-start(bf16[512,2048]{1,0:T(8,128)(2,1)} %fusion.15), channel_id=1, source_target_pairs={{3,2},{19,18},{4,5},{20,21},{12,13},{28,29}} | collective-permute-start | bytes 6291464 | tf_op jit(solution)/shard_map/ppermute | solution.py:68
  536.0 31.6 %collective-permute-start.60 = (bf16[2,64,1024]{2,1,0:T(8,128)(2,1)S(1)}, bf16[2,64,1024]{2,1,0:T(8,128)(2,1)S(1)}, u32[]{:S(2)}, u32[]{:S(2)}) collective-permute-start(bf16[2,64,1024]{2,1,0:T(8,128)(2,1)S(1)} %get-tuple-element.91), channel_id=1, source_target_pairs={{0,1},{4,5},{8,9},{12,13},{16,17},{20,21},{24,25},{28,29},{1,2},{5... | collective-permute-start | bytes 786440 | tf_op jit(solution)/shard_map/ppermute | solution.py:68
  536.7 30.9 %collective-permute-start.61 = (bf16[2,64,1024]{2,1,0:T(8,128)(2,1)S(1)}, bf16[2,64,1024]{2,1,0:T(8,128)(2,1)S(1)}, u32[]{:S(2)}, u32[]{:S(2)}) collective-permute-start(bf16[2,64,1024]{2,1,0:T(8,128)(2,1)S(1)} %get-tuple-element.90), channel_id=1, source_target_pairs={{0,2},{4,6},{8,10},{12,14},{16,18},{20,22},{24,26},{28,30},{1,3},{... | collective-permute-start | bytes 786440 | tf_op jit(solution)/shard_map/ppermute | solution.py:68
  545.2 60.9 %collective-permute-start.38 = (bf16[512,2048]{1,0:T(8,128)(2,1)S(1)}, bf16[512,2048]{1,0:T(8,128)(2,1)S(1)}, u32[]{:S(2)}, u32[]{:S(2)}) collective-permute-start(bf16[512,2048]{1,0:T(8,128)(2,1)S(1)} %add_convert_fusion.2), channel_id=1, source_target_pairs={{2,1},{18,17},{5,6},{21,22},{11,10},{8,9},{27,26},{24,25},{13,14},... | collective-permute-start | bytes 6291464 | tf_op jit(solution)/shard_map/ppermute | solution.py:68
  567.6 36.7 %collective-permute-start.55 = (bf16[2,64,1024]{2,1,0:T(8,128)(2,1)S(1)}, bf16[2,64,1024]{2,1,0:T(8,128)(2,1)S(1)}, u32[]{:S(2)}, u32[]{:S(2)}) collective-permute-start(bf16[2,64,1024]{2,1,0:T(8,128)(2,1)S(1)} %get-tuple-element.94), channel_id=1, source_target_pairs={{0,2},{4,6},{8,10},{12,14},{16,18},{20,22},{24,26},{28,30},{1,3},{... | collective-permute-start | bytes 786440 | tf_op jit(solution)/shard_map/ppermute | solution.py:68
  567.7 36.7 %collective-permute-start.56 = (bf16[2,64,1024]{2,1,0:T(8,128)(2,1)S(1)}, bf16[2,64,1024]{2,1,0:T(8,128)(2,1)S(1)}, u32[]{:S(2)}, u32[]{:S(2)}) collective-permute-start(bf16[2,64,1024]{2,1,0:T(8,128)(2,1)S(1)} %get-tuple-element.93), channel_id=1, source_target_pairs={{0,3},{4,7},{8,11},{12,15},{16,19},{20,23},{24,27},{28,31},{1,0},{... | collective-permute-start | bytes 786440 | tf_op jit(solution)/shard_map/ppermute | solution.py:68
  583.7 30.2 %collective-permute-start.24 = (bf16[512,2048]{1,0:T(8,128)(2,1)S(1)}, bf16[512,2048]{1,0:T(8,128)(2,1)S(1)}, u32[]{:S(2)}, u32[]{:S(2)}) collective-permute-start(bf16[512,2048]{1,0:T(8,128)(2,1)S(1)} %add_convert_fusion.6), channel_id=1, source_target_pairs={{2,1},{18,17},{5,6},{21,22},{11,10},{8,9},{27,26},{24,25},{13,14},... | collective-permute-start | bytes 6291464 | tf_op jit(solution)/shard_map/ppermute | solution.py:68
  614.8 43.4 %collective-permute-start.25 = (bf16[512,2048]{1,0:T(8,128)(2,1)S(1)}, bf16[512,2048]{1,0:T(8,128)(2,1)S(1)}, u32[]{:S(2)}, u32[]{:S(2)}) collective-permute-start(bf16[512,2048]{1,0:T(8,128)(2,1)S(1)} %add_convert_fusion.5), channel_id=1, source_target_pairs={{1,0},{17,16},{6,7},{22,23},{10,9},{26,25},{15,14},{31,30}} | collective-permute-start | bytes 6291464 | tf_op jit(solution)/shard_map/ppermute | solution.py:68
  (117 other events, 2368.9 us)
Sparse Core Ops, SparseCore 0:
  679.3 124.3 all-reduce.1

commit v2 on v1

v2 whole, which is shorter than its diff:
```python
import functools

import jax
import jax.numpy as jnp
from jax import lax
from jax.experimental import pallas as pl
from jax.experimental.pallas import tpu as pltpu
from jax.sharding import PartitionSpec as P

H = 8
HD = 256
ROT = 64
AXES = ("ctx", "shard")
MESH = pl.DeviceIdType.MESH

norm_epsilon = 1e-05
masked_score = -1e30
contract_last = (((1,), (1,)), ((), ()))
contract_first = (((0,), (0,)), ((), ()))


def dot32(left, right, dims=(((1,), (0,)), ((), ()))):
    return lax.dot_general(left, right, dims, preferred_element_type=jnp.float32)


def normalize(values):
    center = values - jnp.mean(values, axis=-1, keepdims=True)
    spread = jnp.mean(center * center, axis=-1, keepdims=True)
    scale = lax.rsqrt(spread + norm_epsilon)
    return center * scale, scale


def rotary(values, positions):
    half_rot = ROT // 2
    inv_freq = 10000.0 ** (-(jnp.arange(half_rot, dtype=jnp.float32) * 2.0) / ROT)
    angles = positions.astype(jnp.float32)[:, None] * inv_freq[None, :]
    cosine = jnp.cos(angles)
    sine = jnp.sin(angles)
    first_half = values[:, :half_rot]
    second_half = values[:, half_rot:ROT]
    return jnp.concatenate(
        [
            first_half * cosine - second_half * sine,
            second_half * cosine + first_half * sine,
            values[:, ROT:],
        ],
        axis=-1,
    )


def exact_gelu(values):
    return jax.nn.gelu(values, approximate=False)


class Layout:
    def __init__(self, mesh):
        self.nz = mesh.shape["shard"]
        self.nc = mesh.shape["ctx"]
        self.nlo = self.nz
        self.nhi = self.nc // self.nlo
        assert self.nhi == 2 and self.nz * self.nhi == self.nc
        self.bits = [1 << b for b in range(self.nlo.bit_length() - 1)]
        assert 1 << len(self.bits) == self.nlo
        self.seq_of_lo = [
            lo // 2 if lo % 2 == 0 else self.nz - 1 - lo // 2 for lo in range(self.nlo)
        ]
        self.lo_of_seq = [self.seq_of_lo.index(s) for s in range(self.nz)]

    def flat(self, z, hi, lo):
        return (hi * self.nlo + lo) * self.nz + z


def flip(value, mask, count):
    bit = 1
    while bit < count:
        if mask & bit:
            value = value + bit - 2 * bit * ((value // bit) % 2)
        bit *= 2
    return value


def low_bit(mask):
    return mask & -mask


def place(lay):
    ctx = lax.axis_index("ctx")
    z = lax.axis_index("shard")
    return z, ctx // lay.nlo, ctx % lay.nlo


def remote(src, dst, send, recv, device):
    return pltpu.make_async_remote_copy(
        src_ref=src, dst_ref=dst, send_sem=send, recv_sem=recv, device_id=device, device_id_type=MESH
    )


def enter(devices):
    barrier = pltpu.get_barrier_semaphore()
    for device in devices:
        pl.semaphore_signal(barrier, inc=1, device_id=device, device_id_type=MESH)
    pl.semaphore_wait(barrier, len(devices))


def gather_schedule(order_w, nlo, by_bit, n_groups):
    w = [("W", g, i) for g, i in order_w]
    arrive = [("E", g, i, 0) for g, i in order_w]
    last = [("E", g, i, r) for r in by_bit for g, i in order_w]

    def tokens(a):
        events = [("D", a, 0)]
        for k in range(1, nlo):
            events += [("Z", a, k), ("D", a, k)]
        return events

    first, second = tokens(0), tokens(1)
    events = [("N", 0)] + first[:3] + [("N", 1)] + first[3:]
    k = 0
    for item in second:
        events += [item] + arrive[k : k + 2]
        k += 2
    events += arrive[k:] + last
    window, start = 3, 4
    schedule, k = [], window
    for n, item in enumerate(events):
        if n == start:
            schedule += w[:window]
        schedule.append(item)
        if item[0] == "E" and item[3] == 0 and k < len(w):
            schedule.append(w[k])
            k += 1
    return schedule


def gather_kernel(lay, sizes, tok, cot, qkv, up, down, seq_t, seq_c, w_qkv, w_up, w_down, stage_t, stage_c,
                  near_r, near_s, home_c, z_r, z_s, y_r, y_s, wz_r, wz_s, wf_r, wf_s):
    rows, width, weight_rows, ff, repeat = sizes
    nz, nlo, nhi = lay.nz, lay.nlo, lay.nhi
    z, hi, lo = place(lay)
    half, quarter = nlo * rows, weight_rows // nlo
    odd = lo % 2
    s = (1 - odd) * (lo // 2) + odd * (nz - 1 - lo // 2)

    def dev(z, hi, lo):
        return (hi * nlo + lo, z)

    enter(
        [dev((z + i) % nz, hi, lo) for i in range(1, nz)]
        + [dev(z, hi, flip(lo, r, nlo)) for r in range(1, nlo)]
        + [dev(z, 1 - hi, lo)]
    )

    groups = []
    for part in range(3):
        groups.append((qkv, w_qkv, lambda rank, part=part: part * width + (rank // repeat) * HD, part * HD, HD))
    groups.append((up, w_up, lambda rank: rank * ff, 0, ff))
    groups.append((down, w_down, lambda rank: rank * ff, 0, ff))
    bits = list(reversed(lay.bits))

    def weight_z(g, i):
        src, dst, column, at, wide = groups[g]
        to = (z + i) % nz
        first = pl.multiple_of(column(to * nhi + hi), 128)
        return remote(
            src.at[pl.ds(pl.multiple_of(lo * quarter, quarter), quarter), pl.ds(first, wide)],
            dst.at[pl.ds(pl.multiple_of(z * weight_rows + lo * quarter, quarter), quarter), pl.ds(at, wide)],
            wz_s.at[g, i - 1], wz_r.at[g, i - 1], dev(to, hi, lo),
        )

    def weight_forward(g, i, r, b):
        _, dst, _, at, wide = groups[g]
        row = ((z + nz - i) % nz) * weight_rows + flip(lo, r, nlo) * quarter
        piece = dst.at[pl.ds(pl.multiple_of(row, quarter), quarter), pl.ds(at, wide)]
        k = bits.index(b)
        return remote(piece, piece, wf_s.at[g, i - 1, r, k], wf_r.at[g, i - 1, r ^ b], dev(z, hi, flip(lo, b, nlo)))

    inputs, staged, sequences = (tok, cot), (stage_t, stage_c), (seq_t, seq_c)
    distance = jnp.abs(z - s)

    def home_of(seq):
        late = seq // (nz // 2)
        return (1 - late) * (2 * seq) + late * (2 * (nz - 1 - seq) + 1)

    def seq_rows(a, which, r):
        row = which * half + flip(lo, r, nlo) * rows
        return sequences[a].at[pl.ds(pl.multiple_of(row, rows), rows)]

    def along(a, src, seq, way):
        return remote(src, staged[a].at[seq], z_s.at[a, seq, way], z_r.at[a, seq], dev((z + 1 - 2 * way + nz) % nz, hi, lo))

    def near(a, src, seq):
        return remote(src, seq_rows(a, hi, 0), near_s.at[a, seq], near_r.at[a, lo], dev(z, hi, home_of(seq)))

    def near_arrival(a, r):
        piece = seq_rows(a, hi, r)
        return remote(piece, piece, near_s.at[a, 0], near_r.at[a, flip(lo, r, nlo)], dev(z, hi, flip(lo, r, nlo)))

    def stay(a, src):
        return pltpu.make_async_copy(src, seq_rows(a, hi, 0), home_c.at[a])

    def across(a, src, r):
        return remote(src, seq_rows(a, hi, r), y_s.at[a, r], y_r.at[a, r], dev(z, 1 - hi, lo))

    def across_arrival(a, r):
        piece = seq_rows(a, 1 - hi, r)
        return remote(piece, piece, y_s.at[a, r], y_r.at[a, r], dev(z, 1 - hi, lo))

    def sources(a):
        yield (z >= 0, inputs[a], z, z < nz - 1, z > 0)
        for k in range(1, nz):
            yield (z >= k, staged[a].at[(z + nz - k) % nz], (z + nz - k) % nz, z < nz - 1, z < 0)
            yield (z < nz - k, staged[a].at[(z + k) % nz], (z + k) % nz, z < 0, z > 0)

    def dispatch(a, which):
        valid, src, seq, up, down = list(sources(a))[which]

        @pl.when(valid & up)
        def _():
            along(a, src, seq, 0).start()

        @pl.when(valid & down)
        def _():
            along(a, src, seq, 1).start()

        @pl.when(valid & (lo == home_of(seq)))
        def _():
            across(a, src, 0).start()
            stay(a, src).start()

        @pl.when(valid & (lo != home_of(seq)))
        def _():
            near(a, src, seq).start()

    def settle(a, which):
        valid, src, seq, up, down = list(sources(a))[which]

        @pl.when(valid & up)
        def _():
            along(a, src, seq, 0).wait_send()

        @pl.when(valid & down)
        def _():
            along(a, src, seq, 1).wait_send()

        @pl.when(valid & (lo == home_of(seq)))
        def _():
            across(a, src, 0).wait_send()
            stay(a, src).wait()

        @pl.when(valid & (lo != home_of(seq)))
        def _():
            near(a, src, seq).wait_send()

    def chain_event(a, k):
        for which, valid, seq in ((2 * k - 1, z >= k, (z + nz - k) % nz), (2 * k, z < nz - k, (z + k) % nz)):
            @pl.when(valid)
            def _(seq=seq):
                along(a, staged[a].at[seq], seq, 0).wait_recv()

            dispatch(a, which)

    def near_event(a, d):
        @pl.when(distance == d)
        def _():
            for r in range(1, nlo):
                near_arrival(a, r).wait_recv()
                across(a, seq_rows(a, hi, r), r).start()

    def forward_from(g, i, r):
        for b in bits:
            if r == 0 or b < low_bit(r):
                weight_forward(g, i, r, b).start()

    def weight_event(g, i, r):
        if r == 0:
            weight_z(g, i).wait_recv()
        else:
            weight_forward(g, i, r ^ low_bit(r), low_bit(r)).wait_recv()
        forward_from(g, i, r)

    order_w = [(g, i) for g in range(len(groups)) for i in range(1, nz)]
    by_bit = sorted(range(1, nlo), key=lambda r: -low_bit(r))
    act = dict(N=lambda a: dispatch(a, 0), Z=chain_event, D=near_event, W=lambda g, i: weight_z(g, i).start(), E=weight_event)
    for item in gather_schedule(order_w, nlo, by_bit, len(groups)):
        act[item[0]](*item[1:])
    for a in range(2):
        for j in range(nlo):
            across_arrival(a, j).wait_recv()
    for g, i in order_w:
        weight_z(g, i).wait_send()
        for r in range(nlo):
            for b in bits:
                if r == 0 or b < low_bit(r):
                    weight_forward(g, i, r, b).wait_send()
    for a in range(2):
        for which in range(2 * nz - 1):
            settle(a, which)
        for r in range(1, nlo):
            across(a, seq_rows(a, hi, r), r).wait_send()


def gather_all(lay, tok, cot, qkv, up, down):
    rows, width = tok.shape
    nz, nlo = lay.nz, lay.nlo
    ranks = nz * lay.nhi
    ff = up.shape[1] // ranks
    repeat = max(1, ranks // H)
    sizes = (rows, width, qkv.shape[0], ff, repeat)
    bits = len(lay.bits)
    anywhere = pl.BlockSpec(memory_space=pl.ANY)
    dma = pltpu.SemaphoreType.DMA
    bf16 = jnp.bfloat16
    total = 2 * nlo * rows
    return pl.pallas_call(
        functools.partial(gather_kernel, lay, sizes),
        out_shape=[
            jax.ShapeDtypeStruct((total, width), bf16),
            jax.ShapeDtypeStruct((total, width), bf16),
            jax.ShapeDtypeStruct((width, 3 * HD), bf16),
            jax.ShapeDtypeStruct((width, ff), bf16),
            jax.ShapeDtypeStruct((width, ff), bf16),
            jax.ShapeDtypeStruct((nz, rows, width), bf16),
            jax.ShapeDtypeStruct((nz, rows, width), bf16),
        ],
        in_specs=[anywhere] * 5,
        out_specs=[anywhere] * 7,
        scratch_shapes=[
            dma((2, nlo)), dma((2, nz)), dma((2,)), dma((2, nz)), dma((2, nz, 2)), dma((2, nlo)), dma((2, nlo)),
            dma((5, nz - 1)), dma((5, nz - 1)), dma((5, nz - 1, nlo)), dma((5, nz - 1, nlo, bits)),
        ],
        compiler_params=pltpu.CompilerParams(collective_id=1, has_side_effects=True),
        name="gather_all",
    )(tok, cot, qkv, up, down)[:5]

def add_rows(into, left, right, step):
    rows = into.shape[0]
    step = min(step, rows)

    def body(k, carry):
        at = pl.ds(pl.multiple_of(k * step, step), step)
        into[at, :] = (left[at, :].astype(jnp.float32) + right[at, :].astype(jnp.float32)).astype(into.dtype)
        return carry

    lax.fori_loop(0, rows // step, body, 0)


def scatter_chunks(width, ff, repeat):
    cut = max(ff // 2, 256)
    chunks = []
    for source in (0, 1):
        for first in range(0, ff, cut):
            chunks.append((source, first, cut, lambda rank, first=first: rank * ff + first, True))
    for part in range(3):
        chunks.append((2, part * HD, HD, lambda rank, part=part: part * width + (rank // repeat) * HD, repeat == 1))
    return chunks


def scatter_schedule(nz, nlo, n_chunks, stages):
    schedule = [("Y", 0), ("M",), ("P",)] + [("C", g) for g in range(n_chunks)] + [("Y", 1)]
    schedule += [("X", g, 0) for g in range(3)]
    schedule += [("A", 0, q) for q in range(nlo)]
    schedule += [("X", g, 0) for g in range(3, n_chunks)]
    schedule += [("X", g, 1) for g in range(2)]
    chain = []
    for a in range(2):
        part = []
        for m in range(nz):
            if m < nz - 1:
                part.append(("B", a, nz - 1 - m, 0))
            if m < nz - 1:
                part.append(("B", a, m, 1))
        chain.append(part + [("F", a)])
    schedule += chain[0]
    schedule += [("A", 1, q) for q in range(nlo)]
    schedule += [("X", g, 1) for g in range(2, n_chunks)]
    schedule += chain[1]
    for t in range(2, stages):
        schedule += [("X", g, t) for g in range(n_chunks)]
    schedule += [("Q", t) for t in range(stages)] + [("N", t) for t in range(2 * stages + 1)]
    schedule += [("G", g) for g in range(n_chunks)]
    return schedule


def scatter_kernel(lay, sizes, *refs):
    rows, width, ff, repeat = sizes
    nz, nlo, nhi = lay.nz, lay.nlo, lay.nhi
    stages = len(lay.bits)
    chunks = scatter_chunks(width, ff, repeat)
    n = len(chunks)
    refs = list(refs)

    def take(count):
        taken = refs[:count]
        del refs[:count]
        return taken

    partial_o, partial_s, wg_down, wg_up, wg_qkv, wg_out, small = take(7)
    sum_o, sum_s, all_down, all_up, all_qkv, all_out, small_sum = take(7)
    own, across_buf, near_buf, up_buf, down_buf = take(5)
    acc = take(n)
    got = [take(stages) for _ in range(n)]
    out_acc, = take(1)
    out_got = take(stages)
    small_buf, small_got = take(2)
    (own_c, y_r, y_s, near_r, near_s, z_r, z_s, acc_c, st_r, st_s, g_r, g_s, keep_c,
     out_c, out_r, out_s, move_r, move_s, sm_r, sm_s) = take(20)

    z, hi, lo = place(lay)
    rank = z * nhi + hi
    half = nlo * rows
    grain = width // (nz * nhi * nlo)
    span = nz * grain

    def dev(z, hi, lo):
        return (hi * nlo + lo, z)

    ctx = hi * nlo + lo
    moves = (ctx != rank) | (z != lo)
    barrier = pltpu.get_barrier_semaphore()
    mates = [
        dev((z + dz) % nz, flip(hi, dh, nhi), lo) for dz in range(nz) for dh in range(nhi) if dz or dh
    ] + [dev(z, hi, flip(lo, r, nlo)) for r in range(1, nlo)]
    for device in mates:
        pl.semaphore_signal(barrier, inc=1, device_id=device, device_id_type=MESH)

    @pl.when(moves)
    def _():
        pl.semaphore_signal(barrier, inc=1, device_id=(rank, lo), device_id_type=MESH)
        pl.semaphore_signal(barrier, inc=1, device_id=dev(ctx // nhi, ctx % nhi, z), device_id_type=MESH)
        pl.semaphore_wait(barrier, len(mates) + 2)

    @pl.when(jnp.logical_not(moves))
    def _():
        pl.semaphore_wait(barrier, len(mates))

    partial, summed = (partial_o, partial_s), (sum_o, sum_s)

    def load_own(a):
        row = pl.multiple_of(hi * half, half)
        return pltpu.make_async_copy(
            partial[a].at[pl.ds(row, half)], own.at[a], own_c.at[a]
        )

    def across(a, q):
        row = pl.multiple_of((1 - hi) * half + q * rows, rows)
        return remote(
            partial[a].at[pl.ds(row, rows)], across_buf.at[a, q], y_s.at[a, q], y_r.at[a, q], dev(z, 1 - hi, lo)
        )

    def near(a, q):
        return remote(
            own.at[a, pl.ds(q * rows, rows)], near_buf.at[a, lo], near_s.at[a, q], near_r.at[a, lo], dev(z, hi, q)
        )

    def near_arrival(a, q):
        piece = near_buf.at[a, q]
        return remote(piece, piece, near_s.at[a, q], near_r.at[a, q], dev(z, hi, q))

    def along(a, seq, way):
        buf = (up_buf, down_buf)[way]
        return remote(
            near_buf.at[a, lay.lo_of_seq[seq]], buf.at[a, seq], z_s.at[a, seq], z_r.at[a, seq, way],
            dev((z + 1 - 2 * way + nz) % nz, hi, lo),
        )

    def start_across(a):
        load_own(a).start()
        for q in range(nlo):
            across(a, q).start()

    def across_event(a, q):
        if q == 0:
            load_own(a).wait()
        across(a, q).wait_recv()
        mine = own.at[a, pl.ds(q * rows, rows)]

        @pl.when(lo == q)
        def _():
            add_rows(near_buf.at[a, q], mine, across_buf.at[a, q], 16)

        @pl.when(lo != q)
        def _():
            add_rows(mine, mine, across_buf.at[a, q], 16)
            near(a, q).start()

    def chain_event(a, seq, way):
        q = lay.lo_of_seq[seq]
        active = (z < seq) if way == 0 else (z > seq)
        first = (z == 0) if way == 0 else (z == nz - 1)
        buf = (up_buf, down_buf)[way]

        @pl.when(active)
        def _():
            @pl.when(lo != q)
            def _():
                near_arrival(a, q).wait_recv()

            @pl.when(jnp.logical_not(first))
            def _():
                along(a, seq, way).wait_recv()
                add_rows(near_buf.at[a, q], near_buf.at[a, q], buf.at[a, seq], 16)

            along(a, seq, way).start()

    def final_event(a):
        late = z // (nz // 2)
        home = (1 - late) * (2 * z) + late * (2 * (nz - 1 - z) + 1)
        piece = near_buf.at[a, home]

        @pl.when(lo != home)
        def _():
            remote(piece, piece, near_s.at[a, 0], near_r.at[a, home], dev(z, hi, home)).wait_recv()

        @pl.when(z > 0)
        def _():
            arrived = up_buf.at[a, z]
            remote(arrived, arrived, z_s.at[a, 0], z_r.at[a, z, 0], dev(z, hi, lo)).wait_recv()

        @pl.when(z < nz - 1)
        def _():
            arrived = down_buf.at[a, z]
            remote(arrived, arrived, z_s.at[a, 0], z_r.at[a, z, 1], dev(z, hi, lo)).wait_recv()

        def body(k, carry):
            at = pl.ds(pl.multiple_of(k * 16, 16), 16)
            total = piece[at, :].astype(jnp.float32)
            total = total + jnp.where(z > 0, up_buf[a, z, at, :].astype(jnp.float32), 0.0)
            total = total + jnp.where(z < nz - 1, down_buf[a, z, at, :].astype(jnp.float32), 0.0)
            summed[a][at, :] = total
            return carry

        lax.fori_loop(0, rows // 16, body, 0)

    sources = (wg_down, wg_up, wg_qkv)
    targets = (all_down, all_up, all_qkv)

    def rows_of(g, h, rel):
        source, first, wide, _, _ = chunks[g]
        row = (h * nlo + flip(lo, rel, nlo)) * span
        return sources[source].at[pl.ds(pl.multiple_of(row, span), span), pl.ds(first, wide)]

    def load_acc(g, h, rel):
        return pltpu.make_async_copy(rows_of(g, h, rel), acc[g].at[h, rel // 2], acc_c.at[g, h, rel // 2])

    def stage_pieces(t):
        return [rel for rel in range(nlo) if rel % (2 << t) == (1 << t)]

    def stage_send(g, t, h, rel):
        src = rows_of(g, h, rel) if t == 0 else acc[g].at[h, rel // 2]
        k = rel >> (t + 1)
        return remote(
            src, got[g][t].at[h, k], st_s.at[g, t, h, k], st_r.at[g, t, h, k], dev(z, hi, flip(lo, 1 << t, nlo))
        )

    def stage_start(g, t):
        for h in range(nhi):
            for rel in stage_pieces(t):
                stage_send(g, t, h, rel).start()

    def start_chunk(g):
        stage_start(g, 0)
        for h in range(nhi):
            for rel in range(0, nlo, 2):
                load_acc(g, h, rel).start()

    def stage_event(g, t):
        order = list(reversed(range(0, nlo, 2 << t)))
        for h in range(nhi):
            for rel in order:
                k = rel >> (t + 1)
                if t == 0:
                    load_acc(g, h, rel).wait()
                stage_send(g, t, h, rel | (1 << t)).wait_recv()
                add_rows(acc[g].at[h, rel // 2], acc[g].at[h, rel // 2], got[g][t].at[h, k], 64)
                if t + 1 < stages and rel % (4 << t) == (2 << t):
                    stage_send(g, t + 1, h, rel).start()
        if t + 1 == stages:
            deliver(g)

    def owner_send(g, dz, dh):
        source, _, wide, column, _ = chunks[g]
        to_z, to_hi = (z + dz) % nz, flip(hi, dh, nhi)
        first = pl.multiple_of(column(rank), 128)
        k = dz * nhi + dh
        return remote(
            acc[g].at[to_hi, 0, pl.ds(pl.multiple_of(to_z * grain, grain), grain)],
            targets[source].at[:, pl.ds(first, wide)],
            g_s.at[g, k], g_r.at[g, k], dev(to_z, to_hi, lo),
        )

    def owner_arrival(g, dz, dh):
        source, _, wide, column, _ = chunks[g]
        from_z, from_hi = (z + nz - dz) % nz, flip(hi, dh, nhi)
        first = pl.multiple_of(column(from_z * nhi + from_hi), 128)
        piece = targets[source].at[:, pl.ds(first, wide)]
        k = dz * nhi + dh
        return remote(piece, piece, g_s.at[g, k], g_r.at[g, k], dev(from_z, from_hi, lo))

    def keep(g):
        source, _, wide, column, _ = chunks[g]
        first = pl.multiple_of(column(rank), 128)
        return pltpu.make_async_copy(
            acc[g].at[hi, 0, pl.ds(pl.multiple_of(z * grain, grain), grain)],
            targets[source].at[:, pl.ds(first, wide)], keep_c.at[g],
        )

    others = [(dz, dh) for dz in range(nz) for dh in range(nhi) if dz or dh]

    def when_sent(g, from_hi, act):
        if chunks[g][4]:
            act()
        else:
            pl.when(from_hi % repeat == 0)(act)

    def deliver(g):
        def act():
            for dz, dh in others:
                owner_send(g, dz, dh).start()
            keep(g).start()

        when_sent(g, hi, act)

    def finish_chunk(g):
        def sent():
            for dz, dh in others:
                owner_send(g, dz, dh).wait_send()
            keep(g).wait()

        when_sent(g, hi, sent)
        for dz, dh in others:
            when_sent(g, flip(hi, dh, nhi), lambda dz=dz, dh=dh: owner_arrival(g, dz, dh).wait_recv())

    def out_rows(rel):
        return wg_out.at[pl.ds(pl.multiple_of(flip(lo, rel, nlo) * grain, grain), grain)]

    def out_load(rel):
        return pltpu.make_async_copy(out_rows(rel), out_acc.at[rel // 2], out_c.at[rel // 2])

    def out_send(t, rel):
        src = out_rows(rel) if t == 0 else out_acc.at[rel // 2]
        k = rel >> (t + 1)
        return remote(src, out_got[t].at[k], out_s.at[t, k], out_r.at[t, k], dev(z, hi, flip(lo, 1 << t, nlo)))

    def out_start():
        for rel in stage_pieces(0):
            out_send(0, rel).start()
        for rel in range(0, nlo, 2):
            out_load(rel).start()

    def out_event(t):
        for rel in reversed(range(0, nlo, 2 << t)):
            if t == 0:
                out_load(rel).wait()
            out_send(t, rel | (1 << t)).wait_recv()
            add_rows(out_acc.at[rel // 2], out_acc.at[rel // 2], out_got[t].at[rel >> (t + 1)], 16)
            if t + 1 < stages and rel % (4 << t) == (2 << t):
                out_send(t + 1, rel).start()
        if t + 1 == stages:
            @pl.when(moves)
            def _():
                out_move().start()

            @pl.when(jnp.logical_not(moves))
            def _():
                out_stay().start()

    def out_move():
        return remote(out_acc.at[0], all_out, move_s, move_r, (rank, lo))

    def out_stay():
        return pltpu.make_async_copy(out_acc.at[0], all_out, move_s)

    doubling = (
        [dev(z, hi, flip(lo, b, nlo)) for b in lay.bits]
        + [dev(z, flip(hi, 1, nhi), lo)]
        + [dev(flip(z, b, nz), hi, lo) for b in lay.bits]
    )

    def small_send(t):
        src = small if t == 0 else small_buf.at[t - 1]
        return remote(src, small_got.at[t], sm_s.at[t], sm_r.at[t], doubling[t])

    def small_event(t):
        small_send(t).wait_recv()
        mine = small if t == 0 else small_buf.at[t - 1]
        into = small_sum if t + 1 == len(doubling) else small_buf.at[t]
        into[...] = mine[...] + small_got[t]
        if t + 1 < len(doubling):
            small_send(t + 1).start()

    act = dict(
        Y=start_across, A=across_event, B=chain_event, F=final_event, C=start_chunk, X=stage_event, G=finish_chunk,
        P=out_start, Q=out_event, M=lambda: small_send(0).start(), N=small_event,
    )
    for item in scatter_schedule(nz, nlo, n, stages):
        act[item[0]](*item[1:])

    for a in range(2):
        for q in range(nlo):
            across(a, q).wait_send()

            @pl.when(lo != q)
            def _(a=a, q=q):
                near(a, q).wait_send()

        for seq in range(nz):
            @pl.when(z != seq)
            def _(a=a, seq=seq):
                along(a, seq, 0).wait_send()

    for g in range(n):
        for t in range(stages):
            for h in range(nhi):
                for rel in stage_pieces(t):
                    stage_send(g, t, h, rel).wait_send()
    for t in range(stages):
        for rel in stage_pieces(t):
            out_send(t, rel).wait_send()

    @pl.when(moves)
    def _():
        out_move().wait()

    @pl.when(jnp.logical_not(moves))
    def _():
        out_stay().wait()

    for t in range(len(doubling)):
        small_send(t).wait_send()


def scatter_all(lay, partial_o, partial_s, wg_down, wg_up, wg_qkv, wg_out, small):
    total, width = partial_o.shape
    nz, nlo, nhi = lay.nz, lay.nlo, lay.nhi
    rows = total // (nhi * nlo)
    ranks = nz * nhi
    ff = wg_down.shape[1]
    repeat = max(1, ranks // H)
    grain = width // (ranks * nlo)
    span = nz * grain
    stages = len(lay.bits)
    chunks = scatter_chunks(width, ff, repeat)
    n = len(chunks)
    steps = 2 * stages + 1
    anywhere = pl.BlockSpec(memory_space=pl.ANY)
    inside = pl.BlockSpec(memory_space=pltpu.VMEM)
    dma = pltpu.SemaphoreType.DMA
    bf16, f32 = jnp.bfloat16, jnp.float32
    scratch = [
        pltpu.VMEM((2, nlo * rows, width), bf16),
        pltpu.VMEM((2, nlo, rows, width), bf16),
        pltpu.VMEM((2, nlo, rows, width), bf16),
        pltpu.VMEM((2, nz, rows, width), bf16),
        pltpu.VMEM((2, nz, rows, width), bf16),
    ]
    for chunk in chunks:
        scratch.append(pltpu.VMEM((nhi, nlo // 2, span, chunk[2]), bf16))
    for chunk in chunks:
        for t in range(stages):
            scratch.append(pltpu.VMEM((nhi, nlo >> (t + 1), span, chunk[2]), bf16))
    scratch.append(pltpu.VMEM((nlo // 2, grain, width), bf16))
    for t in range(stages):
        scratch.append(pltpu.VMEM((nlo >> (t + 1), grain, width), bf16))
    scratch += [pltpu.VMEM((steps,) + small.shape, f32), pltpu.VMEM((steps,) + small.shape, f32)]
    most = nlo // 2
    scratch += [
        dma((2,)), dma((2, nlo)), dma((2, nlo)), dma((2, nlo)), dma((2, nlo)), dma((2, nz, 2)), dma((2, nz)),
        dma((n, nhi, most)), dma((n, stages, nhi, most)), dma((n, stages, nhi, most)), dma((n, ranks)), dma((n, ranks)),
        dma((n,)), dma((most,)), dma((stages, most)), dma((stages, most)), dma, dma, dma((steps,)), dma((steps,)),
    ]
    return pl.pallas_call(
        functools.partial(scatter_kernel, lay, (rows, width, ff, repeat)),
        out_shape=[
            jax.ShapeDtypeStruct((rows, width), f32),
            jax.ShapeDtypeStruct((rows, width), f32),
            jax.ShapeDtypeStruct((grain, ff * ranks), bf16),
            jax.ShapeDtypeStruct((grain, ff * ranks), bf16),
            jax.ShapeDtypeStruct((grain, 3 * width), bf16),
            jax.ShapeDtypeStruct((grain, width), bf16),
            jax.ShapeDtypeStruct(small.shape, f32),
        ],
        in_specs=[anywhere] * 6 + [inside],
        out_specs=[inside, inside, anywhere, anywhere, anywhere, anywhere, inside],
        scratch_shapes=scratch,
        compiler_params=pltpu.CompilerParams(
            collective_id=2, has_side_effects=True, vmem_limit_bytes=60 * 1024 * 1024
        ),
        name="scatter_all",
    )(partial_o, partial_s, wg_down, wg_up, wg_qkv, wg_out, small)


def local_block(
    lay,
    tokens,
    qkv_weight,
    qkv_bias,
    out_weight,
    out_bias,
    up_weight,
    up_bias,
    down_weight,
    down_bias,
    attn_norm_gain,
    attn_norm_bias,
    mlp_norm_gain,
    mlp_norm_bias,
    cotangent,
):
    f32, bf16 = jnp.float32, jnp.bfloat16
    nz, nlo, nhi = lay.nz, lay.nlo, lay.nhi
    ranks = nz * nhi
    rows = tokens.shape[1]
    width = tokens.shape[2]
    hidden_width = up_weight.shape[1]
    weight_rows = qkv_weight.shape[0]
    half = nlo * rows
    ctx = lax.axis_index("ctx")
    z = lax.axis_index("shard")
    hi, lo = ctx // nlo, ctx % nlo
    rank = z * nhi + hi
    ff = hidden_width // ranks
    repeat = max(1, ranks // H)
    head = rank // repeat
    score_scale = HD ** (-0.5)
    own = tokens[0]
    own_cotangent = cotangent[0]
    seq_tokens, seq_cotangent, qkv_here, up_here, down_here = gather_all(
        lay, own, own_cotangent, qkv_weight, up_weight, down_weight
    )
    own_qkv = jnp.concatenate(
        [
            lax.dynamic_slice(qkv_weight, (0, part * width + head * HD), (weight_rows, HD))
            for part in range(3)
        ],
        axis=1,
    )
    own_up = lax.dynamic_slice(up_weight, (0, rank * ff), (weight_rows, ff))
    own_down = lax.dynamic_slice(down_weight, (0, rank * ff), (weight_rows, ff))
    qkv_here = lax.dynamic_update_slice(qkv_here, own_qkv, (z * weight_rows, 0))
    up_here = lax.dynamic_update_slice(up_here, own_up, (z * weight_rows, 0))
    down_here = lax.dynamic_update_slice(down_here, own_down, (z * weight_rows, 0))
    out_head = lax.dynamic_slice(out_weight, (head * HD - z * weight_rows, 0), (HD, width))
    out_rows = width // ranks
    out_at = rank * out_rows - head * HD

    positions = jnp.arange(2 * half, dtype=jnp.int32)

    normed, _ = normalize(seq_tokens.astype(f32))
    attn_in = (normed * attn_norm_gain + attn_norm_bias).astype(bf16)
    mlp_in = (normed * mlp_norm_gain + mlp_norm_bias).astype(bf16)
    bias_here = jnp.concatenate(
        [lax.dynamic_slice(qkv_bias, (part * width + head * HD,), (HD,)) for part in range(3)]
    )
    projected = dot32(attn_in, qkv_here) + bias_here
    queries = rotary(projected[:, :HD], positions).astype(bf16)
    keys = rotary(projected[:, HD : 2 * HD], positions).astype(bf16)
    values = projected[:, 2 * HD :].astype(bf16)
    causal = positions[:, None] >= positions[None, :]
    scores = jnp.where(causal, dot32(queries, keys, contract_last) * score_scale, masked_score)
    top = jnp.max(scores, axis=-1, keepdims=True)
    weights = jnp.where(causal, jnp.exp(scores - top), 0.0)
    total = jnp.sum(weights, axis=-1, keepdims=True)
    mixed_full = dot32(weights.astype(bf16), values) / total
    log_total = top + jnp.log(total)
    mixed = mixed_full.astype(bf16)
    mixed_mine = lax.dynamic_slice(mixed, (0, out_at), (mixed.shape[0], out_rows))
    out_mine = lax.dynamic_slice(out_head, (out_at, 0), (out_rows, width))
    hidden = dot32(mlp_in, up_here) + lax.dynamic_slice(up_bias, (rank * ff,), (ff,))
    activated_full, gelu_pull = jax.vjp(exact_gelu, hidden)
    activated = activated_full.astype(bf16)
    out_partial = dot32(mixed_mine, out_mine) + dot32(activated, down_here, contract_last)
    down_grad = dot32(seq_cotangent, activated, contract_first)
    out_grad = dot32(mixed_mine, seq_cotangent, contract_first)
    grad_hidden = gelu_pull(dot32(seq_cotangent, down_here))[0].astype(bf16)
    up_grad = dot32(mlp_in, grad_hidden, contract_first)
    grad_mixed = dot32(seq_cotangent, out_head, contract_last).astype(bf16)
    row_dot = jnp.sum(grad_mixed.astype(f32) * mixed_full, axis=-1, keepdims=True)
    probs = jnp.where(causal, jnp.exp(scores - log_total), 0.0)
    grad_values = dot32(probs.astype(bf16), grad_mixed, contract_first)
    grad_probs = dot32(grad_mixed, values, contract_last)
    grad_scores = (probs * (grad_probs - row_dot)).astype(bf16)
    grad_queries = dot32(grad_scores, keys) * score_scale
    grad_keys = dot32(grad_scores, queries, contract_first) * score_scale
    grad_projected = jnp.concatenate(
        [rotary(grad_queries, -positions), rotary(grad_keys, -positions), grad_values], axis=1
    ).astype(bf16)
    qkv_grad = dot32(attn_in, grad_projected, contract_first)
    grad_attn_in = dot32(grad_projected, qkv_here, contract_last) * (1.0 / repeat)
    grad_mlp_in = dot32(grad_hidden, up_here, contract_last)
    in_partial = grad_attn_in * attn_norm_gain + grad_mlp_in * mlp_norm_gain

    first_copy = jnp.where(rank % repeat == 0, 1.0, 0.0)
    qkv_bias_part = jnp.sum(grad_projected.astype(f32), axis=0) * first_copy
    qkv_bias_full = jnp.zeros((3, width), f32)
    qkv_bias_full = lax.dynamic_update_slice(
        qkv_bias_full, qkv_bias_part.reshape(3, HD), (0, head * HD)
    ).reshape(-1)
    up_bias_full = lax.dynamic_update_slice(
        jnp.zeros((hidden_width,), f32),
        jnp.sum(grad_hidden.astype(f32), axis=0),
        (rank * ff,),
    )
    small = jnp.concatenate(
        [
            qkv_bias_full,
            up_bias_full,
            jnp.sum(own_cotangent.astype(f32), axis=0),
            jnp.sum(grad_attn_in * normed, axis=0),
            jnp.sum(grad_attn_in, axis=0),
            jnp.sum(grad_mlp_in * normed, axis=0),
            jnp.sum(grad_mlp_in, axis=0),
        ]
    ).reshape(-1, 128)
    summed_out, summed_in, all_down, all_up, all_qkv, all_out, small = scatter_all(
        lay,
        out_partial.astype(bf16),
        in_partial.astype(bf16),
        down_grad.astype(bf16),
        up_grad.astype(bf16),
        qkv_grad.astype(bf16),
        out_grad.astype(bf16),
        small,
    )
    output = (own.astype(f32) + summed_out + (out_bias + down_bias)).astype(bf16)[None]
    own_normed, own_scale = normalize(own.astype(f32))
    input_grad = own_scale * (
        summed_in
        - jnp.mean(summed_in, axis=-1, keepdims=True)
        - own_normed * jnp.mean(summed_in * own_normed, axis=-1, keepdims=True)
    )
    tokens_grad = (own_cotangent.astype(f32) + input_grad)[None]

    small = small.reshape(-1)
    cuts = [3 * width, hidden_width, width, width, width, width, width]
    small_parts, at = [], 0
    for size in cuts:
        small_parts.append(small[at : at + size])
        at += size

    qkv_weight_grad = all_qkv.astype(f32)
    out_weight_grad = all_out.astype(f32)
    up_weight_grad = all_up.astype(f32)
    down_weight_grad = all_down.astype(f32)
    return (
        output,
        tokens_grad,
        qkv_weight_grad,
        small_parts[0],
        out_weight_grad,
        small_parts[2],
        up_weight_grad,
        small_parts[1],
        down_weight_grad,
        small_parts[2],
        small_parts[3],
        small_parts[4],
        small_parts[5],
        small_parts[6],
    )


def solution(mesh):
    lay = Layout(mesh)

    def local(*args):
        return local_block(lay, *args)

    sharded = P("shard", "ctx", None)
    by_rows = P("shard", None)
    owned = P(("ctx", "shard"), None)
    in_specs = (
        sharded, by_rows, P(), by_rows, P(), by_rows, P(), by_rows, P(),
        P(), P(), P(), P(), sharded,
    )
    out_specs = (
        sharded, sharded, owned, P(), owned, P(), owned, P(), owned,
        P(), P(), P(), P(), P(),
    )
    return jax.shard_map(
        local, mesh=mesh, in_specs=in_specs, out_specs=out_specs, check_vma=False
    )
```

time: 826 us -> 503 us (0.61)
  Pallas kernels: 0 us -> 374 us
  waiting for transfers between devices: 328 us -> 0 us
  starting transfers between devices: 177 us -> 0 us
  other arithmetic: 95.8 us -> 17.4 us
  local copies, waits for them, and re-layouts: 83.7 us -> 14.5 us
  matrix products: 112 us -> 86.7 us
  between operations: 19.3 us -> 1.67 us
    pallas_call x0 -> x2, Pallas kernels: none -> 374 us  [the longest x1 229 us: scatter_all(): pl.pallas_call(functools.partial(scatter_kernel, lay, (rows, width, ff, r...]
    ppermute x64 -> x0, waiting for transfers between devices: 207 us -> none  [permute(): lax.ppermute(value, AXES, [(self.flat(*a), self.flat(*b)) for a, b in pai...]
    ppermute x64 -> x0, starting transfers between devices: 177 us -> none  [permute(): lax.ppermute(value, AXES, [(self.flat(*a), self.flat(*b)) for a, b in pai...]
    psum x1 -> x0, waiting for transfers between devices: 120 us -> none  [local_block(): lax.psum(jnp.concatenate([qkv_bias_full, up_bias_full, jnp.sum(own_cotang...]
    dot_general x18, matrix products: 112 us -> 86.7 us  [dot32(): lax.dot_general(left, right, dims, preferred_element_type=jnp.float32)]
    select_n x13 -> x0, other arithmetic: 24.3 us -> none  [the longest x6 18.7 us: gather_sequence(): current = jnp.where(received(k), arrived, current)]
    convert_element_type x17 -> x5, other arithmetic: 28 us -> 5.67 us  [the longest x1 1.46 us: local_block(): down_weight_grad = all_down.astype(f32)]
    gather x6 -> x0, local copies, waits for them, and re-layouts: 20.6 us -> none  [gather_weight(): held[:, jnp.asarray(inverse)]]
  transfers between devices with their start and end apart: 65 -> 0, of which waited for: 24 -> 0; matrix products, arithmetic and copies ran while one was open for 28% -> 0% of each run, Pallas kernels for 0% -> 0%
where the time goes in v2:
time: 503 us; the launch traced here: 494 us
  Pallas kernels  374 us (74%)
  matrix products  86.7 us (17%)
  other arithmetic  17.4 us (3%)
  local copies, waits for them, and re-layouts  14.5 us (3%)
    pallas_call x1, Pallas kernels, scatter_all(): pl.pallas_call(functools.partial(scatter_kernel, lay, (rows, width, ff, r...  229 us
    pallas_call x1, Pallas kernels, gather_all(): pl.pallas_call(functools.partial(gather_kernel, lay, sizes), out_shape=[j...  145 us
    dot_general x18, matrix products, dot32(): lax.dot_general(left, right, dims, preferred_element_type=jnp.float32)  86.7 us

profile of v2, /device:TPU:0, one launch (start us, length us, event | category | flops | bytes accessed | tf_op | source)
XLA Modules:
  0.0 494.4 jit_solution(3667670208167376277)
XLA Ops:
  0.7 144.6 %gather_all.1 = (bf16[1024,2048]{1,0:T(8,128)(2,1)}, bf16[1024,2048]{1,0:T(8,128)(2,1)}, bf16[2048,768]{1,0:T(8,128)(2,1)}, bf16[2048,1024]{1,0:T(8,128)(2,1)}, ...) custom-call(bf16[128,2048]{1,0:T(8,128)(2,1)} %bitcast.50, ...), custom_call_target="tpu_custom_call" | custom-call | tf_op jit(solution)/shard_map/gather_all/pallas_call | solution.py:314
  145.3 3.2 dynamic-slice_dynamic-update-slice_fusion
  149.1 1.2 fusion.12
  150.7 5.0 %fusion.103 = f32[1024,1024]{0,1:T(8,128)S(1)} fusion(bf16[2048,1024]{1,0:T(8,128)(2,1)S(1)} %copy-done.19, bf16[1024,2048]{1,0:T(8,128)(2,1)S(1)} %copy-done.2, f32[2048]{0:T(1024)S(1)} %copy-done.23, f32[2048]{0:T(1024)S(1)} %copy-done.24, f32[1024]{0:T(1024)S(1)} %add_rsqrt_fusion, f32[1024]{0:T(1024)S(1)} %broadcast_multiply_fusion), kind=kOutput, calls=%fused_computation.170 | convolution fusion | flops 4307550208 | bytes 12607488 | tf_op jit(solution)/shard_map/dot_general | solution.py:23
  156.3 16.1 %convert_reduce_fusion.1 = (f32[1024]{0:T(1024)S(1)}, bf16[1024,1024]{0,1:T(8,128)(2,1)}, f32[1024,1024]{0,1:T(8,128)S(1)}) fusion(f32[1024,1024]{0,1:T(8,128)S(1)} %fusion.103, f32[1024]{0:T(1024)S(1)} %dynamic_slice.40, bf16[1024,2048]{1,0:T(8,128)(2,1)S(1)} %copy-done.17, bf16[2048,1024]{1,0:T(8,128)(2,1)S(1)} %copy-done.21), kind=kOutput, calls=%fused_computation.19 | convolution fusion | flops 4373609472 | bytes 18882560 | tf_op jit(solution)/shard_map/dot_general | solution.py:23
  173.1 1.3 copy-done.6
  174.4 6.9 %fusion.115 = f32[1024,2048]{1,0:T(8,128)} fusion(bf16[1024,1024]{0,1:T(8,128)(2,1)S(1)} %multiply_convert_fusion.1, bf16[2048,1024]{1,0:T(8,128)(2,1)S(1)} %copy-done.21), kind=kOutput, calls=%fused_computation.178 | convolution fusion | flops 4294967296 | bytes 14680064 | tf_op jit(solution)/shard_map/dot_general | solution.py:23
  181.4 3.5 convolution_convert_fusion.4
  185.7 1.2 constant_dynamic-slice_fusion.2
  186.9 1.0 maximum_dynamic-update-slice_fusion
  187.9 7.2 %fusion.113 = (bf16[1024,768]{0,1:T(8,128)(2,1)S(1)}, f32[1024,768]{0,1:T(8,128)S(1)}) fusion(f32[768]{0:T(1024)S(1)} %pad_maximum_fusion.6, bf16[2048,768]{1,0:T(8,128)(2,1)} %maximum_dynamic-update-slice_fusion, bf16[1024,2048]{1,0:T(8,128)(2,1)} %get-tuple-element.26, f32[2048]{0:T(1024)S(1)} %copy-done.25, f32[2048]{0:T(1024)S(1)} %copy-done.26, ...), kind=kOutput, calls=%fused_computation.176 | convolution fusion | flops 3235381248 | bytes 12086272 | tf_op jit(solution)/shard_map/dot_general | solution.py:23
  195.8 0.9 fusion.114
  197.2 0.9 multiply_reduce_fusion
  198.0 0.9 slice-done
  198.9 1.4 slice-done.1
  200.3 3.3 add_convert_fusion.1.refs_0_
  203.6 0.9 multiply_convert_fusion
  206.4 1.0 convolution_multiply_fusion.1
  209.4 1.1 copy-done.22
  210.5 5.7 %fusion.116 = f32[1024,2048]{1,0:T(8,128)} fusion(bf16[1024,768]{0,1:T(8,128)(2,1)S(1)} %fusion.33, bf16[2048,768]{1,0:T(8,128)(2,1)S(1)} %copy-done.22), kind=kOutput, calls=%fused_computation.179 | convolution fusion | flops 3221225472 | bytes 13107200 | tf_op jit(solution)/shard_map/dot_general | solution.py:23
  216.1 12.0 %fusion.107 = (f32[2048]{0:T(1024)S(1)}, f32[2048]{0:T(1024)S(1)}, bf16[1024,2048]{1,0:T(8,128)(2,1)}, f32[2048]{0:T(1024)S(1)}, f32[2048]{0:T(1024)S(1)}) fusion(f32[1024]{0:T(1024)S(1)} %add_rsqrt_fusion, f32[1024]{0:T(1024)S(1)} %broadcast_multiply_fusion, bf16[1024,2048]{1,0:T(8,128)(2,1)S(1)} %copy-done.3, f32[2048]{0:T(1024)S(1)} %copy-done.24, ...), kind=kOutput, calls=%fused_computation.171 | convolution fusion | flops 4322222080 | bytes 23126016 | tf_op jit(solution)/shard_map/dot_general | solution.py:23
  228.1 6.4 %convolution_convert_fusion.1.refs_2_ = bf16[2048,1024]{1,0:T(8,128)(2,1)} fusion(bf16[1024,2048]{1,0:T(8,128)(2,1)S(1)} %copy-done.18, bf16[1024,1024]{0,1:T(8,128)(2,1)S(1)} %copy-done.7), kind=kOutput, calls=%fused_computation.41 | convolution fusion | flops 4297064448 | bytes 10485760 | tf_op jit(solution)/shard_map/dot_general | solution.py:23
  234.5 7.2 %convolution_convert_fusion.refs_3_ = bf16[2048,1024]{1,0:T(8,128)(2,1)} fusion(bf16[1024,1024]{0,1:T(8,128)(2,1)S(1)} %copy-done.27, bf16[1024,2048]{1,0:T(8,128)(2,1)S(1)} %copy-done.3, f32[2048]{0:T(1024)S(1)} %copy-done.23, f32[2048]{0:T(1024)S(1)} %copy-done.24, f32[1024]{0:T(1024)S(1)} %add_rsqrt_fusion, f32[1024]{0:T(1024)S(1)} %broadcast_multiply_fusion), kind=kOutput, calls=%fused_computation.40 | convolution fusion | flops 4309647360 | bytes 10510336 | tf_op jit(solution)/shard_map/dot_general | solution.py:23
  241.8 6.0 %convolution_convert_fusion.2.refs_4_ = bf16[2048,768]{1,0:T(8,128)(2,1)} fusion(bf16[1024,768]{0,1:T(8,128)(2,1)S(1)} %fusion.33, bf16[1024,2048]{1,0:T(8,128)(2,1)S(1)} %copy-done.3, f32[2048]{0:T(1024)S(1)} %copy-done.25, f32[2048]{0:T(1024)S(1)} %copy-done.26, f32[1024]{0:T(1024)S(1)} %add_rsqrt_fusion, f32[1024]{0:T(1024)S(1)} %broadcast_multiply_fusion), kind=kOutput, calls=%fused_computation.42 | convolution fusion | flops 3235381248 | bytes 8937472 | tf_op jit(solution)/shard_map/dot_general | solution.py:23
  247.8 2.2 convolution_convert_fusion.3.refs_5_
  251.5 229.5 %scatter_all.1 = (f32[128,2048]{1,0:T(8,128)}, f32[128,2048]{1,0:T(8,128)}, bf16[64,8192]{1,0:T(8,128)(2,1)}, bf16[64,8192]{1,0:T(8,128)(2,1)}, bf16[64,6144]{1,...) custom-call(bf16[1024,2048]{1,0:T(8,128)(2,1)} %add_convert_fusion.1.refs_0_, ...), custom_call_target="tpu_custom_call" | custom-call | tf_op jit(solution)/shard_map/scatter_all/pallas_call | solution.py:771
  481.5 1.6 fusion.109
  483.2 3.3 fusion.44
  486.5 1.2 convert_element_type.152
  488.3 0.8 convert_element_type.153
  489.8 1.5 convert_element_type.154
  491.9 1.5 convert_element_type.155
  (105 shorter events, 12.4 us)
Async XLA Ops:
  0.6 180.7 %copy-start = (bf16[512,2048]{1,0:T(8,128)(2,1)S(1)}, bf16[512,2048]{1,0:T(8,128)(2,1)}, u32[]{:S(2)}) copy-start(bf16[512,2048]{1,0:T(8,128)(2,1)} %param.17) | copy-start | bytes 6291460
  145.3 3.2 copy-start.2
  148.5 2.2 copy-start.19
  148.5 2.2 copy-start.23
  148.5 2.2 copy-start.24
  150.7 5.7 %copy-start.17 = (bf16[1024,2048]{1,0:T(8,128)(2,1)S(1)}, bf16[1024,2048]{1,0:T(8,128)(2,1)}, u32[]{:S(2)}) copy-start(bf16[1024,2048]{1,0:T(8,128)(2,1)} %get-tuple-element.30) | copy-start | bytes 12582916
  150.7 5.7 %copy-start.21 = (bf16[2048,1024]{1,0:T(8,128)(2,1)S(1)}, bf16[2048,1024]{1,0:T(8,128)(2,1)}, u32[]{:S(2)}) copy-start(bf16[2048,1024]{1,0:T(8,128)(2,1)} %get-tuple-element.75) | copy-start | bytes 12582916
  173.1 1.3 copy-start.6
  181.4 6.5 %copy-start.25 = (f32[2048]{0:T(1024)S(1)}, f32[2048]{0:T(1024)}, u32[]{:S(2)}) copy-start(f32[2048]{0:T(1024)} %param.24) | copy-start | bytes 24580
  181.4 6.5 %copy-start.26 = (f32[2048]{0:T(1024)S(1)}, f32[2048]{0:T(1024)}, u32[]{:S(2)}) copy-start(f32[2048]{0:T(1024)} %param.23) | copy-start | bytes 24580
  196.7 2.2 slice-start
  197.2 3.2 slice-start.1
  208.6 1.9 copy-start.22
  210.4 5.7 %copy-start.3 = (bf16[1024,2048]{1,0:T(8,128)(2,1)S(1)}, bf16[1024,2048]{1,0:T(8,128)(2,1)}, u32[]{:S(2)}) copy-start(bf16[1024,2048]{1,0:T(8,128)(2,1)} %get-tuple-element.26) | copy-start | bytes 12582916
  210.5 5.7 %copy-start.20 = (bf16[2048,1024]{1,0:T(8,128)(2,1)S(1)}, bf16[2048,1024]{1,0:T(8,128)(2,1)}, u32[]{:S(2)}) copy-start(bf16[2048,1024]{1,0:T(8,128)(2,1)} %get-tuple-element.76) | copy-start | bytes 12582916
  216.1 12.0 %copy-start.7 = (bf16[1024,1024]{0,1:T(8,128)(2,1)S(1)}, bf16[1024,1024]{0,1:T(8,128)(2,1)}, u32[]{:S(2)}) copy-start(bf16[1024,1024]{0,1:T(8,128)(2,1)} %copy-done.6) | copy-start | bytes 6291460
  216.1 12.0 %copy-start.18 = (bf16[1024,2048]{1,0:T(8,128)(2,1)S(1)}, bf16[1024,2048]{1,0:T(8,128)(2,1)}, u32[]{:S(2)}) copy-start(bf16[1024,2048]{1,0:T(8,128)(2,1)} %get-tuple-element.30) | copy-start | bytes 12582916
  228.1 6.4 %copy-start.27 = (bf16[1024,1024]{0,1:T(8,128)(2,1)S(1)}, bf16[1024,1024]{0,1:T(8,128)(2,1)}, u32[]{:S(2)}) copy-start(bf16[1024,1024]{0,1:T(8,128)(2,1)} %get-tuple-element.45) | copy-start | bytes 6291460
  247.8 2.9 copy-start.5
  250.9 0.6 copy-start.12
  251.5 229.5 %copy-start.4 = (bf16[1,128,2048]{2,1,0:T(8,128)(2,1)S(1)}, bf16[1,128,2048]{2,1,0:T(8,128)(2,1)}, u32[]{:S(2)}) copy-start(bf16[1,128,2048]{2,1,0:T(8,128)(2,1)} %param.14) | copy-start | bytes 1572868
  251.5 231.6 %copy-start.15 = (f32[2048]{0:T(1024)S(1)}, f32[2048]{0:T(1024)}, u32[]{:S(2)}) copy-start(f32[2048]{0:T(1024)} %param.18) | copy-start | bytes 24580
  251.5 231.6 %copy-start.16 = (f32[2048]{0:T(1024)S(1)}, f32[2048]{0:T(1024)}, u32[]{:S(2)}) copy-start(f32[2048]{0:T(1024)} %param.22) | copy-start | bytes 24580
  481.0 5.4 %copy-start.10 = (bf16[64,6144]{1,0:T(8,128)(2,1)S(1)}, bf16[64,6144]{1,0:T(8,128)(2,1)}, u32[]{:S(2)}) copy-start(bf16[64,6144]{1,0:T(8,128)(2,1)} %get-tuple-element.33) | copy-start | bytes 2359300
  481.5 6.2 %copy-start.13 = (f32[192,128]{1,0:T(8,128)S(1)}, f32[192,128]{1,0:T(8,128)}, u32[]{:S(2)}) copy-start(f32[192,128]{1,0:T(8,128)} %get-tuple-element.34) | copy-start | bytes 294916
  481.5 6.8 %copy-start.11 = (bf16[64,2048]{1,0:T(8,128)(2,1)S(1)}, bf16[64,2048]{1,0:T(8,128)(2,1)}, u32[]{:S(2)}) copy-start(bf16[64,2048]{1,0:T(8,128)(2,1)} %get-tuple-element.35) | copy-start | bytes 786436
  483.1 6.7 %copy-start.9 = (bf16[64,8192]{1,0:T(8,128)(2,1)S(1)}, bf16[64,8192]{1,0:T(8,128)(2,1)}, u32[]{:S(2)}) copy-start(bf16[64,8192]{1,0:T(8,128)(2,1)} %get-tuple-element.36) | copy-start | bytes 3145732
  486.5 5.4 %copy-start.8 = (bf16[64,8192]{1,0:T(8,128)(2,1)S(1)}, bf16[64,8192]{1,0:T(8,128)(2,1)}, u32[]{:S(2)}) copy-start(bf16[64,8192]{1,0:T(8,128)(2,1)} %get-tuple-element.37) | copy-start | bytes 3145732
  486.5 7.5 %copy-start.1 = (bf16[512,2048]{1,0:T(8,128)(2,1)S(1)}, bf16[512,2048]{1,0:T(8,128)(2,1)}, u32[]{:S(2)}) copy-start(bf16[512,2048]{1,0:T(8,128)(2,1)} %param.17) | copy-start | bytes 6291460
  489.8 4.1 copy-start.14

commit v3 on v2

--- a/solution.py
+++ b/solution.py
@@ -332,6 +332,469 @@
         name="gather_all",
     )(tok, cot, qkv, up, down)[:5]
 
+def turn(values, cosine, sine):
+    left = values[:, :128]
+    lane = lax.broadcasted_iota(jnp.int32, left.shape, 1)
+    swapped = jnp.where(lane < ROT // 2, pltpu.roll(left, 128 - ROT // 2, 1), pltpu.roll(left, ROT // 2, 1))
+    return jnp.concatenate([left * cosine + swapped * sine, values[:, 128:]], axis=1)
+
+
+def block_schedule(order_w, nlo, by_bit, n_groups, blocks, n_short):
+    timed = [(t, ("N", a)) for a, t in ((0, -9), (1, 10))]
+    timed += [(-5, ("WO",))]
+    for a, (first, step) in enumerate(((12, 12), (40, 12))):
+        timed.append((first - 1, ("D", a, 0)))
+        for k in range(1, nlo):
+            timed.append((first + step * (k - 1), ("Z", a, k)))
+            timed.append((first + step * (k - 1) + 8, ("D", a, k)))
+    sizes = [1, 1, 1, 4, 4]
+    sent = 0.0
+    for g, i in order_w:
+        timed.append((20 + 2.5 * sent, ("W", g, i)))
+        timed.append((20 + 2.5 * sent + 20, ("E", g, i, 0)))
+        for r in by_bit:
+            timed.append((20 + 2.5 * sent + 20 + (20 if low_bit(r) > 1 else 20 + 8), ("E", g, i, r)))
+        sent += sizes[g]
+    after = {}
+
+    def put(name, time, item):
+        timed.append((time, item))
+        after[name] = max(after.get(name, 0), time) + 0.01
+
+    ready = [max(t for t, item in timed if item[0] == "E" and item[1] == g) for g in range(n_groups)]
+    seen = [max(t for t, item in timed if item[0] == "D" and item[1] == a) for a in range(2)]
+    put("H", max(50, seen[0] + 0.1), ("H", 0))
+    put("H", max(70, after["H"]), ("H", 1))
+    put("CO", max(100, seen[1] + 0.1, after["H"]), ("CO",))
+    for k in range(blocks):
+        put("K", max(after["H"], max(ready[:3])) + 0.1 + 0.01 * k, ("K", k))
+    for k in range(blocks):
+        put("AF", after["K"] + 0.01 * k, ("AF", k))
+    for k in range(blocks):
+        put("U", max(after["AF"], ready[3]) + 0.1 + 0.01 * k, ("U", k))
+    for k in range(blocks):
+        put("GM", max(after["CO"], after["U"]) + 0.1 + 0.01 * k, ("GM", k))
+    for k in range(blocks):
+        put("AB", after["GM"] + 0.1 + 0.01 * k, ("AB", k))
+    put("BP", after["AB"] + 0.1, ("BP",))
+    for k in range(blocks):
+        put("O", max(after["BP"], max(ready)) + 0.1 + 0.01 * k, ("O", k))
+    for k in range(blocks):
+        put("GH", max(after["O"], max(ready)) + 0.1 + 0.01 * k, ("GH", k))
+    for k in range(n_short):
+        put("S", max(after["GH"], after["BP"]) + 0.1, ("S", k))
+    timed.sort(key=lambda entry: entry[0])
+    return [entry[1] for entry in timed]
+
+
+def block_kernel(lay, sizes, *refs):
+    rows, width, weight_rows, ff = sizes
+    nz, nlo, nhi = lay.nz, lay.nlo, lay.nhi
+    f32, bf16 = jnp.float32, jnp.bfloat16
+    refs = list(refs)
+
+    def take(count):
+        taken = refs[:count]
+        del refs[:count]
+        return taken
+
+    tok, cot, qkv, up, down, out_w = take(6)
+    qkv_b, up_b, gain_a, shift_a, gain_m, shift_m, cos_t, sin_t = take(8)
+    seq_c_out, attn_out, mlp_out, act_out, gh_out, gp_out, mixed_out, o_out, s_out, stage_t, stage_c = take(11)
+    vec_out, qkv_b_out, up_b_out = take(3)
+    seq_t, seq_c, w_qkv, w_up, w_down, w_out = take(6)
+    attn_in, mlp_in, q_ref, k_ref, v_ref, mixed, mixed_full, lse, slope, act, gh, gm = take(12)
+    dq, dk, dv, gp, o_buf, s_buf, means, scales = take(8)
+    near_r, near_s, home_c, z_r, z_s, y_r, y_s, wz_r, wz_s, wf_r, wf_s, own_c, out_c, o_c, s_c = take(15)
+
+    z, hi, lo = place(lay)
+    half, quarter = nlo * rows, weight_rows // nlo
+    total = 2 * half
+    rank = z * nhi + hi
+    odd = lo % 2
+    s = (1 - odd) * (lo // 2) + odd * (nz - 1 - lo // 2)
+    score_scale = HD ** (-0.5)
+
+    def dev(z, hi, lo):
+        return (hi * nlo + lo, z)
+
+    enter(
+        [dev((z + i) % nz, hi, lo) for i in range(1, nz)]
+        + [dev(z, hi, flip(lo, r, nlo)) for r in range(1, nlo)]
+        + [dev(z, 1 - hi, lo)]
+    )
+
+    groups = []
+    for part in range(3):
+        groups.append((qkv, w_qkv, lambda rank, part=part: part * width + rank * HD, part * HD, HD))
+    groups.append((up, w_up, lambda rank: rank * ff, 0, ff))
+    groups.append((down, w_down, lambda rank: rank * ff, 0, ff))
+    bits = list(reversed(lay.bits))
+
+    def weight_z(g, i):
+        src, dst, column, at, wide = groups[g]
+        to = (z + i) % nz
+        first = pl.multiple_of(column(to * nhi + hi), 128)
+        return remote(
+            src.at[pl.ds(pl.multiple_of(lo * quarter, quarter), quarter), pl.ds(first, wide)],
+            dst.at[pl.ds(pl.multiple_of(z * weight_rows + lo * quarter, quarter), quarter), pl.ds(at, wide)],
+            wz_s.at[g, i - 1], wz_r.at[g, i - 1], dev(to, hi, lo),
+        )
+
+    def weight_forward(g, i, r, b):
+        _, dst, _, at, wide = groups[g]
+        row = ((z + nz - i) % nz) * weight_rows + flip(lo, r, nlo) * quarter
+        piece = dst.at[pl.ds(pl.multiple_of(row, quarter), quarter), pl.ds(at, wide)]
+        k = bits.index(b)
+        return remote(piece, piece, wf_s.at[g, i - 1, r, k], wf_r.at[g, i - 1, r ^ b], dev(z, hi, flip(lo, b, nlo)))
+
+    inputs, staged, sequences = (tok, cot), (stage_t, stage_c), (seq_t, seq_c)
+    distance = jnp.abs(z - s)
+
+    def home_of(seq):
+        late = seq // (nz // 2)
+        return (1 - late) * (2 * seq) + late * (2 * (nz - 1 - seq) + 1)
+
+    def seq_rows(a, which, r):
+        row = which * half + flip(lo, r, nlo) * rows
+        return sequences[a].at[pl.ds(pl.multiple_of(row, rows), rows)]
+
+    def along(a, src, seq, way):
+        return remote(src, staged[a].at[seq], z_s.at[a, seq, way], z_r.at[a, seq], dev((z + 1 - 2 * way + nz) % nz, hi, lo))
+
+    def near(a, src, seq):
+        return remote(src, seq_rows(a, hi, 0), near_s.at[a, seq], near_r.at[a, lo], dev(z, hi, home_of(seq)))
+
+    def near_arrival(a, r):
+        piece = seq_rows(a, hi, r)
+        return remote(piece, piece, near_s.at[a, 0], near_r.at[a, flip(lo, r, nlo)], dev(z, hi, flip(lo, r, nlo)))
+
+    def stay(a, src):
+        return pltpu.make_async_copy(src, seq_rows(a, hi, 0), home_c.at[a])
+
+    def across(a, src, r):
+        return remote(src, seq_rows(a, hi, r), y_s.at[a, r], y_r.at[a, r], dev(z, 1 - hi, lo))
+
+    def across_arrival(a, r):
+        piece = seq_rows(a, 1 - hi, r)
+        return remote(piece, piece, y_s.at[a, r], y_r.at[a, r], dev(z, 1 - hi, lo))
+
+    def sources(a):
+        yield (z >= 0, inputs[a], z, z < nz - 1, z > 0)
+        for k in range(1, nz):
+            yield (z >= k, staged[a].at[(z + nz - k) % nz], (z + nz - k) % nz, z < nz - 1, z < 0)
+            yield (z < nz - k, staged[a].at[(z + k) % nz], (z + k) % nz, z < 0, z > 0)
+
+    def dispatch(a, which):
+        valid, src, seq, up, down = list(sources(a))[which]
+
+        @pl.when(valid & up)
+        def _():
+            along(a, src, seq, 0).start()
+
+        @pl.when(valid & down)
+        def _():
+            along(a, src, seq, 1).start()
+
+        @pl.when(valid & (lo == home_of(seq)))
+        def _():
+            across(a, src, 0).start()
+            stay(a, src).start()
+
+        @pl.when(valid & (lo != home_of(seq)))
+        def _():
+            near(a, src, seq).start()
+
+    def settle(a, which):
+        valid, src, seq, up, down = list(sources(a))[which]
+
+        @pl.when(valid & up)
+        def _():
+            along(a, src, seq, 0).wait_send()
+
+        @pl.when(valid & down)
+        def _():
+            along(a, src, seq, 1).wait_send()
+
+        @pl.when(valid & (lo == home_of(seq)))
+        def _():
+            across(a, src, 0).wait_send()
+
+        @pl.when(valid & (lo != home_of(seq)))
+        def _():
+            near(a, src, seq).wait_send()
+
+    def chain_event(a, k):
+        for which, valid, seq in ((2 * k - 1, z >= k, (z + nz - k) % nz), (2 * k, z < nz - k, (z + k) % nz)):
+            @pl.when(valid)
+            def _(seq=seq):
+                along(a, staged[a].at[seq], seq, 0).wait_recv()
+
+            dispatch(a, which)
+
+    def near_event(a, d):
+        @pl.when(distance == d)
+        def _():
+            for r in range(1, nlo):
+                near_arrival(a, r).wait_recv()
+                across(a, seq_rows(a, hi, r), r).start()
+
+    def forward_from(g, i, r):
+        for b in bits:
+            if r == 0 or b < low_bit(r):
+                weight_forward(g, i, r, b).start()
+
+    def weight_event(g, i, r):
+        if r == 0:
+            weight_z(g, i).wait_recv()
+        else:
+            weight_forward(g, i, r ^ low_bit(r), low_bit(r)).wait_recv()
+        forward_from(g, i, r)
+
+    def own_weight(g):
+        if g == len(groups):
+            first = pl.multiple_of(rank * HD - z * weight_rows, HD)
+            return pltpu.make_async_copy(out_w.at[pl.ds(first, HD)], w_out, own_c.at[g])
+        src, dst, column, at, wide = groups[g]
+        first = pl.multiple_of(column(rank), 128)
+        return pltpu.make_async_copy(
+            src.at[:, pl.ds(first, wide)],
+            dst.at[pl.ds(pl.multiple_of(z * weight_rows, weight_rows), weight_rows), pl.ds(at, wide)],
+            own_c.at[g],
+        )
+
+    def own_start():
+        for g in range(len(groups) + 1):
+            own_weight(g).start()
+
+    tall = 256
+    blocks = total // tall
+    kept = ((seq_c, seq_c_out), (attn_in, attn_out), (mlp_in, mlp_out), (act, act_out), (gh, gh_out), (gp, gp_out), (mixed, mixed_out))
+
+    def save(k):
+        return pltpu.make_async_copy(*kept[k], out_c.at[k])
+
+    def at_block(i):
+        return pl.ds(i * tall, tall)
+
+    def norm(which):
+        if which == 0:
+            stay(0, tok).wait()
+        else:
+            for r in range(nlo):
+                across_arrival(0, r).wait_recv()
+        start = (hi if which == 0 else 1 - hi) * half
+        step = 64
+
+        def body(i, carry):
+            at = pl.ds(pl.multiple_of(start + i * step, step), step)
+            values = seq_t[at, :].astype(f32)
+            mean = jnp.mean(values, axis=-1, keepdims=True)
+            center = values - mean
+            scale = lax.rsqrt(jnp.mean(center * center, axis=-1, keepdims=True) + norm_epsilon)
+            normed = center * scale
+            attn_in[at, :] = (normed * gain_a[...] + shift_a[...]).astype(bf16)
+            mlp_in[at, :] = (normed * gain_m[...] + shift_m[...]).astype(bf16)
+            means[at, :] = jnp.broadcast_to(mean, (step, 128))
+            scales[at, :] = jnp.broadcast_to(scale, (step, 128))
+            return carry
+
+        lax.fori_loop(0, half // step, body, 0)
+        if which == 1:
+            save(1).start()
+            save(2).start()
+
+    def project(i):
+        if i == 0:
+            for g in range(3):
+                own_weight(g).wait()
+        at = at_block(i)
+        raw = jnp.dot(attn_in[at, :], w_qkv[...], preferred_element_type=f32) + qkv_b[...]
+        q_ref[at, :] = turn(raw[:, :HD], cos_t[at, :], sin_t[at, :]).astype(bf16)
+        k_ref[at, :] = turn(raw[:, HD : 2 * HD], cos_t[at, :], sin_t[at, :]).astype(bf16)
+        v_ref[at, :] = raw[:, 2 * HD :].astype(bf16)
+
+    def scores_of(i):
+        reach = (i + 1) * tall
+        scores = dot32(q_ref[at_block(i), :], k_ref[:reach, :], contract_last) * score_scale
+        row = lax.broadcasted_iota(jnp.int32, scores.shape, 0) + i * tall
+        column = lax.broadcasted_iota(jnp.int32, scores.shape, 1)
+        return jnp.where(row >= column, scores, masked_score), reach
+
+    def attend(i):
+        scores, reach = scores_of(i)
+        top = jnp.max(scores, axis=-1, keepdims=True)
+        weights = jnp.exp(scores - top)
+        summed = jnp.sum(weights, axis=-1, keepdims=True)
+        full = dot32(weights.astype(bf16), v_ref[:reach, :]) / summed
+        at = at_block(i)
+        mixed_full[at, :] = full
+        mixed[at, :] = full.astype(bf16)
+        lse[at, :] = jnp.broadcast_to(top + jnp.log(summed), (tall, 128))
+        if i == blocks - 1:
+            save(6).start()
+
+    def hidden(i):
+        if i == 0:
+            own_weight(3).wait()
+        at = at_block(i)
+        value = jnp.dot(mlp_in[at, :], w_up[...], preferred_element_type=f32) + up_b[...]
+        cdf = (1.0 + lax.erf(value * (0.5 ** 0.5))) * 0.5
+        act[at, :] = (value * cdf).astype(bf16)
+        slope[at, :] = cdf + value * jnp.exp(value * value * (-0.5)) * 0.3989422804014327
+        if i == blocks - 1:
+            save(3).start()
+
+    def cotangent_here():
+        stay(1, cot).wait()
+        for r in range(nlo):
+            across_arrival(1, r).wait_recv()
+        save(0).start()
+        own_weight(5).wait()
+
+    def back_mixed(i):
+        at = at_block(i)
+        gm[at, :] = dot32(seq_c[at, :], w_out[...], contract_last).astype(bf16)
+
+    def back_hidden(i):
+        if i == 0:
+            up_b_out[...] = jnp.zeros_like(up_b_out)
+        at = at_block(i)
+        part = (jnp.dot(seq_c[at, :], w_down[...], preferred_element_type=f32) * slope[at, :]).astype(bf16)
+        gh[at, :] = part
+        up_b_out[...] += jnp.sum(part.astype(f32), axis=0, keepdims=True)
+        if i == blocks - 1:
+            save(4).start()
+
+    def out_store(i):
+        return pltpu.make_async_copy(o_buf.at[at_block(i)], o_out.at[at_block(i)], o_c.at[i])
+
+    def out_block(i):
+        if i == 0:
+            own_weight(4).wait()
+        at = at_block(i)
+        part = jnp.dot(mixed[at, :], w_out[...], preferred_element_type=f32)
+        part = part + dot32(act[at, :], w_down[...], contract_last)
+        o_buf[at, :] = part.astype(bf16)
+        out_store(i).start()
+
+    def back_attend(i):
+        if i == 0:
+            dk[...] = jnp.zeros_like(dk)
+            dv[...] = jnp.zeros_like(dv)
+        at = at_block(i)
+        scores, reach = scores_of(i)
+        probs = jnp.exp(scores - lse[at, :1])
+        grad = gm[at, :]
+        row_dot = jnp.sum(grad.astype(f32) * mixed_full[at, :], axis=-1, keepdims=True)
+        dv[:reach, :] += dot32(probs.astype(bf16), grad, contract_first)
+        grad_scores = (probs * (dot32(grad, v_ref[:reach, :], contract_last) - row_dot)).astype(bf16)
+        dq[at, :] = dot32(grad_scores, k_ref[:reach, :]) * score_scale
+        dk[:reach, :] += dot32(grad_scores, q_ref[at, :], contract_first) * score_scale
+
+    def back_project():
+        qkv_b_out[...] = jnp.zeros_like(qkv_b_out)
+        for i in range(blocks):
+            at = at_block(i)
+            part = jnp.concatenate(
+                [turn(dq[at, :], cos_t[at, :], -sin_t[at, :]), turn(dk[at, :], cos_t[at, :], -sin_t[at, :]), dv[at, :]],
+                axis=1,
+            ).astype(bf16)
+            gp[at, :] = part
+            qkv_b_out[...] += jnp.sum(part.astype(f32), axis=0, keepdims=True)
+        save(5).start()
+
+    short = 128
+
+    def in_store(i):
+        return pltpu.make_async_copy(s_buf.at[pl.ds(i * short, short)], s_out.at[pl.ds(i * short, short)], s_c.at[i])
+
+    def in_block(i):
+        if i == 0:
+            vec_out[...] = jnp.zeros_like(vec_out)
+        at = pl.ds(i * short, short)
+        grad_a = dot32(gp[at, :], w_qkv[...], contract_last)
+        grad_m = dot32(gh[at, :], w_up[...], contract_last)
+        s_buf[at, :] = (grad_a * gain_a[...] + grad_m * gain_m[...]).astype(bf16)
+        normed = (seq_t[at, :].astype(f32) - means[at, :1]) * scales[at, :1]
+        for k, term in enumerate((grad_a * normed, grad_a, grad_m * normed, grad_m)):
+            vec_out[k : k + 1, :] += jnp.sum(term, axis=0, keepdims=True)
+        in_store(i).start()
+
+    act_of = dict(
+        N=lambda a: dispatch(a, 0), Z=chain_event, D=near_event, W=lambda g, i: weight_z(g, i).start(), E=weight_event,
+        WO=own_start, H=norm, K=project, AF=attend, U=hidden, CO=cotangent_here, GM=back_mixed, GH=back_hidden,
+        O=out_block, AB=back_attend, BP=back_project, S=in_block,
+    )
+    order_w = [(g, i) for g in range(len(groups)) for i in range(1, nz)]
+    by_bit = sorted(range(1, nlo), key=lambda r: -low_bit(r))
+    for item in block_schedule(order_w, nlo, by_bit, len(groups), blocks, total // short):
+        act_of[item[0]](*item[1:])
+
+    for k in range(len(kept)):
+        save(k).wait()
+    for i in range(blocks):
+        out_store(i).wait()
+    for i in range(total // short):
+        in_store(i).wait()
+    for g, i in order_w:
+        weight_z(g, i).wait_send()
+        for r in range(nlo):
+            for b in bits:
+                if r == 0 or b < low_bit(r):
+                    weight_forward(g, i, r, b).wait_send()
+    for a in range(2):
+        for which in range(2 * nz - 1):
+            settle(a, which)
+        for r in range(1, nlo):
+            across(a, seq_rows(a, hi, r), r).wait_send()
+
+
+def block_all(lay, tok, cot, qkv, up, down, out_w, qkv_b, up_b, gains, cos_t, sin_t):
+    rows, width = tok.shape
+    nz, nlo = lay.nz, lay.nlo
+    ff = up_b.shape[1]
+    bits = len(lay.bits)
+    anywhere = pl.BlockSpec(memory_space=pl.ANY)
+    inside = pl.BlockSpec(memory_space=pltpu.VMEM)
+    dma = pltpu.SemaphoreType.DMA
+    bf16, f32 = jnp.bfloat16, jnp.float32
+    total = 2 * nlo * rows
+
+    def shape(*dims, kind=bf16):
+        return jax.ShapeDtypeStruct(dims, kind)
+
+    def vmem(*dims, kind=bf16):
+        return pltpu.VMEM(dims, kind)
+
+    return pl.pallas_call(
+        functools.partial(block_kernel, lay, (rows, width, qkv.shape[0], ff)),
+        out_shape=[
+            shape(total, width), shape(total, width), shape(total, width), shape(total, ff), shape(total, ff),
+            shape(total, 3 * HD), shape(total, HD), shape(total, width), shape(total, width),
+            shape(nz, rows, width), shape(nz, rows, width),
+            shape(4, width, kind=f32), shape(1, 3 * HD, kind=f32), shape(1, ff, kind=f32),
+        ],
+        in_specs=[anywhere] * 6 + [inside] * 8,
+        out_specs=[anywhere] * 11 + [inside] * 3,
+        scratch_shapes=[
+            vmem(total, width), vmem(total, width), vmem(width, 3 * HD), vmem(width, ff), vmem(width, ff), vmem(HD, width),
+            vmem(total, width), vmem(total, width), vmem(total, HD), vmem(total, HD), vmem(total, HD), vmem(total, HD),
+            vmem(total, HD, kind=f32), vmem(total, 128, kind=f32), vmem(total, ff, kind=f32), vmem(total, ff),
+            vmem(total, ff), vmem(total, HD),
+            vmem(total, HD, kind=f32), vmem(total, HD, kind=f32), vmem(total, HD, kind=f32), vmem(total, 3 * HD),
+            vmem(total, width), vmem(total, width), vmem(total, 128, kind=f32), vmem(total, 128, kind=f32),
+            dma((2, nlo)), dma((2, nz)), dma((2,)), dma((2, nz)), dma((2, nz, 2)), dma((2, nlo)), dma((2, nlo)),
+            dma((5, nz - 1)), dma((5, nz - 1)), dma((5, nz - 1, nlo)), dma((5, nz - 1, nlo, bits)), dma((6,)),
+            dma((7,)), dma((total // 256,)), dma((total // 128,)),
+        ],
+        compiler_params=pltpu.CompilerParams(
+            collective_id=3, has_side_effects=True, vmem_limit_bytes=62 * 1024 * 1024
+        ),
+        name="block_all",
+    )(tok, cot, qkv, up, down, out_w, qkv_b, up_b, *gains, cos_t, sin_t)
+
+
 def add_rows(into, left, right, step):
     rows = into.shape[0]
     step = min(step, rows)
@@ -342,6 +805,14 @@
         return carry
 
     lax.fori_loop(0, rows // step, body, 0)
+
+
+def differ(one, other, count):
+    result, bit = 0, 1
+    while bit < count:
+        result = result + bit * ((one // bit + other // bit) % 2)
+        bit *= 2
+    return result
 
 
 def scatter_chunks(width, ff, repeat):
@@ -356,29 +827,24 @@
 
 
 def scatter_schedule(nz, nlo, n_chunks, stages):
-    schedule = [("Y", 0), ("M",), ("P",)] + [("C", g) for g in range(n_chunks)] + [("Y", 1)]
-    schedule += [("X", g, 0) for g in range(3)]
-    schedule += [("A", 0, q) for q in range(nlo)]
-    schedule += [("X", g, 0) for g in range(3, n_chunks)]
-    schedule += [("X", g, 1) for g in range(2)]
-    chain = []
-    for a in range(2):
-        part = []
-        for m in range(nz):
-            if m < nz - 1:
-                part.append(("B", a, nz - 1 - m, 0))
-            if m < nz - 1:
-                part.append(("B", a, m, 1))
-        chain.append(part + [("F", a)])
-    schedule += chain[0]
-    schedule += [("A", 1, q) for q in range(nlo)]
-    schedule += [("X", g, 1) for g in range(2, n_chunks)]
-    schedule += chain[1]
-    for t in range(2, stages):
-        schedule += [("X", g, t) for g in range(n_chunks)]
-    schedule += [("Q", t) for t in range(stages)] + [("N", t) for t in range(2 * stages + 1)]
-    schedule += [("G", g) for g in range(n_chunks)]
-    return schedule
+    timed = [(-4, ("M",)), (-3, ("L",)), (-2, ("Y", 0)), (30, ("Y", 1))]
+    for g in range(n_chunks):
+        timed.append((0 + 4 * g, ("C", g)))
+        for t in range(stages):
+            timed.append((10 + 14 * g + 20 * t, ("X", g, t)))
+    for a, (first, step, chain, hop) in enumerate(((14, 11.4, 60, 11), (60, 11.4, 106, 11))):
+        for q in range(nlo):
+            timed.append((first + step * q, ("A", a, q)))
+        for m in range(nz - 1):
+            timed.append((chain + hop * m, ("B", a, nz - 1 - m, 0)))
+            timed.append((chain + hop * m, ("B", a, m, 1)))
+        timed.append((chain + hop * (nz - 1), ("F", a)))
+    for t in range(stages):
+        timed.append((100 + 10 * t, ("Q", t)))
+    for t in range(2 * stages + 1):
+        timed.append((1 + 4 * t, ("N", t)))
+    timed.sort(key=lambda entry: entry[0])
+    return [entry[1] for entry in timed] + [("G", g) for g in range(n_chunks)]
 
 
 def scatter_kernel(lay, sizes, *refs):
@@ -394,16 +860,17 @@
         del refs[:count]
         return taken
 
-    partial_o, partial_s, wg_down, wg_up, wg_qkv, wg_out, small = take(7)
+    partial_o, partial_s, x_down, x_up, x_qkv, g_down, g_up, g_qkv, g_out, small = take(10)
     sum_o, sum_s, all_down, all_up, all_qkv, all_out, small_sum = take(7)
-    own, across_buf, near_buf, up_buf, down_buf = take(5)
+    own, across_buf, near_buf, chain_buf = take(4)
     acc = take(n)
     got = [take(stages) for _ in range(n)]
     out_acc, = take(1)
     out_got = take(stages)
     small_buf, small_got = take(2)
-    (own_c, y_r, y_s, near_r, near_s, z_r, z_s, acc_c, st_r, st_s, g_r, g_s, keep_c,
-     out_c, out_r, out_s, move_r, move_s, sm_r, sm_s) = take(20)
+    left, right_down, right_up, right_qkv, right_out, staged, out_part = take(7)
+    (own_c, y_r, y_s, near_r, near_s, z_r, z_s, st_r, st_s, g_r, g_s, keep_c,
+     out_r, out_s, move_r, move_s, sm_r, sm_s, left_c, right_c) = take(20)
 
     z, hi, lo = place(lay)
     rank = z * nhi + hi
@@ -435,11 +902,9 @@
 
     partial, summed = (partial_o, partial_s), (sum_o, sum_s)
 
-    def load_own(a):
-        row = pl.multiple_of(hi * half, half)
-        return pltpu.make_async_copy(
-            partial[a].at[pl.ds(row, half)], own.at[a], own_c.at[a]
-        )
+    def load_own(a, q):
+        row = pl.multiple_of(hi * half + q * rows, rows)
+        return pltpu.make_async_copy(partial[a].at[pl.ds(row, rows)], own.at[a, q % 2], own_c.at[a, q % 2])
 
     def across(a, q):
         row = pl.multiple_of((1 - hi) * half + q * rows, rows)
@@ -449,7 +914,7 @@
 
     def near(a, q):
         return remote(
-            own.at[a, pl.ds(q * rows, rows)], near_buf.at[a, lo], near_s.at[a, q], near_r.at[a, lo], dev(z, hi, q)
+            across_buf.at[a, q], near_buf.at[a, lo], near_s.at[a, q], near_r.at[a, lo], dev(z, hi, q)
         )
 
     def near_arrival(a, q):
@@ -457,37 +922,39 @@
         return remote(piece, piece, near_s.at[a, q], near_r.at[a, q], dev(z, hi, q))
 
     def along(a, seq, way):
-        buf = (up_buf, down_buf)[way]
+        slot = seq if way == 0 else jnp.where(z == seq + 1, nz, seq)
         return remote(
-            near_buf.at[a, lay.lo_of_seq[seq]], buf.at[a, seq], z_s.at[a, seq], z_r.at[a, seq, way],
+            near_buf.at[a, lay.lo_of_seq[seq]], chain_buf.at[a, slot], z_s.at[a, seq], z_r.at[a, seq, way],
             dev((z + 1 - 2 * way + nz) % nz, hi, lo),
         )
 
     def start_across(a):
-        load_own(a).start()
+        for q in range(2):
+            load_own(a, q).start()
         for q in range(nlo):
             across(a, q).start()
 
     def across_event(a, q):
-        if q == 0:
-            load_own(a).wait()
+        load_own(a, q).wait()
         across(a, q).wait_recv()
-        mine = own.at[a, pl.ds(q * rows, rows)]
+        mine, arrived = own.at[a, q % 2], across_buf.at[a, q]
 
         @pl.when(lo == q)
         def _():
-            add_rows(near_buf.at[a, q], mine, across_buf.at[a, q], 16)
+            add_rows(near_buf.at[a, q], mine, arrived, 16)
 
         @pl.when(lo != q)
         def _():
-            add_rows(mine, mine, across_buf.at[a, q], 16)
+            add_rows(arrived, mine, arrived, 16)
             near(a, q).start()
+
+        if q + 2 < nlo:
+            load_own(a, q + 2).start()
 
     def chain_event(a, seq, way):
         q = lay.lo_of_seq[seq]
         active = (z < seq) if way == 0 else (z > seq)
         first = (z == 0) if way == 0 else (z == nz - 1)
-        buf = (up_buf, down_buf)[way]
 
         @pl.when(active)
         def _():
@@ -498,7 +965,7 @@
             @pl.when(jnp.logical_not(first))
             def _():
                 along(a, seq, way).wait_recv()
-                add_rows(near_buf.at[a, q], near_buf.at[a, q], buf.at[a, seq], 16)
+                add_rows(near_buf.at[a, q], near_buf.at[a, q], chain_buf.at[a, seq], 16)
 
             along(a, seq, way).start()
 
@@ -513,63 +980,103 @@
 
         @pl.when(z > 0)
         def _():
-            arrived = up_buf.at[a, z]
+            arrived = chain_buf.at[a, z]
             remote(arrived, arrived, z_s.at[a, 0], z_r.at[a, z, 0], dev(z, hi, lo)).wait_recv()
 
         @pl.when(z < nz - 1)
         def _():
-            arrived = down_buf.at[a, z]
+            arrived = chain_buf.at[a, nz]
             remote(arrived, arrived, z_s.at[a, 0], z_r.at[a, z, 1], dev(z, hi, lo)).wait_recv()
 
         def body(k, carry):
             at = pl.ds(pl.multiple_of(k * 16, 16), 16)
             total = piece[at, :].astype(jnp.float32)
-            total = total + jnp.where(z > 0, up_buf[a, z, at, :].astype(jnp.float32), 0.0)
-            total = total + jnp.where(z < nz - 1, down_buf[a, z, at, :].astype(jnp.float32), 0.0)
+            total = total + jnp.where(z > 0, chain_buf[a, z, at, :].astype(jnp.float32), 0.0)
+            total = total + jnp.where(z < nz - 1, chain_buf[a, nz, at, :].astype(jnp.float32), 0.0)
             summed[a][at, :] = total
             return carry
 
         lax.fori_loop(0, rows // 16, body, 0)
 
-    sources = (wg_down, wg_up, wg_qkv)
     targets = (all_down, all_up, all_qkv)
-
-    def rows_of(g, h, rel):
+    lefts = (x_down, x_up, x_qkv)
+    n_slots = left.shape[0]
+    slots = [source % n_slots for source in range(3)]
+    rights = ((g_down, right_down), (g_up, right_up), (g_qkv, right_qkv), (g_out, right_out))
+
+    def load_left(source):
+        return pltpu.make_async_copy(lefts[source], left.at[slots[source]], left_c.at[source])
+
+    def load_right(source):
+        return pltpu.make_async_copy(*rights[source], right_c.at[source])
+
+    def start_loads():
+        for source in (0, 3, 1, 2):
+            if source < n_slots:
+                load_left(source).start()
+            load_right(source).start()
+
+    def ready(source):
+        load_left(source).wait()
+        load_right(source).wait()
+
+    def product(g, h, rel):
         source, first, wide, _, _ = chunks[g]
-        row = (h * nlo + flip(lo, rel, nlo)) * span
-        return sources[source].at[pl.ds(pl.multiple_of(row, span), span), pl.ds(first, wide)]
-
-    def load_acc(g, h, rel):
-        return pltpu.make_async_copy(rows_of(g, h, rel), acc[g].at[h, rel // 2], acc_c.at[g, h, rel // 2])
+        row = (h * nlo + differ(lo, rel, nlo)) * span
+        rows_at = pl.ds(pl.multiple_of(row, span), span)
+        part = lax.dot_general(
+            left[slots[source], :, rows_at], rights[source][1][:, first : first + wide],
+            contract_first, preferred_element_type=jnp.float32,
+        )
+        return part.astype(jnp.bfloat16)
 
     def stage_pieces(t):
         return [rel for rel in range(nlo) if rel % (2 << t) == (1 << t)]
 
     def stage_send(g, t, h, rel):
-        src = rows_of(g, h, rel) if t == 0 else acc[g].at[h, rel // 2]
+        if t == 0:
+            src = staged.at[g % 3, h, rel // 2, :, pl.ds(0, chunks[g][2])]
+        else:
+            src = acc[g].at[h, rel // 2]
         k = rel >> (t + 1)
         return remote(
             src, got[g][t].at[h, k], st_s.at[g, t, h, k], st_r.at[g, t, h, k], dev(z, hi, flip(lo, 1 << t, nlo))
         )
 
-    def stage_start(g, t):
-        for h in range(nhi):
-            for rel in stage_pieces(t):
-                stage_send(g, t, h, rel).start()
+    pairs = nhi * (nlo // 2)
 
     def start_chunk(g):
-        stage_start(g, 0)
-        for h in range(nhi):
-            for rel in range(0, nlo, 2):
-                load_acc(g, h, rel).start()
+        source, first, wide, _, _ = chunks[g]
+        if first == 0:
+            ready(source)
+        if g >= 3:
+            for h in range(nhi):
+                for rel in stage_pieces(0):
+                    stage_send(g - 3, 0, h, rel).wait_send()
+
+        def send(i, carry):
+            h, k = i // (nlo // 2), i % (nlo // 2)
+            staged[g % 3, h, k, :, :wide] = product(g, h, 2 * k + 1)
+            stage_send(g, 0, h, 2 * k + 1).start()
+            return carry
+
+        def keep_own(i, carry):
+            h, k = i // (nlo // 2), i % (nlo // 2)
+            acc[g][h, k] = product(g, h, 2 * k)
+            return carry
+
+        lax.fori_loop(0, pairs, send, 0)
+        lax.fori_loop(0, pairs, keep_own, 0)
+        if g == 0:
+            out_start()
+        if (g + 1 == n or chunks[g + 1][0] != source) and source + n_slots < 3:
+            load_left(source + n_slots).start()
 
     def stage_event(g, t):
         order = list(reversed(range(0, nlo, 2 << t)))
         for h in range(nhi):
             for rel in order:
                 k = rel >> (t + 1)
-                if t == 0:
-                    load_acc(g, h, rel).wait()
                 stage_send(g, t, h, rel | (1 << t)).wait_recv()
                 add_rows(acc[g].at[h, rel // 2], acc[g].at[h, rel // 2], got[g][t].at[h, k], 64)
                 if t + 1 < stages and rel % (4 << t) == (2 << t):
@@ -631,10 +1138,7 @@
             when_sent(g, flip(hi, dh, nhi), lambda dz=dz, dh=dh: owner_arrival(g, dz, dh).wait_recv())
 
     def out_rows(rel):
-        return wg_out.at[pl.ds(pl.multiple_of(flip(lo, rel, nlo) * grain, grain), grain)]
-
-    def out_load(rel):
-        return pltpu.make_async_copy(out_rows(rel), out_acc.at[rel // 2], out_c.at[rel // 2])
+        return out_part.at[pl.ds(pl.multiple_of(flip(lo, rel, nlo) * grain, grain), grain)]
 
     def out_send(t, rel):
         src = out_rows(rel) if t == 0 else out_acc.at[rel // 2]
@@ -642,17 +1146,26 @@
         return remote(src, out_got[t].at[k], out_s.at[t, k], out_r.at[t, k], dev(z, hi, flip(lo, 1 << t, nlo)))
 
     def out_start():
+        load_right(3).wait()
+        wide = min(512, width)
+
+        def body(i, carry):
+            at = pl.ds(pl.multiple_of(i * wide, wide), wide)
+            part = lax.dot_general(
+                right_out[...], left[0, :, at], contract_first, preferred_element_type=jnp.float32
+            )
+            out_part[:, at] = part.astype(jnp.bfloat16)
+            return carry
+
+        lax.fori_loop(0, width // wide, body, 0)
         for rel in stage_pieces(0):
             out_send(0, rel).start()
-        for rel in range(0, nlo, 2):
-            out_load(rel).start()
 
     def out_event(t):
         for rel in reversed(range(0, nlo, 2 << t)):
-            if t == 0:
-                out_load(rel).wait()
             out_send(t, rel | (1 << t)).wait_recv()
-            add_rows(out_acc.at[rel // 2], out_acc.at[rel // 2], out_got[t].at[rel >> (t + 1)], 16)
+            mine = out_rows(rel) if t == 0 else out_acc.at[rel // 2]
+            add_rows(out_acc.at[rel // 2], mine, out_got[t].at[rel >> (t + 1)], 16)
             if t + 1 < stages and rel % (4 << t) == (2 << t):
                 out_send(t + 1, rel).start()
         if t + 1 == stages:
@@ -671,8 +1184,8 @@
         return pltpu.make_async_copy(out_acc.at[0], all_out, move_s)
 
     doubling = (
-        [dev(z, hi, flip(lo, b, nlo)) for b in lay.bits]
-        + [dev(z, flip(hi, 1, nhi), lo)]
+        [dev(z, flip(hi, 1, nhi), lo)]
+        + [dev(z, hi, flip(lo, b, nlo)) for b in reversed(lay.bits)]
         + [dev(flip(z, b, nz), hi, lo) for b in lay.bits]
     )
 
@@ -690,7 +1203,7 @@
 
     act = dict(
         Y=start_across, A=across_event, B=chain_event, F=final_event, C=start_chunk, X=stage_event, G=finish_chunk,
-        P=out_start, Q=out_event, M=lambda: small_send(0).start(), N=small_event,
+        L=start_loads, Q=out_event, M=lambda: small_send(0).start(), N=small_event,
     )
     for item in scatter_schedule(nz, nlo, n, stages):
         act[item[0]](*item[1:])
@@ -710,6 +1223,8 @@
 
     for g in range(n):
         for t in range(stages):
+            if t == 0 and g + 3 < n:
+                continue
             for h in range(nhi):
                 for rel in stage_pieces(t):
                     stage_send(g, t, h, rel).wait_send()
@@ -729,12 +1244,12 @@
         small_send(t).wait_send()
 
 
-def scatter_all(lay, partial_o, partial_s, wg_down, wg_up, wg_qkv, wg_out, small):
+def scatter_all(lay, partial_o, partial_s, x_down, x_up, x_qkv, g_down, g_up, g_qkv, g_out, small):
     total, width = partial_o.shape
     nz, nlo, nhi = lay.nz, lay.nlo, lay.nhi
     rows = total // (nhi * nlo)
     ranks = nz * nhi
-    ff = wg_down.shape[1]
+    ff = g_down.shape[1]
     repeat = max(1, ranks // H)
     grain = width // (ranks * nlo)
     span = nz * grain
@@ -747,11 +1262,10 @@
     dma = pltpu.SemaphoreType.DMA
     bf16, f32 = jnp.bfloat16, jnp.float32
     scratch = [
-        pltpu.VMEM((2, nlo * rows, width), bf16),
+        pltpu.VMEM((2, 2, rows, width), bf16),
         pltpu.VMEM((2, nlo, rows, width), bf16),
         pltpu.VMEM((2, nlo, rows, width), bf16),
-        pltpu.VMEM((2, nz, rows, width), bf16),
-        pltpu.VMEM((2, nz, rows, width), bf16),
+        pltpu.VMEM((2, nz + 1, rows, width), bf16),
     ]
     for chunk in chunks:
         scratch.append(pltpu.VMEM((nhi, nlo // 2, span, chunk[2]), bf16))
@@ -762,11 +1276,19 @@
     for t in range(stages):
         scratch.append(pltpu.VMEM((nlo >> (t + 1), grain, width), bf16))
     scratch += [pltpu.VMEM((steps,) + small.shape, f32), pltpu.VMEM((steps,) + small.shape, f32)]
+    widest = max(chunk[2] for chunk in chunks)
+    scratch += [
+        pltpu.VMEM((2 if total <= 1024 else 1, total, width), bf16),
+        pltpu.VMEM(g_down.shape, bf16), pltpu.VMEM(g_up.shape, bf16), pltpu.VMEM(g_qkv.shape, bf16),
+        pltpu.VMEM(g_out.shape, bf16),
+        pltpu.VMEM((3, nhi, nlo // 2, span, widest), bf16),
+        pltpu.VMEM((width // ranks, width), bf16),
+    ]
     most = nlo // 2
     scratch += [
-        dma((2,)), dma((2, nlo)), dma((2, nlo)), dma((2, nlo)), dma((2, nlo)), dma((2, nz, 2)), dma((2, nz)),
-        dma((n, nhi, most)), dma((n, stages, nhi, most)), dma((n, stages, nhi, most)), dma((n, ranks)), dma((n, ranks)),
-        dma((n,)), dma((most,)), dma((stages, most)), dma((stages, most)), dma, dma, dma((steps,)), dma((steps,)),
+        dma((2, 2)), dma((2, nlo)), dma((2, nlo)), dma((2, nlo)), dma((2, nlo)), dma((2, nz, 2)), dma((2, nz)),
+        dma((n, stages, nhi, most)), dma((n, stages, nhi, most)), dma((n, ranks)), dma((n, ranks)),
+        dma((n,)), dma((stages, most)), dma((stages, most)), dma, dma, dma((steps,)), dma((steps,)), dma((3,)), dma((4,)),
     ]
     return pl.pallas_call(
         functools.partial(scatter_kernel, lay, (rows, width, ff, repeat)),
@@ -779,14 +1301,133 @@
             jax.ShapeDtypeStruct((grain, width), bf16),
             jax.ShapeDtypeStruct(small.shape, f32),
         ],
-        in_specs=[anywhere] * 6 + [inside],
+        in_specs=[anywhere] * 9 + [inside],
         out_specs=[inside, inside, anywhere, anywhere, anywhere, anywhere, inside],
         scratch_shapes=scratch,
         compiler_params=pltpu.CompilerParams(
             collective_id=2, has_side_effects=True, vmem_limit_bytes=60 * 1024 * 1024
         ),
         name="scatter_all",
-    )(partial_o, partial_s, wg_down, wg_up, wg_qkv, wg_out, small)
+    )(partial_o, partial_s, x_down, x_up, x_qkv, g_down, g_up, g_qkv, g_out, small)
+
+
+def plain_block(lay, operands):
+    f32, bf16 = jnp.float32, jnp.bfloat16
+    (own, own_cotangent, qkv_weight, qkv_bias, out_weight, up_weight, up_bias, down_weight,
+     attn_norm_gain, attn_norm_bias, mlp_norm_gain, mlp_norm_bias) = operands
+    nz, nlo, nhi = lay.nz, lay.nlo, lay.nhi
+    ranks = nz * nhi
+    rows, width = own.shape
+    weight_rows = qkv_weight.shape[0]
+    half = nlo * rows
+    z, hi, lo = place(lay)
+    rank = z * nhi + hi
+    ff = up_weight.shape[1] // ranks
+    repeat = max(1, ranks // H)
+    head = rank // repeat
+    score_scale = HD ** (-0.5)
+    seq_tokens, seq_cotangent, qkv_here, up_here, down_here = gather_all(
+        lay, own, own_cotangent, qkv_weight, up_weight, down_weight
+    )
+    own_qkv = jnp.concatenate(
+        [
+            lax.dynamic_slice(qkv_weight, (0, part * width + head * HD), (weight_rows, HD))
+            for part in range(3)
+        ],
+        axis=1,
+    )
+    own_up = lax.dynamic_slice(up_weight, (0, rank * ff), (weight_rows, ff))
+    own_down = lax.dynamic_slice(down_weight, (0, rank * ff), (weight_rows, ff))
+    qkv_here = lax.dynamic_update_slice(qkv_here, own_qkv, (z * weight_rows, 0))
+    up_here = lax.dynamic_update_slice(up_here, own_up, (z * weight_rows, 0))
+    down_here = lax.dynamic_update_slice(down_here, own_down, (z * weight_rows, 0))
+    out_head = lax.dynamic_slice(out_weight, (head * HD - z * weight_rows, 0), (HD, width))
+    out_rows = width // ranks
+    out_at = rank * out_rows - head * HD
+
+    positions = jnp.arange(2 * half, dtype=jnp.int32)
+
+    normed, _ = normalize(seq_tokens.astype(f32))
+    attn_in = (normed * attn_norm_gain + attn_norm_bias).astype(bf16)
+    mlp_in = (normed * mlp_norm_gain + mlp_norm_bias).astype(bf16)
+    bias_here = jnp.concatenate(
+        [lax.dynamic_slice(qkv_bias, (part * width + head * HD,), (HD,)) for part in range(3)]
+    )
+    projected = dot32(attn_in, qkv_here) + bias_here
+    queries = rotary(projected[:, :HD], positions).astype(bf16)
+    keys = rotary(projected[:, HD : 2 * HD], positions).astype(bf16)
+    values = projected[:, 2 * HD :].astype(bf16)
+    causal = positions[:, None] >= positions[None, :]
+    scores = jnp.where(causal, dot32(queries, keys, contract_last) * score_scale, masked_score)
+    top = jnp.max(scores, axis=-1, keepdims=True)
+    weights = jnp.where(causal, jnp.exp(scores - top), 0.0)
+    total = jnp.sum(weights, axis=-1, keepdims=True)
+    mixed_full = dot32(weights.astype(bf16), values) / total
+    log_total = top + jnp.log(total)
+    mixed = mixed_full.astype(bf16)
+    mixed_mine = lax.dynamic_slice(mixed, (0, out_at), (mixed.shape[0], out_rows))
+    out_mine = lax.dynamic_slice(out_head, (out_at, 0), (out_rows, width))
+    hidden = dot32(mlp_in, up_here) + lax.dynamic_slice(up_bias, (rank * ff,), (ff,))
+    activated_full, gelu_pull = jax.vjp(exact_gelu, hidden)
+    activated = activated_full.astype(bf16)
+    out_partial = dot32(mixed_mine, out_mine) + dot32(activated, down_here, contract_last)
+    grad_hidden = gelu_pull(dot32(seq_cotangent, down_here))[0].astype(bf16)
+    grad_mixed = dot32(seq_cotangent, out_head, contract_last).astype(bf16)
+    row_dot = jnp.sum(grad_mixed.astype(f32) * mixed_full, axis=-1, keepdims=True)
+    probs = jnp.where(causal, jnp.exp(scores - log_total), 0.0)
+    grad_values = dot32(probs.astype(bf16), grad_mixed, contract_first)
+    grad_probs = dot32(grad_mixed, values, contract_last)
+    grad_scores = (probs * (grad_probs - row_dot)).astype(bf16)
+    grad_queries = dot32(grad_scores, keys) * score_scale
+    grad_keys = dot32(grad_scores, queries, contract_first) * score_scale
+    grad_projected = jnp.concatenate(
+        [rotary(grad_queries, -positions), rotary(grad_keys, -positions), grad_values], axis=1
+    ).astype(bf16)
+    grad_attn_in = dot32(grad_projected, qkv_here, contract_last) * (1.0 / repeat)
+    grad_mlp_in = dot32(grad_hidden, up_here, contract_last)
+    in_partial = grad_attn_in * attn_norm_gain + grad_mlp_in * mlp_norm_gain
+    sums = jnp.stack(
+        [
+            jnp.sum(grad_attn_in * normed, axis=0),
+            jnp.sum(grad_attn_in, axis=0),
+            jnp.sum(grad_mlp_in * normed, axis=0),
+            jnp.sum(grad_mlp_in, axis=0),
+        ]
+    )
+    first_copy = jnp.where(rank % repeat == 0, 1.0, 0.0)
+    return (
+        seq_cotangent, attn_in, mlp_in, activated, grad_hidden, grad_projected, mixed_mine,
+        out_partial.astype(bf16), in_partial.astype(bf16), sums,
+        jnp.sum(grad_projected.astype(f32), axis=0) * first_copy,
+        jnp.sum(grad_hidden.astype(f32), axis=0),
+    )
+
+
+def fused_block(lay, operands):
+    f32 = jnp.float32
+    (own, own_cotangent, qkv_weight, qkv_bias, out_weight, up_weight, up_bias, down_weight,
+     attn_norm_gain, attn_norm_bias, mlp_norm_gain, mlp_norm_bias) = operands
+    rows, width = own.shape
+    z, hi, _ = place(lay)
+    rank = z * lay.nhi + hi
+    ff = up_weight.shape[1] // (lay.nz * lay.nhi)
+    total = lay.nhi * lay.nlo * rows
+    bias_here = jnp.concatenate(
+        [lax.dynamic_slice(qkv_bias, (part * width + rank * HD,), (HD,)) for part in range(3)]
+    )
+    half_rot = ROT // 2
+    inv_freq = 10000.0 ** (-(jnp.arange(half_rot, dtype=f32) * 2.0) / ROT)
+    angles = jnp.arange(total, dtype=f32)[:, None] * inv_freq[None, :]
+    cosine, sine = jnp.cos(angles), jnp.sin(angles)
+    rest = jnp.zeros((total, 128 - ROT), f32)
+    found = block_all(
+        lay, own, own_cotangent, qkv_weight, up_weight, down_weight, out_weight,
+        bias_here[None], lax.dynamic_slice(up_bias, (rank * ff,), (ff,))[None],
+        [v[None] for v in (attn_norm_gain, attn_norm_bias, mlp_norm_gain, mlp_norm_bias)],
+        jnp.concatenate([cosine, cosine, rest + 1.0], axis=1),
+        jnp.concatenate([-sine, sine, rest], axis=1),
+    )
+    return tuple(found[:9]) + (found[11], found[12][0], found[13][0])
 
 
 def local_block(
@@ -821,83 +1462,23 @@
     ff = hidden_width // ranks
     repeat = max(1, ranks // H)
     head = rank // repeat
-    score_scale = HD ** (-0.5)
     own = tokens[0]
     own_cotangent = cotangent[0]
-    seq_tokens, seq_cotangent, qkv_here, up_here, down_here = gather_all(
-        lay, own, own_cotangent, qkv_weight, up_weight, down_weight
-    )
-    own_qkv = jnp.concatenate(
-        [
-            lax.dynamic_slice(qkv_weight, (0, part * width + head * HD), (weight_rows, HD))
-            for part in range(3)
-        ],
-        axis=1,
-    )
-    own_up = lax.dynamic_slice(up_weight, (0, rank * ff), (weight_rows, ff))
-    own_down = lax.dynamic_slice(down_weight, (0, rank * ff), (weight_rows, ff))
-    qkv_here = lax.dynamic_update_slice(qkv_here, own_qkv, (z * weight_rows, 0))
-    up_here = lax.dynamic_update_slice(up_here, own_up, (z * weight_rows, 0))
-    down_here = lax.dynamic_update_slice(down_here, own_down, (z * weight_rows, 0))
-    out_head = lax.dynamic_slice(out_weight, (head * HD - z * weight_rows, 0), (HD, width))
-    out_rows = width // ranks
-    out_at = rank * out_rows - head * HD
-
-    positions = jnp.arange(2 * half, dtype=jnp.int32)
-
-    normed, _ = normalize(seq_tokens.astype(f32))
-    attn_in = (normed * attn_norm_gain + attn_norm_bias).astype(bf16)
-    mlp_in = (normed * mlp_norm_gain + mlp_norm_bias).astype(bf16)
-    bias_here = jnp.concatenate(
-        [lax.dynamic_slice(qkv_bias, (part * width + head * HD,), (HD,)) for part in range(3)]
-    )
-    projected = dot32(attn_in, qkv_here) + bias_here
-    queries = rotary(projected[:, :HD], positions).astype(bf16)
-    keys = rotary(projected[:, HD : 2 * HD], positions).astype(bf16)
-    values = projected[:, 2 * HD :].astype(bf16)
-    causal = positions[:, None] >= positions[None, :]
-    scores = jnp.where(causal, dot32(queries, keys, contract_last) * score_scale, masked_score)
-    top = jnp.max(scores, axis=-1, keepdims=True)
-    weights = jnp.where(causal, jnp.exp(scores - top), 0.0)
-    total = jnp.sum(weights, axis=-1, keepdims=True)
-    mixed_full = dot32(weights.astype(bf16), values) / total
-    log_total = top + jnp.log(total)
-    mixed = mixed_full.astype(bf16)
-    mixed_mine = lax.dynamic_slice(mixed, (0, out_at), (mixed.shape[0], out_rows))
-    out_mine = lax.dynamic_slice(out_head, (out_at, 0), (out_rows, width))
-    hidden = dot32(mlp_in, up_here) + lax.dynamic_slice(up_bias, (rank * ff,), (ff,))
-    activated_full, gelu_pull = jax.vjp(exact_gelu, hidden)
-    activated = activated_full.astype(bf16)
-    out_partial = dot32(mixed_mine, out_mine) + dot32(activated, down_here, contract_last)
-    down_grad = dot32(seq_cotangent, activated, contract_first)
-    out_grad = dot32(mixed_mine, seq_cotangent, contract_first)
-    grad_hidden = gelu_pull(dot32(seq_cotangent, down_here))[0].astype(bf16)
-    up_grad = dot32(mlp_in, grad_hidden, contract_first)
-    grad_mixed = dot32(seq_cotangent, out_head, contract_last).astype(bf16)
-    row_dot = jnp.sum(grad_mixed.astype(f32) * mixed_full, axis=-1, keepdims=True)
-    probs = jnp.where(causal, jnp.exp(scores - log_total), 0.0)
-    grad_values = dot32(probs.astype(bf16), grad_mixed, contract_first)
-    grad_probs = dot32(grad_mixed, values, contract_last)
-    grad_scores = (probs * (grad_probs - row_dot)).astype(bf16)
-    grad_queries = dot32(grad_scores, keys) * score_scale
-    grad_keys = dot32(grad_scores, queries, contract_first) * score_scale
-    grad_projected = jnp.concatenate(
-        [rotary(grad_queries, -positions), rotary(grad_keys, -positions), grad_values], axis=1
-    ).astype(bf16)
-    qkv_grad = dot32(attn_in, grad_projected, contract_first)
-    grad_attn_in = dot32(grad_projected, qkv_here, contract_last) * (1.0 / repeat)
-    grad_mlp_in = dot32(grad_hidden, up_here, contract_last)
-    in_partial = grad_attn_in * attn_norm_gain + grad_mlp_in * mlp_norm_gain
-
-    first_copy = jnp.where(rank % repeat == 0, 1.0, 0.0)
-    qkv_bias_part = jnp.sum(grad_projected.astype(f32), axis=0) * first_copy
+    operands = (
+        own, own_cotangent, qkv_weight, qkv_bias, out_weight, up_weight, up_bias, down_weight,
+        attn_norm_gain, attn_norm_bias, mlp_norm_gain, mlp_norm_bias,
+    )
+    fits = repeat == 1 and nhi * half * width <= 1024 * 2048
+    (seq_cotangent, attn_in, mlp_in, activated, grad_hidden, grad_projected, mixed_mine,
+     out_partial, in_partial, sums, qkv_bias_part, up_bias_part) = (fused_block if fits else plain_block)(lay, operands)
+
     qkv_bias_full = jnp.zeros((3, width), f32)
     qkv_bias_full = lax.dynamic_update_slice(
         qkv_bias_full, qkv_bias_part.reshape(3, HD), (0, head * HD)
     ).reshape(-1)
     up_bias_full = lax.dynamic_update_slice(
         jnp.zeros((hidden_width,), f32),
-        jnp.sum(grad_hidden.astype(f32), axis=0),
+        up_bias_part,
         (rank * ff,),
     )
     small = jnp.concatenate(
@@ -905,20 +1486,20 @@
             qkv_bias_full,
             up_bias_full,
             jnp.sum(own_cotangent.astype(f32), axis=0),
-            jnp.sum(grad_attn_in * normed, axis=0),
-            jnp.sum(grad_attn_in, axis=0),
-            jnp.sum(grad_mlp_in * normed, axis=0),
-            jnp.sum(grad_mlp_in, axis=0),
+            sums.reshape(-1),
         ]
     ).reshape(-1, 128)
     summed_out, summed_in, all_down, all_up, all_qkv, all_out, small = scatter_all(
         lay,
-        out_partial.astype(bf16),
-        in_partial.astype(bf16),
-        down_grad.astype(bf16),
-        up_grad.astype(bf16),
-        qkv_grad.astype(bf16),
-        out_grad.astype(bf16),
+        out_partial,
+        in_partial,
+        seq_cotangent,
+        mlp_in,
+        attn_in,
+        activated,
+        grad_hidden,
+        grad_projected,
+        mixed_mine,
         small,
     )
     output = (own.astype(f32) + summed_out + (out_bias + down_bias)).astype(bf16)[None]

time: 503 us -> 423 us (0.84)
  the two profiles are of different devices: /device:TPU:0 before, /device:TPU:19 now
where the time goes in v3:
time: 423 us; the launch traced here: 417 us
  Pallas kernels  395 us (93%)
  other arithmetic  13.5 us (3%)
  local copies, waits for them, and re-layouts  7.48 us (2%)
    pallas_call x1, Pallas kernels, scatter_all(): pl.pallas_call(functools.partial(scatter_kernel, lay, (rows, width, ff, r...  214 us
    pallas_call x1, Pallas kernels, block_all(): pl.pallas_call(functools.partial(block_kernel, lay, (rows, width, qkv.sha...  181 us

profile of v3, /device:TPU:19, one launch (start us, length us, event | category | flops | bytes accessed | tf_op | source)
XLA Modules:
  0.0 417.1 jit_solution(7914714480546791805)
XLA Ops:
  0.7 1.3 dynamic_slice.15
  2.0 0.8 fusion.16
  2.8 0.6 broadcast_in_dim.40.refs_6_
  3.4 2.0 fusion.14
  5.3 0.1 pad.6.clone
  5.4 0.1 pad.9.clone
  5.5 1.3 maximum_maximum_fusion
  6.8 180.6 %block_all.1 = (bf16[1024,2048]{1,0:T(8,128)(2,1)}, bf16[1024,2048]{1,0:T(8,128)(2,1)}, bf16[1024,2048]{1,0:T(8,128)(2,1)}, bf16[1024,1024]{1,0:T(8,128)(2,1)}, ...) custom-call(bf16[128,2048]{1,0:T(8,128)(2,1)} %bitcast.37, ...), custom_call_target="tpu_custom_call" | custom-call | tf_op jit(solution)/shard_map/block_all/pallas_call | solution.py:770
  187.4 0.7 reduce
  188.2 0.9 dynamic_update_slice.7
  189.1 0.8 copy.28
  189.8 0.0 copy-done.1
  189.8 0.1 convert_reduce_fusion.1
  189.9 0.6 maximum_bitcast_fusion.refs_9_
  190.6 214.3 %scatter_all.1 = (f32[128,2048]{1,0:T(8,128)}, f32[128,2048]{1,0:T(8,128)}, bf16[64,8192]{1,0:T(8,128)(2,1)}, bf16[64,8192]{1,0:T(8,128)(2,1)}, bf16[64,6144]{1,...) custom-call(bf16[1024,2048]{1,0:T(8,128)(2,1)} %get-tuple-element.33.refs_0_, ...), custom_call_target="tpu_custom_call" | custom-call | tf_op jit(solution)/shard_map/scatter_all/pallas_call | solution.py:1293
  404.9 0.0 copy-start.3
  404.9 2.8 convert_element_type.28
  407.7 1.5 convert_element_type.29
  409.1 0.2 convert_reduce_fusion
  409.3 0.3 fusion.7
  409.6 0.2 copy-done.2
  409.8 0.3 fusion.15
  410.1 0.0 copy-done.9
  410.2 0.0 copy-done.10
  410.2 0.3 copy-done.4
  410.5 1.7 fusion.8
  412.2 1.2 convert_element_type.26
  413.4 0.8 convert_element_type.27
  414.2 0.6 slice_bitcast_fusion.2
  414.9 0.6 slice_bitcast_fusion
  415.5 0.6 slice_bitcast_fusion.1
  416.1 0.6 copy.32
  (30 shorter events, 0.1 us)
Async XLA Ops:
  6.8 183.0 %copy-start.1 = (bf16[1,128,2048]{2,1,0:T(8,128)(2,1)S(1)}, bf16[1,128,2048]{2,1,0:T(8,128)(2,1)}, u32[]{:S(2)}) copy-start(bf16[1,128,2048]{2,1,0:T(8,128)(2,1)} %param.27) | copy-start | bytes 1572868
  404.9 2.8 copy-start.3
  407.7 1.5 copy-start
  407.7 2.1 copy-start.2
  409.1 1.0 copy-start.9
  409.1 1.0 copy-start.10
  409.1 1.3 copy-start.4
  410.5 1.7 copy-start.5
  412.1 1.3 copy-start.6
  412.2 2.1 copy-start.7
  414.9 1.8 copy-start.8

commit v4 on v3

--- a/solution.py
+++ b/solution.py
@@ -339,52 +339,26 @@
     return jnp.concatenate([left * cosine + swapped * sine, values[:, 128:]], axis=1)
 
 
-def block_schedule(order_w, nlo, by_bit, n_groups, blocks, n_short):
-    timed = [(t, ("N", a)) for a, t in ((0, -9), (1, 10))]
-    timed += [(-5, ("WO",))]
-    for a, (first, step) in enumerate(((12, 12), (40, 12))):
-        timed.append((first - 1, ("D", a, 0)))
-        for k in range(1, nlo):
-            timed.append((first + step * (k - 1), ("Z", a, k)))
-            timed.append((first + step * (k - 1) + 8, ("D", a, k)))
-    sizes = [1, 1, 1, 4, 4]
-    sent = 0.0
-    for g, i in order_w:
-        timed.append((20 + 2.5 * sent, ("W", g, i)))
-        timed.append((20 + 2.5 * sent + 20, ("E", g, i, 0)))
-        for r in by_bit:
-            timed.append((20 + 2.5 * sent + 20 + (20 if low_bit(r) > 1 else 20 + 8), ("E", g, i, r)))
-        sent += sizes[g]
-    after = {}
-
-    def put(name, time, item):
-        timed.append((time, item))
-        after[name] = max(after.get(name, 0), time) + 0.01
-
-    ready = [max(t for t, item in timed if item[0] == "E" and item[1] == g) for g in range(n_groups)]
-    seen = [max(t for t, item in timed if item[0] == "D" and item[1] == a) for a in range(2)]
-    put("H", max(50, seen[0] + 0.1), ("H", 0))
-    put("H", max(70, after["H"]), ("H", 1))
-    put("CO", max(100, seen[1] + 0.1, after["H"]), ("CO",))
-    for k in range(blocks):
-        put("K", max(after["H"], max(ready[:3])) + 0.1 + 0.01 * k, ("K", k))
-    for k in range(blocks):
-        put("AF", after["K"] + 0.01 * k, ("AF", k))
-    for k in range(blocks):
-        put("U", max(after["AF"], ready[3]) + 0.1 + 0.01 * k, ("U", k))
-    for k in range(blocks):
-        put("GM", max(after["CO"], after["U"]) + 0.1 + 0.01 * k, ("GM", k))
-    for k in range(blocks):
-        put("AB", after["GM"] + 0.1 + 0.01 * k, ("AB", k))
-    put("BP", after["AB"] + 0.1, ("BP",))
-    for k in range(blocks):
-        put("O", max(after["BP"], max(ready)) + 0.1 + 0.01 * k, ("O", k))
-    for k in range(blocks):
-        put("GH", max(after["O"], max(ready)) + 0.1 + 0.01 * k, ("GH", k))
-    for k in range(n_short):
-        put("S", max(after["GH"], after["BP"]) + 0.1, ("S", k))
-    timed.sort(key=lambda entry: entry[0])
-    return [entry[1] for entry in timed]
+def block_schedule():
+    return [
+        ("N", 0), ("WO",), ("N", 1), ("D", 0, 0), ("Z", 0, 1), ("D", 0, 1), ("W", 0, 1), ("W", 0, 2), ("Z", 0, 2),
+        ("W", 0, 3), ("W", 1, 1), ("W", 1, 2), ("D", 0, 2), ("W", 1, 3), ("W", 2, 1), ("Z", 0, 3), ("W", 2, 2),
+        ("D", 1, 0), ("Z", 1, 1), ("E", 0, 1, 0), ("W", 2, 3), ("E", 0, 2, 0), ("W", 3, 1), ("D", 0, 3),
+        ("E", 0, 3, 0), ("E", 1, 1, 0), ("D", 1, 1), ("E", 1, 2, 0), ("H", 0), ("Z", 1, 2), ("E", 1, 3, 0),
+        ("W", 3, 2), ("E", 2, 1, 0), ("E", 2, 2, 0), ("D", 1, 2), ("E", 0, 1, 2), ("E", 2, 3, 0), ("E", 0, 2, 2),
+        ("E", 3, 1, 0), ("W", 3, 3), ("Z", 1, 3), ("E", 0, 3, 2), ("E", 1, 1, 2), ("E", 0, 1, 1), ("E", 0, 1, 3),
+        ("E", 1, 2, 2), ("H", 1), ("E", 0, 2, 1), ("E", 0, 2, 3), ("D", 1, 3), ("E", 1, 3, 2), ("E", 3, 2, 0),
+        ("W", 4, 1), ("E", 0, 3, 1), ("E", 0, 3, 3), ("E", 2, 1, 2), ("E", 1, 1, 1), ("E", 1, 1, 3), ("E", 2, 2, 2),
+        ("E", 1, 2, 1), ("E", 1, 2, 3), ("E", 2, 3, 2), ("E", 1, 3, 1), ("E", 1, 3, 3), ("E", 3, 1, 2),
+        ("E", 3, 3, 0), ("W", 4, 2), ("E", 2, 1, 1), ("E", 2, 1, 3), ("E", 2, 2, 1), ("E", 2, 2, 3), ("E", 2, 3, 1),
+        ("E", 2, 3, 3), ("K", 0), ("K", 1), ("K", 2), ("K", 3), ("AF", 0), ("AF", 1), ("AF", 2), ("AF", 3),
+        ("E", 3, 1, 1), ("E", 3, 1, 3), ("E", 3, 2, 2), ("E", 4, 1, 0), ("W", 4, 3), ("CO",), ("GM", 0), ("GM", 1),
+        ("GM", 2), ("GM", 3), ("E", 3, 2, 1), ("E", 3, 2, 3), ("AB", 0), ("AB", 1), ("E", 3, 3, 2), ("E", 4, 2, 0),
+        ("AB", 2), ("AB", 3), ("BP",), ("E", 3, 3, 1), ("E", 3, 3, 3), ("U", 0), ("U", 1), ("E", 4, 1, 2), ("U", 2),
+        ("U", 3), ("E", 4, 3, 0), ("E", 4, 1, 1), ("E", 4, 1, 3), ("V", 0), ("E", 4, 2, 2), ("E", 4, 2, 1),
+        ("E", 4, 2, 3), ("V", 1), ("E", 4, 3, 2), ("VX", 0), ("E", 4, 3, 1), ("E", 4, 3, 3), ("VX", 1), ("O", 0),
+        ("O", 1), ("O", 2), ("O", 3), ("VO",), ("GH", 0), ("GH", 1), ("GH", 2), ("GH", 3), ("VY", 0), ("VY", 1),
+    ]
 
 
 def block_kernel(lay, sizes, *refs):
@@ -400,12 +374,15 @@
 
     tok, cot, qkv, up, down, out_w = take(6)
     qkv_b, up_b, gain_a, shift_a, gain_m, shift_m, cos_t, sin_t = take(8)
-    seq_c_out, attn_out, mlp_out, act_out, gh_out, gp_out, mixed_out, o_out, s_out, stage_t, stage_c = take(11)
-    vec_out, qkv_b_out, up_b_out = take(3)
+    seq_c_out, attn_out, mlp_out, act_out, gh_out, gp_out, mixed_out, o_out, stage_t, stage_c = take(10)
+    seq_t_out, w_qkv_out, w_up_out, means_out, scales_out = take(5)
+    early_out, part_out = take(2), take(1)[0]
+    qkv_b_out, up_b_out = take(2)
     seq_t, seq_c, w_qkv, w_up, w_down, w_out = take(6)
     attn_in, mlp_in, q_ref, k_ref, v_ref, mixed, mixed_full, lse, slope, act, gh, gm = take(12)
-    dq, dk, dv, gp, o_buf, s_buf, means, scales = take(8)
-    near_r, near_s, home_c, z_r, z_s, y_r, y_s, wz_r, wz_s, wf_r, wf_s, own_c, out_c, o_c, s_c = take(15)
+    dq, dk, dv, gp, o_buf, means, scales, out_part, theirs = take(9)
+    mine, came, last = take(2), take(2), take(2)
+    near_r, near_s, home_c, z_r, z_s, y_r, y_s, wz_r, wz_s, wf_r, wf_s, own_c, out_c, o_c, pair_r, pair_s, last_r, last_s, early_c = take(19)
 
     z, hi, lo = place(lay)
     half, quarter = nlo * rows, weight_rows // nlo
@@ -569,7 +546,8 @@
 
     tall = 256
     blocks = total // tall
-    kept = ((seq_c, seq_c_out), (attn_in, attn_out), (mlp_in, mlp_out), (act, act_out), (gh, gh_out), (gp, gp_out), (mixed, mixed_out))
+    kept = ((seq_c, seq_c_out), (attn_in, attn_out), (mlp_in, mlp_out), (act, act_out), (gh, gh_out), (gp, gp_out), (mixed, mixed_out),
+            (seq_t, seq_t_out), (w_qkv, w_qkv_out), (w_up, w_up_out), (means, means_out), (scales, scales_out))
 
     def save(k):
         return pltpu.make_async_copy(*kept[k], out_c.at[k])
@@ -601,13 +579,14 @@
 
         lax.fori_loop(0, half // step, body, 0)
         if which == 1:
-            save(1).start()
-            save(2).start()
+            for k in (1, 2, 7, 10, 11):
+                save(k).start()
 
     def project(i):
         if i == 0:
             for g in range(3):
                 own_weight(g).wait()
+            save(8).start()
         at = at_block(i)
         raw = jnp.dot(attn_in[at, :], w_qkv[...], preferred_element_type=f32) + qkv_b[...]
         q_ref[at, :] = turn(raw[:, :HD], cos_t[at, :], sin_t[at, :]).astype(bf16)
@@ -637,6 +616,7 @@
     def hidden(i):
         if i == 0:
             own_weight(3).wait()
+            save(9).start()
         at = at_block(i)
         value = jnp.dot(mlp_in[at, :], w_up[...], preferred_element_type=f32) + up_b[...]
         cdf = (1.0 + lax.erf(value * (0.5 ** 0.5))) * 0.5
@@ -704,39 +684,94 @@
             qkv_b_out[...] += jnp.sum(part.astype(f32), axis=0, keepdims=True)
         save(5).start()
 
-    short = 128
-
-    def in_store(i):
-        return pltpu.make_async_copy(s_buf.at[pl.ds(i * short, short)], s_out.at[pl.ds(i * short, short)], s_c.at[i])
-
-    def in_block(i):
-        if i == 0:
-            vec_out[...] = jnp.zeros_like(vec_out)
-        at = pl.ds(i * short, short)
-        grad_a = dot32(gp[at, :], w_qkv[...], contract_last)
-        grad_m = dot32(gh[at, :], w_up[...], contract_last)
-        s_buf[at, :] = (grad_a * gain_a[...] + grad_m * gain_m[...]).astype(bf16)
-        normed = (seq_t[at, :].astype(f32) - means[at, :1]) * scales[at, :1]
-        for k, term in enumerate((grad_a * normed, grad_a, grad_m * normed, grad_m)):
-            vec_out[k : k + 1, :] += jnp.sum(term, axis=0, keepdims=True)
-        in_store(i).start()
+    grain = width // (nz * nhi * nlo)
+    span = nz * grain
+    part_ff = ff // 2
+
+    def product(c, h, rel):
+        row = (h * nlo + differ(lo, rel, nlo)) * span
+        rows_at = pl.ds(pl.multiple_of(row, span), span)
+        return dot32(seq_c[:, rows_at], act[:, c * part_ff : (c + 1) * part_ff], contract_first).astype(bf16)
+
+    def pair_send(c, h, k):
+        return remote(
+            theirs.at[h, k], came[c].at[h, k], pair_s.at[c, h, k], pair_r.at[c, h, k], dev(z, hi, flip(lo, 1, nlo))
+        )
+
+    def last_send(c, h):
+        return remote(
+            mine[c].at[h, 1], last[c].at[h], last_s.at[c, h], last_r.at[c, h], dev(z, hi, flip(lo, 2, nlo))
+        )
+
+    def pair_start(c):
+        if c == 1:
+            for h in range(nhi):
+                for k in range(2):
+                    pair_send(0, h, k).wait_send()
+
+        def send(i, carry):
+            h, k = i // 2, i % 2
+            theirs[h, k] = product(c, h, 2 * k + 1)
+            pair_send(c, h, k).start()
+            return carry
+
+        def keep_own(i, carry):
+            h, k = i // 2, i % 2
+            mine[c][h, k] = product(c, h, 2 * k)
+            return carry
+
+        lax.fori_loop(0, nhi * 2, send, 0)
+        lax.fori_loop(0, nhi * 2, keep_own, 0)
+
+    def pair_event(c):
+        for k in (1, 0):
+            for h in range(nhi):
+                pair_send(c, h, k).wait_recv()
+                add_rows(mine[c].at[h, k], mine[c].at[h, k], came[c].at[h, k], 64)
+                if k == 1:
+                    last_send(c, h).start()
+
+    def early_store(c):
+        return pltpu.make_async_copy(mine[c].at[:, 0], early_out[c], early_c.at[c])
+
+    def last_event(c):
+        for h in range(nhi):
+            last_send(c, h).wait_recv()
+            add_rows(mine[c].at[h, 0], mine[c].at[h, 0], last[c].at[h], 64)
+        early_store(c).start()
+
+    def part_store():
+        return pltpu.make_async_copy(out_part, part_out, early_c.at[2])
+
+    def out_product():
+        step = min(512, width)
+        for first in range(0, width, step):
+            out_part[:, first : first + step] = dot32(
+                mixed[...], seq_c[:, first : first + step], contract_first
+            ).astype(bf16)
+        part_store().start()
 
     act_of = dict(
         N=lambda a: dispatch(a, 0), Z=chain_event, D=near_event, W=lambda g, i: weight_z(g, i).start(), E=weight_event,
         WO=own_start, H=norm, K=project, AF=attend, U=hidden, CO=cotangent_here, GM=back_mixed, GH=back_hidden,
-        O=out_block, AB=back_attend, BP=back_project, S=in_block,
+        O=out_block, AB=back_attend, BP=back_project,
+        V=pair_start, VX=pair_event, VY=last_event, VO=out_product,
     )
     order_w = [(g, i) for g in range(len(groups)) for i in range(1, nz)]
-    by_bit = sorted(range(1, nlo), key=lambda r: -low_bit(r))
-    for item in block_schedule(order_w, nlo, by_bit, len(groups), blocks, total // short):
+    for item in block_schedule():
         act_of[item[0]](*item[1:])
 
     for k in range(len(kept)):
         save(k).wait()
     for i in range(blocks):
         out_store(i).wait()
-    for i in range(total // short):
-        in_store(i).wait()
+    for c in range(2):
+        early_store(c).wait()
+        for h in range(nhi):
+            last_send(c, h).wait_send()
+            for k in range(2 if c == 1 else 0):
+                pair_send(c, h, k).wait_send()
+    part_store().wait()
     for g, i in order_w:
         weight_z(g, i).wait_send()
         for r in range(nlo):
@@ -767,29 +802,34 @@
     def vmem(*dims, kind=bf16):
         return pltpu.VMEM(dims, kind)
 
+    span = width // (lay.nhi * nlo)
     return pl.pallas_call(
         functools.partial(block_kernel, lay, (rows, width, qkv.shape[0], ff)),
         out_shape=[
             shape(total, width), shape(total, width), shape(total, width), shape(total, ff), shape(total, ff),
-            shape(total, 3 * HD), shape(total, HD), shape(total, width), shape(total, width),
+            shape(total, 3 * HD), shape(total, HD), shape(total, width),
             shape(nz, rows, width), shape(nz, rows, width),
-            shape(4, width, kind=f32), shape(1, 3 * HD, kind=f32), shape(1, ff, kind=f32),
+            shape(total, width), shape(width, 3 * HD), shape(width, ff), shape(total, 128, kind=f32), shape(total, 128, kind=f32),
+            shape(lay.nhi, span, ff // 2), shape(lay.nhi, span, ff // 2), shape(HD, width),
+            shape(1, 3 * HD, kind=f32), shape(1, ff, kind=f32),
         ],
         in_specs=[anywhere] * 6 + [inside] * 8,
-        out_specs=[anywhere] * 11 + [inside] * 3,
+        out_specs=[anywhere] * 18 + [inside] * 2,
         scratch_shapes=[
             vmem(total, width), vmem(total, width), vmem(width, 3 * HD), vmem(width, ff), vmem(width, ff), vmem(HD, width),
             vmem(total, width), vmem(total, width), vmem(total, HD), vmem(total, HD), vmem(total, HD), vmem(total, HD),
             vmem(total, HD, kind=f32), vmem(total, 128, kind=f32), vmem(total, ff, kind=f32), vmem(total, ff),
             vmem(total, ff), vmem(total, HD),
             vmem(total, HD, kind=f32), vmem(total, HD, kind=f32), vmem(total, HD, kind=f32), vmem(total, 3 * HD),
-            vmem(total, width), vmem(total, width), vmem(total, 128, kind=f32), vmem(total, 128, kind=f32),
+            vmem(total, width), vmem(total, 128, kind=f32), vmem(total, 128, kind=f32),
+            vmem(HD, width), *[vmem(lay.nhi, 2, span, ff // 2)] * 5, *[vmem(lay.nhi, span, ff // 2)] * 2,
             dma((2, nlo)), dma((2, nz)), dma((2,)), dma((2, nz)), dma((2, nz, 2)), dma((2, nlo)), dma((2, nlo)),
             dma((5, nz - 1)), dma((5, nz - 1)), dma((5, nz - 1, nlo)), dma((5, nz - 1, nlo, bits)), dma((6,)),
-            dma((7,)), dma((total // 256,)), dma((total // 128,)),
+            dma((12,)), dma((total // 256,)),
+            dma((2, lay.nhi, 2)), dma((2, lay.nhi, 2)), dma((2, lay.nhi)), dma((2, lay.nhi)), dma((3,)),
         ],
         compiler_params=pltpu.CompilerParams(
-            collective_id=3, has_side_effects=True, vmem_limit_bytes=62 * 1024 * 1024
+            collective_id=3, has_side_effects=True, vmem_limit_bytes=63 * 1024 * 1024
         ),
         name="block_all",
     )(tok, cot, qkv, up, down, out_w, qkv_b, up_b, *gains, cos_t, sin_t)
@@ -826,29 +866,43 @@
     return chunks
 
 
-def scatter_schedule(nz, nlo, n_chunks, stages):
-    timed = [(-4, ("M",)), (-3, ("L",)), (-2, ("Y", 0)), (30, ("Y", 1))]
+def scatter_schedule(nz, nlo, n_chunks, stages, n_slabs):
+    if n_slabs:
+        return [
+            ("L",), ("Y", 0), ("Y", 1), ("C", 0), ("C", 1), ("P",), ("C", 2), ("X", 0, 0), ("X", 0, 1), ("C", 3),
+            ("X", 2, 0), ("S", 0), ("X", 3, 0), ("S", 1), ("A", 0, 0), ("S", 2), ("A", 0, 1), ("S", 3), ("X", 1, 0),
+            ("X", 1, 1), ("X", 2, 1), ("S", 4), ("A", 0, 2), ("S", 5), ("S", 6), ("A", 0, 3), ("S", 7), ("M",), ("C", 4),
+            ("N", 0), ("A", 1, 0), ("X", 3, 1), ("C", 5), ("N", 1), ("X", 4, 0), ("N", 2), ("Y", 2), ("Y", 3), ("C", 6),
+            ("A", 1, 1), ("A", 1, 2), ("B", 0, 0), ("A", 1, 3), ("N", 3), ("Q", 0), ("X", 5, 0), ("B", 0, 1),
+            ("B", 1, 0), ("N", 4), ("A", 2, 0), ("X", 4, 1), ("X", 6, 0), ("A", 2, 1), ("B", 0, 2), ("B", 1, 1),
+            ("X", 5, 1), ("A", 2, 2), ("X", 6, 1), ("B", 1, 2), ("A", 2, 3), ("Q", 1), ("A", 3, 0), ("B", 2, 0),
+            ("A", 3, 1), ("B", 2, 1), ("A", 3, 2), ("B", 2, 2), ("A", 3, 3), ("B", 3, 0), ("F", 0), ("F", 1),
+            ("B", 3, 1), ("B", 3, 2), ("F", 2), ("F", 3), ("G", 0), ("G", 1), ("G", 2), ("G", 3), ("G", 4), ("G", 5),
+            ("G", 6),
+        ]
+    timed = [(51 if n_slabs else -4, ("M",)), (4, ("P",)), (-3, ("L",)), (-2, ("Y", 0)), (-2, ("Y", 1)), (52, ("Y", 2)), (52, ("Y", 3))]
+    for k in range(n_slabs):
+        timed.append((30 + 2 * k, ("S", k)))
     for g in range(n_chunks):
         timed.append((0 + 4 * g, ("C", g)))
         for t in range(stages):
-            timed.append((10 + 14 * g + 20 * t, ("X", g, t)))
-    for a, (first, step, chain, hop) in enumerate(((14, 11.4, 60, 11), (60, 11.4, 106, 11))):
+            timed.append((10 + 14 * g + 25 * t, ("X", g, t)))
+    for b, (first, step, chain, hop) in enumerate(((14, 11.4, 66, 11), (14, 11.4, 66, 11), (66, 11.4, 112, 11), (66, 11.4, 112, 11))):
         for q in range(nlo):
-            timed.append((first + step * q, ("A", a, q)))
+            timed.append((first + step * q, ("A", b, q)))
         for m in range(nz - 1):
-            timed.append((chain + hop * m, ("B", a, nz - 1 - m, 0)))
-            timed.append((chain + hop * m, ("B", a, m, 1)))
-        timed.append((chain + hop * (nz - 1), ("F", a)))
+            timed.append((chain + hop * m, ("B", b, m)))
+        timed.append((chain + hop * (nz - 1), ("F", b)))
     for t in range(stages):
         timed.append((100 + 10 * t, ("Q", t)))
     for t in range(2 * stages + 1):
-        timed.append((1 + 4 * t, ("N", t)))
+        timed.append((56 + 6 * t, ("N", t)))
     timed.sort(key=lambda entry: entry[0])
     return [entry[1] for entry in timed] + [("G", g) for g in range(n_chunks)]
 
 
 def scatter_kernel(lay, sizes, *refs):
-    rows, width, ff, repeat = sizes
+    rows, width, ff, repeat, inside = sizes
     nz, nlo, nhi = lay.nz, lay.nlo, lay.nhi
     stages = len(lay.bits)
     chunks = scatter_chunks(width, ff, repeat)
@@ -860,17 +914,40 @@
         del refs[:count]
         return taken
 
-    partial_o, partial_s, x_down, x_up, x_qkv, g_down, g_up, g_qkv, g_out, small = take(10)
+    partial_o, = take(1)
+    if inside:
+        x_up, x_qkv, g_up, g_qkv, small = take(5)
+        x_down = g_down = g_out = None
+        seq_t, w_qkv, w_up, means_in, scales_in = take(5)
+        ready, part_in = take(2), take(1)[0]
+        gain_a, gain_m = take(2)
+    else:
+        x_down, x_up, x_qkv, g_down, g_up, g_qkv, g_out, small = take(8)
+        partial_s, = take(1)
+        ready = []
     sum_o, sum_s, all_down, all_up, all_qkv, all_out, small_sum = take(7)
     own, across_buf, near_buf, chain_buf = take(4)
-    acc = take(n)
-    got = [take(stages) for _ in range(n)]
+    acc = [None] * len(ready) + take(n - len(ready))
+    got = [None] * len(ready) + [take(stages) for _ in range(n - len(ready))]
     out_acc, = take(1)
     out_got = take(stages)
     small_buf, small_got = take(2)
-    left, right_down, right_up, right_qkv, right_out, staged, out_part = take(7)
+    left, = take(1)
+    right_down = right_out = None
+    if inside:
+        right_up, right_qkv = take(2)
+    else:
+        right_down, right_up, right_qkv, right_out = take(4)
+    staged, out_part = take(2)
+    if inside:
+        s_buf, ring_t, ring_q, ring_u, means, scales, small_first = take(7)
+        partial_s = s_buf
+    else:
+        small_first = small
     (own_c, y_r, y_s, near_r, near_s, z_r, z_s, st_r, st_s, g_r, g_s, keep_c,
      out_r, out_s, move_r, move_s, sm_r, sm_s, left_c, right_c) = take(20)
+    if inside:
+        slab_c, stat_c = take(2)
 
     z, hi, lo = place(lay)
     rank = z * nhi + hi
@@ -902,56 +979,76 @@
 
     partial, summed = (partial_o, partial_s), (sum_o, sum_s)
 
-    def load_own(a, q):
+    lanes = width // 2
+
+    def part(b):
+        return b // 2, pl.ds((b % 2) * lanes, lanes)
+
+    def load_own(b, q):
+        a, at = part(b)
         row = pl.multiple_of(hi * half + q * rows, rows)
-        return pltpu.make_async_copy(partial[a].at[pl.ds(row, rows)], own.at[a, q % 2], own_c.at[a, q % 2])
-
-    def across(a, q):
+        return pltpu.make_async_copy(partial[a].at[pl.ds(row, rows), at], own.at[a, q % 2, :, at], own_c.at[b, q % 2])
+
+    def own_rows(b, q):
+        a, at = part(b)
+        if a == 1 and inside:
+            return s_buf.at[pl.ds(pl.multiple_of(hi * half + q * rows, rows), rows), at]
+        return own.at[a, q % 2, :, at]
+
+    def across(b, q):
+        a, at = part(b)
         row = pl.multiple_of((1 - hi) * half + q * rows, rows)
         return remote(
-            partial[a].at[pl.ds(row, rows)], across_buf.at[a, q], y_s.at[a, q], y_r.at[a, q], dev(z, 1 - hi, lo)
+            partial[a].at[pl.ds(row, rows), at], across_buf.at[a, q, :, at], y_s.at[b, q], y_r.at[b, q], dev(z, 1 - hi, lo)
         )
 
-    def near(a, q):
+    def near(b, q):
+        a, at = part(b)
         return remote(
-            across_buf.at[a, q], near_buf.at[a, lo], near_s.at[a, q], near_r.at[a, lo], dev(z, hi, q)
+            across_buf.at[a, q, :, at], near_buf.at[a, lo, :, at], near_s.at[b, q], near_r.at[b, lo], dev(z, hi, q)
         )
 
-    def near_arrival(a, q):
-        piece = near_buf.at[a, q]
-        return remote(piece, piece, near_s.at[a, q], near_r.at[a, q], dev(z, hi, q))
-
-    def along(a, seq, way):
+    def near_arrival(b, q):
+        a, at = part(b)
+        piece = near_buf.at[a, q, :, at]
+        return remote(piece, piece, near_s.at[b, q], near_r.at[b, q], dev(z, hi, q))
+
+    def along(b, seq, way):
+        a, at = part(b)
         slot = seq if way == 0 else jnp.where(z == seq + 1, nz, seq)
         return remote(
-            near_buf.at[a, lay.lo_of_seq[seq]], chain_buf.at[a, slot], z_s.at[a, seq], z_r.at[a, seq, way],
+            near_buf.at[a, lay.lo_of_seq[seq], :, at], chain_buf.at[a, slot, :, at], z_s.at[b, seq], z_r.at[b, seq, way],
             dev((z + 1 - 2 * way + nz) % nz, hi, lo),
         )
 
-    def start_across(a):
-        for q in range(2):
-            load_own(a, q).start()
+    def start_across(b):
+        a, _ = part(b)
+        for q in range(0 if a == 1 and inside else 2):
+            load_own(b, q).start()
         for q in range(nlo):
-            across(a, q).start()
-
-    def across_event(a, q):
-        load_own(a, q).wait()
-        across(a, q).wait_recv()
-        mine, arrived = own.at[a, q % 2], across_buf.at[a, q]
+            across(b, q).start()
+
+    def across_event(b, q):
+        a, at = part(b)
+        if not (a == 1 and inside):
+            load_own(b, q).wait()
+        across(b, q).wait_recv()
+        mine, arrived = own_rows(b, q), across_buf.at[a, q, :, at]
 
         @pl.when(lo == q)
         def _():
-            add_rows(near_buf.at[a, q], mine, arrived, 16)
+            add_rows(near_buf.at[a, q, :, at], mine, arrived, 32)
 
         @pl.when(lo != q)
         def _():
-            add_rows(arrived, mine, arrived, 16)
-            near(a, q).start()
-
-        if q + 2 < nlo:
-            load_own(a, q + 2).start()
-
-    def chain_event(a, seq, way):
+            add_rows(arrived, mine, arrived, 32)
+            near(b, q).start()
+
+        if q + 2 < nlo and not (a == 1 and inside):
+            load_own(b, q + 2).start()
+
+    def chain_event(b, seq, way):
+        a, at = part(b)
         q = lay.lo_of_seq[seq]
         active = (z < seq) if way == 0 else (z > seq)
         first = (z == 0) if way == 0 else (z == nz - 1)
@@ -960,40 +1057,53 @@
         def _():
             @pl.when(lo != q)
             def _():
-                near_arrival(a, q).wait_recv()
+                near_arrival(b, q).wait_recv()
 
             @pl.when(jnp.logical_not(first))
             def _():
-                along(a, seq, way).wait_recv()
-                add_rows(near_buf.at[a, q], near_buf.at[a, q], chain_buf.at[a, seq], 16)
-
-            along(a, seq, way).start()
-
-    def final_event(a):
+                along(b, seq, way).wait_recv()
+                mine = near_buf.at[a, q, :, at]
+                add_rows(mine, mine, chain_buf.at[a, seq, :, at], 32)
+
+            along(b, seq, way).start()
+
+    def chain_pair(b, m):
+        @pl.when(z < nz // 2)
+        def _():
+            chain_event(b, nz - 1 - m, 0)
+            chain_event(b, m, 1)
+
+        @pl.when(z >= nz // 2)
+        def _():
+            chain_event(b, m, 1)
+            chain_event(b, nz - 1 - m, 0)
+
+    def final_event(b):
+        a, at = part(b)
         late = z // (nz // 2)
         home = (1 - late) * (2 * z) + late * (2 * (nz - 1 - z) + 1)
-        piece = near_buf.at[a, home]
+        piece = near_buf.at[a, home, :, at]
 
         @pl.when(lo != home)
         def _():
-            remote(piece, piece, near_s.at[a, 0], near_r.at[a, home], dev(z, hi, home)).wait_recv()
+            remote(piece, piece, near_s.at[b, 0], near_r.at[b, home], dev(z, hi, home)).wait_recv()
 
         @pl.when(z > 0)
         def _():
-            arrived = chain_buf.at[a, z]
-            remote(arrived, arrived, z_s.at[a, 0], z_r.at[a, z, 0], dev(z, hi, lo)).wait_recv()
+            arrived = chain_buf.at[a, z, :, at]
+            remote(arrived, arrived, z_s.at[b, 0], z_r.at[b, z, 0], dev(z, hi, lo)).wait_recv()
 
         @pl.when(z < nz - 1)
         def _():
-            arrived = chain_buf.at[a, nz]
-            remote(arrived, arrived, z_s.at[a, 0], z_r.at[a, z, 1], dev(z, hi, lo)).wait_recv()
+            arrived = chain_buf.at[a, nz, :, at]
+            remote(arrived, arrived, z_s.at[b, 0], z_r.at[b, z, 1], dev(z, hi, lo)).wait_recv()
 
         def body(k, carry):
-            at = pl.ds(pl.multiple_of(k * 16, 16), 16)
-            total = piece[at, :].astype(jnp.float32)
-            total = total + jnp.where(z > 0, chain_buf[a, z, at, :].astype(jnp.float32), 0.0)
-            total = total + jnp.where(z < nz - 1, chain_buf[a, nz, at, :].astype(jnp.float32), 0.0)
-            summed[a][at, :] = total
+            line = pl.ds(pl.multiple_of(k * 16, 16), 16)
+            total = piece[line, :].astype(jnp.float32)
+            total = total + jnp.where(z > 0, chain_buf[a, z, line, at].astype(jnp.float32), 0.0)
+            total = total + jnp.where(z < nz - 1, chain_buf[a, nz, line, at].astype(jnp.float32), 0.0)
+            summed[a][line, at] = total
             return carry
 
         lax.fori_loop(0, rows // 16, body, 0)
@@ -1001,7 +1111,7 @@
     targets = (all_down, all_up, all_qkv)
     lefts = (x_down, x_up, x_qkv)
     n_slots = left.shape[0]
-    slots = [source % n_slots for source in range(3)]
+    slots = [0, 0, 1] if inside else [source % n_slots for source in range(3)]
     rights = ((g_down, right_down), (g_up, right_up), (g_qkv, right_qkv), (g_out, right_out))
 
     def load_left(source):
@@ -1011,14 +1121,32 @@
         return pltpu.make_async_copy(*rights[source], right_c.at[source])
 
     def start_loads():
+        if inside:
+            for copy in stat_loads() + slab_loads(0):
+                copy.start()
+            part_load().start()
+            for source in (1, 2):
+                load_left(source).start()
+                load_right(source).start()
+            return
         for source in (0, 3, 1, 2):
             if source < n_slots:
                 load_left(source).start()
             load_right(source).start()
 
-    def ready(source):
+    def part_load():
+        return pltpu.make_async_copy(part_in, out_part, right_c.at[3])
+
+    right_waited = set()
+
+    def right_here(source):
+        if source not in right_waited:
+            right_waited.add(source)
+            load_right(source).wait()
+
+    def loaded(source):
         load_left(source).wait()
-        load_right(source).wait()
+        right_here(source)
 
     def product(g, h, rel):
         source, first, wide, _, _ = chunks[g]
@@ -1047,9 +1175,11 @@
 
     def start_chunk(g):
         source, first, wide, _, _ = chunks[g]
+        if g < len(ready):
+            return
         if first == 0:
-            ready(source)
-        if g >= 3:
+            loaded(source)
+        if g >= 3 + len(ready):
             for h in range(nhi):
                 for rel in stage_pieces(0):
                     stage_send(g - 3, 0, h, rel).wait_send()
@@ -1067,12 +1197,18 @@
 
         lax.fori_loop(0, pairs, send, 0)
         lax.fori_loop(0, pairs, keep_own, 0)
+        if inside:
+            return
         if g == 0:
             out_start()
         if (g + 1 == n or chunks[g + 1][0] != source) and source + n_slots < 3:
             load_left(source + n_slots).start()
 
     def stage_event(g, t):
+        if g < len(ready):
+            if t == 0:
+                deliver(g)
+            return
         order = list(reversed(range(0, nlo, 2 << t)))
         for h in range(nhi):
             for rel in order:
@@ -1089,8 +1225,9 @@
         to_z, to_hi = (z + dz) % nz, flip(hi, dh, nhi)
         first = pl.multiple_of(column(rank), 128)
         k = dz * nhi + dh
+        from_rows = pl.ds(pl.multiple_of(to_z * grain, grain), grain)
         return remote(
-            acc[g].at[to_hi, 0, pl.ds(pl.multiple_of(to_z * grain, grain), grain)],
+            ready[g].at[to_hi, from_rows] if g < len(ready) else acc[g].at[to_hi, 0, from_rows],
             targets[source].at[:, pl.ds(first, wide)],
             g_s.at[g, k], g_r.at[g, k], dev(to_z, to_hi, lo),
         )
@@ -1106,8 +1243,9 @@
     def keep(g):
         source, _, wide, column, _ = chunks[g]
         first = pl.multiple_of(column(rank), 128)
+        from_rows = pl.ds(pl.multiple_of(z * grain, grain), grain)
         return pltpu.make_async_copy(
-            acc[g].at[hi, 0, pl.ds(pl.multiple_of(z * grain, grain), grain)],
+            ready[g].at[hi, from_rows] if g < len(ready) else acc[g].at[hi, 0, from_rows],
             targets[source].at[:, pl.ds(first, wide)], keep_c.at[g],
         )
 
@@ -1146,6 +1284,11 @@
         return remote(src, out_got[t].at[k], out_s.at[t, k], out_r.at[t, k], dev(z, hi, flip(lo, 1 << t, nlo)))
 
     def out_start():
+        if inside:
+            part_load().wait()
+            for rel in stage_pieces(0):
+                out_send(0, rel).start()
+            return
         load_right(3).wait()
         wide = min(512, width)
 
@@ -1184,46 +1327,96 @@
         return pltpu.make_async_copy(out_acc.at[0], all_out, move_s)
 
     doubling = (
-        [dev(z, flip(hi, 1, nhi), lo)]
-        + [dev(z, hi, flip(lo, b, nlo)) for b in reversed(lay.bits)]
-        + [dev(flip(z, b, nz), hi, lo) for b in lay.bits]
+        [dev(flip(z, b, nz), hi, lo) for b in lay.bits]
+        + [dev(z, hi, flip(lo, lay.bits[0], nlo))]
+        + [dev(z, flip(hi, 1, nhi), lo)]
+        + [dev(z, hi, flip(lo, b, nlo)) for b in lay.bits[1:]]
     )
 
     def small_send(t):
-        src = small if t == 0 else small_buf.at[t - 1]
+        src = small_first if t == 0 else small_buf.at[t - 1]
         return remote(src, small_got.at[t], sm_s.at[t], sm_r.at[t], doubling[t])
 
     def small_event(t):
         small_send(t).wait_recv()
-        mine = small if t == 0 else small_buf.at[t - 1]
+        mine = small_first if t == 0 else small_buf.at[t - 1]
         into = small_sum if t + 1 == len(doubling) else small_buf.at[t]
         into[...] = mine[...] + small_got[t]
         if t + 1 < len(doubling):
             small_send(t + 1).start()
 
+    slab = 256
+    wide = slab // 128
+
+    def slab_loads(k):
+        at = pl.ds(k * slab, slab)
+        return [
+            pltpu.make_async_copy(seq_t.at[:, at], ring_t.at[k % 2], slab_c.at[k % 2, 0]),
+            pltpu.make_async_copy(w_qkv.at[at], ring_q.at[k % 2], slab_c.at[k % 2, 1]),
+            pltpu.make_async_copy(w_up.at[at], ring_u.at[k % 2], slab_c.at[k % 2, 2]),
+        ]
+
+    def stat_loads():
+        return [
+            pltpu.make_async_copy(means_in, means, stat_c.at[0]),
+            pltpu.make_async_copy(scales_in, scales, stat_c.at[1]),
+        ]
+
+    def in_slab(k):
+        if k == 0:
+            small_first[...] = small[...]
+            for copy in stat_loads():
+                copy.wait()
+            right_here(1)
+            right_here(2)
+        for copy in slab_loads(k):
+            copy.wait()
+        if (k + 1) * slab < width:
+            for copy in slab_loads(k + 1):
+                copy.start()
+        features = pl.ds(k * slab, slab)
+
+        def body(i, sums):
+            at = pl.ds(pl.multiple_of(i * 256, 256), 256)
+            grad_a = dot32(right_qkv[at, :], ring_q[k % 2], contract_last)
+            grad_m = dot32(right_up[at, :], ring_u[k % 2], contract_last)
+            s_buf[at, features] = (grad_a * gain_a[:, features] + grad_m * gain_m[:, features]).astype(jnp.bfloat16)
+            mean, scale = jnp.concatenate([means[at, :]] * wide, axis=1), jnp.concatenate([scales[at, :]] * wide, axis=1)
+            normed = (ring_t[k % 2, at, :].astype(jnp.float32) - mean) * scale
+            terms = (grad_a * normed, grad_a, grad_m * normed, grad_m)
+            return tuple(have + jnp.sum(term.reshape(32, 8, slab), axis=0) for have, term in zip(sums, terms))
+
+        sums = lax.fori_loop(0, 2 * half // 256, body, (jnp.zeros((8, slab), jnp.float32),) * 4)
+        first = small.shape[0] - 4 * width // 128
+        for m, have in enumerate(sums):
+            line = jnp.sum(have, axis=0, keepdims=True)
+            for j in range(wide):
+                row = first + (m * width + k * slab) // 128 + j
+                small_first[row : row + 1, :] = line[:, j * 128 : (j + 1) * 128]
+
     act = dict(
-        Y=start_across, A=across_event, B=chain_event, F=final_event, C=start_chunk, X=stage_event, G=finish_chunk,
+        S=in_slab, Y=start_across, P=out_start if inside else (lambda: None), A=across_event, B=chain_pair, F=final_event, C=start_chunk, X=stage_event, G=finish_chunk,
         L=start_loads, Q=out_event, M=lambda: small_send(0).start(), N=small_event,
     )
-    for item in scatter_schedule(nz, nlo, n, stages):
+    for item in scatter_schedule(nz, nlo, n, stages, width // slab if inside else 0):
         act[item[0]](*item[1:])
 
-    for a in range(2):
+    for b in range(4):
         for q in range(nlo):
-            across(a, q).wait_send()
+            across(b, q).wait_send()
 
             @pl.when(lo != q)
-            def _(a=a, q=q):
-                near(a, q).wait_send()
+            def _(b=b, q=q):
+                near(b, q).wait_send()
 
         for seq in range(nz):
             @pl.when(z != seq)
-            def _(a=a, seq=seq):
-                along(a, seq, 0).wait_send()
+            def _(b=b, seq=seq):
+                along(b, seq, 0).wait_send()
 
     for g in range(n):
         for t in range(stages):
-            if t == 0 and g + 3 < n:
+            if g < len(ready) or (t == 0 and g + 3 < n):
                 continue
             for h in range(nhi):
                 for rel in stage_pieces(t):
@@ -1244,7 +1437,7 @@
         small_send(t).wait_send()
 
 
-def scatter_all(lay, partial_o, partial_s, x_down, x_up, x_qkv, g_down, g_up, g_qkv, g_out, small):
+def scatter_all(lay, partial_o, partial_s, x_down, x_up, x_qkv, g_down, g_up, g_qkv, g_out, terms, small):
     total, width = partial_o.shape
     nz, nlo, nhi = lay.nz, lay.nlo, lay.nhi
     rows = total // (nhi * nlo)
@@ -1267,9 +1460,10 @@
         pltpu.VMEM((2, nlo, rows, width), bf16),
         pltpu.VMEM((2, nz + 1, rows, width), bf16),
     ]
-    for chunk in chunks:
+    here = chunks[2:] if terms is not None else chunks
+    for chunk in here:
         scratch.append(pltpu.VMEM((nhi, nlo // 2, span, chunk[2]), bf16))
-    for chunk in chunks:
+    for chunk in here:
         for t in range(stages):
             scratch.append(pltpu.VMEM((nhi, nlo >> (t + 1), span, chunk[2]), bf16))
     scratch.append(pltpu.VMEM((nlo // 2, grain, width), bf16))
@@ -1277,21 +1471,29 @@
         scratch.append(pltpu.VMEM((nlo >> (t + 1), grain, width), bf16))
     scratch += [pltpu.VMEM((steps,) + small.shape, f32), pltpu.VMEM((steps,) + small.shape, f32)]
     widest = max(chunk[2] for chunk in chunks)
+    fused = terms is not None
     scratch += [
         pltpu.VMEM((2 if total <= 1024 else 1, total, width), bf16),
-        pltpu.VMEM(g_down.shape, bf16), pltpu.VMEM(g_up.shape, bf16), pltpu.VMEM(g_qkv.shape, bf16),
-        pltpu.VMEM(g_out.shape, bf16),
+        *[pltpu.VMEM(g.shape, bf16) for g in ((g_up, g_qkv) if fused else (g_down, g_up, g_qkv, g_out))],
         pltpu.VMEM((3, nhi, nlo // 2, span, widest), bf16),
         pltpu.VMEM((width // ranks, width), bf16),
     ]
+    if fused:
+        scratch += [
+            pltpu.VMEM((total, width), bf16), pltpu.VMEM((2, total, 256), bf16), pltpu.VMEM((2, 256, 3 * HD), bf16),
+            pltpu.VMEM((2, 256, ff), bf16), pltpu.VMEM((total, 128), f32), pltpu.VMEM((total, 128), f32),
+            pltpu.VMEM(small.shape, f32),
+        ]
     most = nlo // 2
     scratch += [
-        dma((2, 2)), dma((2, nlo)), dma((2, nlo)), dma((2, nlo)), dma((2, nlo)), dma((2, nz, 2)), dma((2, nz)),
+        dma((4, 2)), dma((4, nlo)), dma((4, nlo)), dma((4, nlo)), dma((4, nlo)), dma((4, nz, 2)), dma((4, nz)),
         dma((n, stages, nhi, most)), dma((n, stages, nhi, most)), dma((n, ranks)), dma((n, ranks)),
         dma((n,)), dma((stages, most)), dma((stages, most)), dma, dma, dma((steps,)), dma((steps,)), dma((3,)), dma((4,)),
     ]
+    if fused:
+        scratch += [dma((2, 3)), dma((2,))]
     return pl.pallas_call(
-        functools.partial(scatter_kernel, lay, (rows, width, ff, repeat)),
+        functools.partial(scatter_kernel, lay, (rows, width, ff, repeat, fused)),
         out_shape=[
             jax.ShapeDtypeStruct((rows, width), f32),
             jax.ShapeDtypeStruct((rows, width), f32),
@@ -1301,14 +1503,17 @@
             jax.ShapeDtypeStruct((grain, width), bf16),
             jax.ShapeDtypeStruct(small.shape, f32),
         ],
-        in_specs=[anywhere] * 9 + [inside],
+        in_specs=([anywhere] * 5 + [inside] + [anywhere] * 8 + [inside] * 2) if fused else ([anywhere] * 8 + [inside, anywhere]),
         out_specs=[inside, inside, anywhere, anywhere, anywhere, anywhere, inside],
         scratch_shapes=scratch,
         compiler_params=pltpu.CompilerParams(
-            collective_id=2, has_side_effects=True, vmem_limit_bytes=60 * 1024 * 1024
+            collective_id=2, has_side_effects=True, vmem_limit_bytes=62 * 1024 * 1024
         ),
         name="scatter_all",
-    )(partial_o, partial_s, x_down, x_up, x_qkv, g_down, g_up, g_qkv, g_out, small)
+    )(
+        partial_o,
+        *((x_up, x_qkv, g_up, g_qkv, small, *terms) if fused else (x_down, x_up, x_qkv, g_down, g_up, g_qkv, g_out, small, partial_s)),
+    )
 
 
 def plain_block(lay, operands):
@@ -1400,6 +1605,7 @@
         out_partial.astype(bf16), in_partial.astype(bf16), sums,
         jnp.sum(grad_projected.astype(f32), axis=0) * first_copy,
         jnp.sum(grad_hidden.astype(f32), axis=0),
+        None,
     )
 
 
@@ -1427,7 +1633,10 @@
         jnp.concatenate([cosine, cosine, rest + 1.0], axis=1),
         jnp.concatenate([-sine, sine, rest], axis=1),
     )
-    return tuple(found[:9]) + (found[11], found[12][0], found[13][0])
+    return tuple(found[:8]) + (
+        None, jnp.zeros((4, width), f32), found[18][0], found[19][0],
+        (*found[10:18], attn_norm_gain[None], mlp_norm_gain[None]),
+    )
 
 
 def local_block(
@@ -1468,9 +1677,9 @@
         own, own_cotangent, qkv_weight, qkv_bias, out_weight, up_weight, up_bias, down_weight,
         attn_norm_gain, attn_norm_bias, mlp_norm_gain, mlp_norm_bias,
     )
-    fits = repeat == 1 and nhi * half * width <= 1024 * 2048
+    fits = repeat == 1 and nlo == 4 and nhi * half * width <= 1024 * 2048
     (seq_cotangent, attn_in, mlp_in, activated, grad_hidden, grad_projected, mixed_mine,
-     out_partial, in_partial, sums, qkv_bias_part, up_bias_part) = (fused_block if fits else plain_block)(lay, operands)
+     out_partial, in_partial, sums, qkv_bias_part, up_bias_part, terms) = (fused_block if fits else plain_block)(lay, operands)
 
     qkv_bias_full = jnp.zeros((3, width), f32)
     qkv_bias_full = lax.dynamic_update_slice(
@@ -1500,6 +1709,7 @@
         grad_hidden,
         grad_projected,
         mixed_mine,
+        terms,
         small,
     )
     output = (own.astype(f32) + summed_out + (out_bias + down_bias)).astype(bf16)[None]

time: 423 us -> 373 us (0.88)
  the two profiles are of different devices: /device:TPU:19 before, /device:TPU:0 now
where the time goes in v4:
time: 373 us; the launch traced here: 370 us
  Pallas kernels  349 us (94%)
  other arithmetic  13.6 us (4%)
  local copies, waits for them, and re-layouts  6.24 us (2%)
    pallas_call x1, Pallas kernels, block_all(): pl.pallas_call(functools.partial(block_kernel, lay, (rows, width, qkv.sha...  180 us
    pallas_call x1, Pallas kernels, scatter_all(): pl.pallas_call(functools.partial(scatter_kernel, lay, (rows, width, ff, r...  169 us

profile of v4, /device:TPU:0, one launch (start us, length us, event | category | flops | bytes accessed | tf_op | source)
XLA Modules:
  0.0 369.6 jit_solution(6492418330373983594)
XLA Ops:
  0.7 1.3 dynamic_slice.15
  2.0 0.8 fusion.16
  2.8 0.6 broadcast_in_dim.39.refs_6_
  3.4 2.0 fusion.14
  5.3 0.1 pad.6.clone
  5.4 0.1 pad.9.clone
  5.5 1.3 maximum_maximum_fusion
  6.8 179.7 %block_all.1 = (bf16[1024,2048]{1,0:T(8,128)(2,1)}, bf16[1024,2048]{1,0:T(8,128)(2,1)}, bf16[1024,2048]{1,0:T(8,128)(2,1)}, bf16[1024,1024]{1,0:T(8,128)(2,1)}, ...) custom-call(bf16[128,2048]{1,0:T(8,128)(2,1)} %bitcast.35, ...), custom_call_target="tpu_custom_call" | custom-call | tf_op jit(solution)/shard_map/block_all/pallas_call | solution.py:806
  186.5 0.7 reduce
  187.3 0.9 dynamic_update_slice.7
  188.2 0.1 convert_reduce_fusion.1
  188.3 0.6 maximum_bitcast_fusion.refs_5_
  188.9 169.0 %scatter_all.1 = (f32[128,2048]{1,0:T(8,128)}, f32[128,2048]{1,0:T(8,128)}, bf16[64,8192]{1,0:T(8,128)(2,1)}, bf16[64,8192]{1,0:T(8,128)(2,1)}, bf16[64,6144]{1,...) custom-call(bf16[1024,2048]{1,0:T(8,128)(2,1)} %get-tuple-element.36.refs_0_, ...), custom_call_target="tpu_custom_call" | custom-call | tf_op jit(solution)/shard_map/scatter_all/pallas_call | solution.py:1495
  358.0 0.0 copy-start
  358.0 0.0 copy-start.2
  358.0 2.8 convert_element_type.28
  360.8 0.0 copy-done.3
  360.8 1.5 convert_element_type.29
  362.3 0.0 copy-done
  362.3 0.2 convert_reduce_fusion
  362.5 0.3 fusion.7
  362.8 0.0 copy-done.2
  362.8 0.0 copy-start.5
  362.8 0.3 fusion.15
  363.1 0.0 copy-done.9
  363.2 1.7 fusion.8
  364.9 1.2 convert_element_type.26
  366.1 0.8 convert_element_type.27
  367.0 0.6 slice_bitcast_fusion.2
  367.6 0.6 slice_bitcast_fusion
  368.2 0.6 slice_bitcast_fusion.1
  368.8 0.6 copy.31
  (30 shorter events, 0.1 us)
Async XLA Ops:
  6.8 181.4 %copy-start.1 = (bf16[1,128,2048]{2,1,0:T(8,128)(2,1)S(1)}, bf16[1,128,2048]{2,1,0:T(8,128)(2,1)}, u32[]{:S(2)}) copy-start(bf16[1,128,2048]{2,1,0:T(8,128)(2,1)} %param.27) | copy-start | bytes 1572868
  358.0 2.9 copy-start.3
  358.0 4.3 %copy-start = (bf16[1,128,2048]{2,1,0:T(8,128)(2,1)S(1)}, bf16[1,128,2048]{2,1,0:T(8,128)(2,1)}, u32[]{:S(2)}) copy-start(bf16[1,128,2048]{2,1,0:T(8,128)(2,1)} %param.14) | copy-start | bytes 1572868
  358.0 4.8 %copy-start.2 = (f32[128,2048]{1,0:T(8,128)S(1)}, f32[128,2048]{1,0:T(8,128)}, u32[]{:S(2)}) copy-start(f32[128,2048]{1,0:T(8,128)} %get-tuple-element.52) | copy-start | bytes 3145732
  360.8 2.3 copy-start.9
  360.8 2.3 copy-start.10
  360.8 2.3 copy-start.4
  362.8 2.1 copy-start.5
  363.2 3.0 copy-start.6
  363.2 3.8 %copy-start.7 = (f32[192,128]{1,0:T(8,128)S(1)}, f32[192,128]{1,0:T(8,128)}, u32[]{:S(2)}) copy-start(f32[192,128]{1,0:T(8,128)} %get-tuple-element.54) | copy-start | bytes 294916
  367.6 1.8 copy-start.8
